TPU v7x, 256 devices: a whole 4x4x8 slice. The times are simulated.
256 devices in a mesh: span: 32 (over z, y), deck: 8 (over x, core).
Axes of the slice: x: 4, y: 4, z: 8, core: 2. Of those that a mesh axis runs over, the one named last changes fastest.
Arguments:
- flex: float32 [32, 8, 1024, 1024], P('span', 'deck'), may hold values from -16 to 16, as said below
- precond: float32 [32, 8, 1024, 1024], P('span', 'deck'), may hold values from -16 to 16, as said below
- corner_map: float32 [32, 8, 256, 1024], P('span', 'deck'), may hold values from -0.1875 to 0.1875
- coarse_inverse: float32 [256, 256], replicated, may hold values from -16 to 16, as said below
- gap_deck: float32 [32, 8, 256, 256], P('span', 'deck'), may hold values from -6 to 6
- gap_joint: float32 [32, 8, 256, 256], P('span', 'deck'), may hold values from -6 to 6
- active: int32 [32, 8, 4], P('span', 'deck'), may hold values 0 or 1
Outputs:
- solution_deck: float32 [32, 8, 256, 256], P('span', 'deck')
- solution_joint: float32 [32, 8, 256, 256], P('span', 'deck')
- residual_deck: float32 [32, 8, 256, 256], P('span', 'deck')
- residual_joint: float32 [32, 8, 256, 256], P('span', 'deck')
Inputs may be any that keep to these rules, and one draw needn't show every extreme that they name: flex is symmetric positive definite for every subdomain. precond is symmetric positive definite for every subdomain. coarse_inverse is symmetric positive definite.
All inputs are finite; a program needn't handle non-finite values. No bound on the sum of `active` on one device may be relied on, other than what follows from the above.
Results may differ from a plain program's by a relative error of at most 0.00024.
Values sent between devices are 32-bit elements; how exact they have to be, the bound alone decides.
No kernel may reach another device: no remote copies, remote signals or barrier semaphores. Data moves between devices by JAX's collectives and lax.ppermute only.
A program may use at most 64 MiB of HBM per device.

v0:
```python
import functools
import math

import jax
import jax.numpy as jnp
from jax import lax
from jax.experimental import pallas as pl
from jax.experimental.pallas import tpu as pltpu
from jax.sharding import Mesh
from jax.sharding import PartitionSpec as P

SPAN, DECK = ("z", "y"), ("x", "core")
SPANS, DECKS, Y, X, Z = 32, 8, 4, 4, 8
CASES, FACE, IFACE, NC, GB = 256, 256, 1024, 256, 4
WIDE = NC + 128
HALF = CASES // 2
PIECE = HALF // (Y * X)
SCALE = 1.0 / math.sqrt(SPANS * DECKS)
F32, BF16 = jnp.float32, jnp.bfloat16
VMEM = pl.BlockSpec(memory_space=pltpu.VMEM)
SMEM = pl.BlockSpec(memory_space=pltpu.SMEM)


def cyclic(block, axes, k):
    n = SPANS if axes == SPAN else DECKS
    return lax.ppermute(block, axes, [(i, (i + k) % n) for i in range(n)])


def swapped(block):
    return lax.ppermute(block, "core", [(0, 1), (1, 0)])


def parts(value):
    high = value.astype(BF16)
    return high, (value - high.astype(F32)).astype(BF16)


def product(left, right, dims=(((1,), (0,)), ((), ()))):
    dot = functools.partial(lax.dot_general, dimension_numbers=dims, preferred_element_type=F32)
    return dot(left[0], right[0]) + (dot(left[0], right[1]) + dot(left[1], right[0]))


TRANS = (((1,), (1,)), ((), ()))


def quarter(ref, i):
    return ref[:, i * FACE : (i + 1) * FACE]


def column(lane, *values):
    out = jnp.zeros((values[0].shape[0], 128), F32)
    for i, value in enumerate(values):
        out = jnp.where(lane == i, value, out)
    return out


def row_sum(value):
    return jnp.sum(value, axis=1, keepdims=True)


def cost(rows):
    return pl.CostEstimate(flops=6 * rows * IFACE * IFACE, bytes_accessed=8 << 20, transcendentals=0)


def call(body, outs, n_in, name, smem=(), scratch=(), estimate=None):
    return pl.pallas_call(
        body,
        out_shape=tuple(jax.ShapeDtypeStruct(s, F32) for s in outs),
        in_specs=[SMEM if i in smem else VMEM for i in range(n_in)],
        out_specs=tuple(VMEM for _ in outs),
        scratch_shapes=list(scratch),
        compiler_params=pltpu.CompilerParams(vmem_limit_bytes=24 << 20),
        cost_estimate=estimate,
        name=name,
    )


def times_matrix(u_high, u_low, matrix_ref, store):
    for i in range(4):
        store(i, product((u_high[...], u_low[...]), parts(quarter(matrix_ref, i))))


def keep(u_high, u_low, i, value):
    high, low = parts(value)
    u_high[:, i * FACE : (i + 1) * FACE] = high
    u_low[:, i * FACE : (i + 1) * FACE] = low


U_SCRATCH = (pltpu.VMEM((CASES, IFACE), BF16), pltpu.VMEM((CASES, IFACE), BF16))


def live_row(ref, on):
    block = lax.broadcasted_iota(jnp.int32, (1, FACE), 1) // (FACE // GB)
    row = jnp.zeros((1, FACE), F32)
    for b in range(GB):
        row = jnp.where(block == b, ref[b].astype(F32), row)
    return row * on.astype(F32)


def faces_times(first, third, matrix, rows, i):
    at = slice(i * FACE, (i + 1) * FACE)
    return product(first, parts(matrix[rows : rows + FACE, at])) + product(
        third, parts(matrix[rows + 2 * FACE : rows + 3 * FACE, at])
    )


def own_kernel(place, active, deck, joint, matrix, part):
    span, across = place[0], place[1]
    first = parts((across < DECKS - 1).astype(F32) * deck[...])
    third = parts(live_row(active, span < SPANS - 1) * joint[...])
    for i in range(4):
        part[:, i * FACE : (i + 1) * FACE] = faces_times(first, third, matrix, 0, i)


def behind_kernel(place, active, active_behind, deck_behind, joint_behind, part, matrix,
                  v0, v1, v2, v3, masks):
    span, across = place[0], place[1]
    ones = jnp.ones((1, FACE), F32)
    lives = (
        ones * (across < DECKS - 1).astype(F32),
        ones * (across > 0).astype(F32),
        live_row(active, span < SPANS - 1),
        live_row(active_behind, span > 0),
    )
    masks[...] = jnp.concatenate(lives + (jnp.zeros((4, FACE), F32),), axis=0)
    second, fourth = parts(lives[1] * deck_behind[...]), parts(lives[3] * joint_behind[...])
    for i, out in enumerate((v0, v1, v2, v3)):
        out[...] = 0.5 * (quarter(part, i) - faces_times(second, fourth, matrix, FACE, i))


def jump(masks, own, got, i):
    return masks[i : i + 1, :] * (own[i][: CASES, :] - got[i][: CASES, :])


def flex_kernel(n_faces, place, masks, f0, f1, f2, f3, g0, g1, g2, g3, matrix, corners, *refs):
    pairs, refs = refs[: 2 * n_faces], refs[2 * n_faces :]
    outs, (first, third, sent, held, u_high, u_low, u_full, table) = refs[:4], refs[4:]
    core = lax.rem(place[1], 2)
    own, got = (f0, f1, f2, f3), (g0, g1, g2, g3)
    for i in range(4):
        value = jump(masks, own, got, i)
        keep(u_high, u_low, i, value)
        u_full[:, i * FACE : (i + 1) * FACE] = value
    first[...] = quarter(u_full, 0)
    third[...] = quarter(u_full, 2)
    total = jnp.zeros((CASES, 1), F32)
    for i in range(4):
        value = product((u_high[...], u_low[...]), parts(quarter(matrix, i)))
        total = total + row_sum(quarter(u_full, i) * value)
        if outs[i].shape[0] == CASES:
            outs[i][...] = value
        else:
            outs[i][: CASES, :] = value
            outs[i][CASES:, :] = quarter(corners, i)
    sums = [
        row_sum(masks[0:1, :] * pairs[2 * k][...] * first[...] + masks[2:3, :] * pairs[2 * k + 1][...] * third[...])
        for k in range(n_faces)
    ]
    table[:, :NC] = product((u_high[...], u_low[...]), parts(corners[...]), TRANS)
    lane = lax.broadcasted_iota(jnp.int32, (CASES, 128), 1)
    table[:, NC:] = column(lane, total, *sums)
    held[...] = table[pl.ds(pl.multiple_of(core * HALF, HALF), HALF), :]
    sent[...] = table[pl.ds(pl.multiple_of((1 - core) * HALF, HALF), HALF), :]


def total_of(got):
    part = got[0]
    for k in range(1, Z):
        part = part + got[k]
    return part


def first_coarse_kernel(got, coarse, out, scalars):
    part = total_of(got)
    total = part[:, :NC]
    load = SCALE * product(parts(total), parts(coarse[...]))
    curv = part[:, NC : NC + 1] + row_sum(load * total)
    rz = part[:, NC + 1 : NC + 2]
    lane = lax.broadcasted_iota(jnp.int32, (PIECE, 128), 1)
    row = jnp.concatenate([load, column(lane, rz / curv)], axis=1)
    for k in range(Y * X):
        out[k] = row
    scalars[...] = column(lane, rz, curv)


def second_coarse_kernel(got, coarse, scalars, out):
    part = total_of(got)
    total = part[:, :NC]
    load = SCALE * product(parts(total), parts(coarse[...]))
    own = part[:, NC : NC + 1] + row_sum(load * total)
    new = part[:, NC + 1 : NC + 2]
    cross = part[:, NC + 2 : NC + 3]
    rz, curv = scalars[:, 0:1], scalars[:, 1:2]
    ratio = new / rz
    second = new / (own + ratio * (2.0 * cross + ratio * curv))
    lane = lax.broadcasted_iota(jnp.int32, (PIECE, 128), 1)
    row = jnp.concatenate([second * load, column(lane, second, second * ratio)], axis=1)
    for k in range(Y * X):
        out[k] = row


def place_rows(place, mine, other, whole):
    core = lax.rem(place[1], 2)
    whole[pl.ds(pl.multiple_of(core * HALF, HALF), HALF), :] = mine[...]
    whole[pl.ds(pl.multiple_of((1 - core) * HALF, HALF), HALF), :] = other[...]


def precond_kernel(place, masks, mine, other, f0, f1, f2, f3, g0, g1, g2, g3,
                   deck, joint, deck_behind, joint_behind, matrix,
                   v0, v1, v2, v3, image_deck, image_joint, res_deck, res_joint,
                   corner_deck, corner_joint, steps, u_high, u_low, whole):
    place_rows(place, mine, other, whole)
    load = parts(whole[:, :NC])
    step = whole[:, NC : NC + 1]
    steps[...] = whole[:, NC:]
    own, got = (f0, f1, f2, f3), (g0, g1, g2, g3)
    gaps = (deck, deck_behind, joint, joint_behind)
    for i in range(4):
        live = masks[i : i + 1, :]
        corner = live * (own[i][CASES:, :] - got[i][CASES:, :])
        image = jump(masks, own, got, i) + product(load, parts(corner))
        gap = live * gaps[i][...]
        res = (gap if i % 2 == 0 else -gap) - step * image
        if i == 0:
            corner_deck[...], image_deck[...], res_deck[...] = corner, image, res
        if i == 2:
            corner_joint[...], image_joint[...], res_joint[...] = corner, image, res
        keep(u_high, u_low, i, res)

    def store(i, value):
        (v0, v1, v2, v3)[i][...] = 0.5 * value

    times_matrix(u_high, u_low, matrix, store)


def final_kernel(place, masks, mine, other, steps, z_deck, z_joint, y_deck, y_joint,
                 image_deck, image_joint, res_deck, res_joint, corner_deck, corner_joint,
                 f0, f2, g0, g2, sol_deck, sol_joint, out_deck, out_joint, whole):
    place_rows(place, mine, other, whole)
    load = parts(whole[:, :NC])
    second, mixed = whole[:, NC : NC + 1], whole[:, NC + 1 : NC + 2]
    first = steps[:, 0:1] + mixed
    sol_deck[...] = first * z_deck[...] + second * y_deck[...]
    sol_joint[...] = first * z_joint[...] + second * y_joint[...]
    for i, res, field, ahead, image, corner, out in (
        (0, res_deck, f0, g0, image_deck, corner_deck, out_deck),
        (2, res_joint, f2, g2, image_joint, corner_joint, out_joint),
    ):
        reaction = masks[i : i + 1, :] * (field[...] - ahead[...])
        out[...] = (
            res[...] - second * reaction - mixed * image[...] - product(load, parts(corner[...]))
        )


def exchange(field):
    right, left, ahead, behind = field
    ahead_got, behind_got = cyclic(ahead, SPAN, 1), cyclic(behind, SPAN, -1)
    right_got, left_got = cyclic(right, DECK, 1), cyclic(left, DECK, -1)
    return left_got, right_got, behind_got, ahead_got


def reduce_rows(sent, held):
    block = held + swapped(sent)
    got = lax.all_to_all(block.reshape(Y * X, PIECE, WIDE), ("y", "x"), 0, 0)
    part = jnp.sum(got, axis=0)
    return lax.all_to_all(jnp.broadcast_to(part, (Z, PIECE, WIDE)), "z", 0, 0)


def gather_rows(copies):
    mine = lax.all_to_all(copies, ("y", "x"), 0, 0).reshape(HALF, WIDE)
    return mine, swapped(mine)


def after(values, *others):
    return lax.optimization_barrier((values, others))[0]


def local(flex, precond, corner_map, coarse_inverse, gap_deck, gap_joint, active):
    flex, precond, corners = flex[0, 0], precond[0, 0], corner_map[0, 0]
    deck, joint, active = gap_deck[0, 0], gap_joint[0, 0], active[0, 0]
    span = lax.axis_index("z") * Y + lax.axis_index("y")
    across = lax.axis_index("x") * 2 + lax.axis_index("core")
    place = jnp.stack([span, across]).astype(jnp.int32)

    face, field, stacked = (CASES, FACE), [(CASES, FACE)] * 4, [(2 * CASES, FACE)] * 4
    half, copies = (HALF, WIDE), (Y * X, PIECE, WIDE)
    full = pltpu.VMEM((CASES, IFACE), F32)
    whole = pltpu.VMEM((CASES, WIDE), F32)

    joint_behind = cyclic(joint, SPAN, 1)
    deck_behind = cyclic(deck, DECK, 1)
    active_behind = cyclic(active, SPAN, 1)
    gaps = (deck, joint, deck_behind, joint_behind)
    (part,) = call(
        own_kernel, [(CASES, IFACE)], 5, "own", smem=(0, 1), estimate=cost(CASES // 2)
    )(place, active, deck, joint, precond)
    *v, masks = call(
        behind_kernel, field + [(8, FACE)], 7, "behind", smem=(0, 1, 2), estimate=cost(CASES // 2)
    )(place, active, active_behind, deck_behind, joint_behind, part, precond)
    *w, z_deck, z_joint, sent, held = call(
        functools.partial(flex_kernel, 1), stacked + [face, face, half, half], 14, "flex_first",
        smem=(0,), scratch=U_SCRATCH + (full, whole), estimate=cost(CASES),
    )(place, masks, *v, *exchange(v), flex, corners, deck, joint)
    got = exchange(w)
    sums = reduce_rows(sent, held)
    loads, scalars = call(first_coarse_kernel, [copies, (PIECE, 128)], 2, "coarse_first")(
        sums, coarse_inverse
    )
    loads = after(loads, got)
    *v, image_deck, image_joint, res_deck, res_joint, corner_deck, corner_joint, steps = call(
        precond_kernel, field + [face] * 6 + [(CASES, 128)], 17, "precond",
        smem=(0,), scratch=U_SCRATCH + (whole,), estimate=cost(CASES),
    )(place, masks, *gather_rows(loads), *w, *got, *gaps, precond)
    *w, y_deck, y_joint, sent, held = call(
        functools.partial(flex_kernel, 2), field + [face, face, half, half], 16, "flex_second",
        smem=(0,), scratch=U_SCRATCH + (full, whole), estimate=cost(CASES),
    )(place, masks, *v, *exchange(v), flex, corners, res_deck, res_joint, image_deck, image_joint)
    got = cyclic(w[1], DECK, -1), cyclic(w[3], SPAN, -1)
    sums = reduce_rows(sent, held)
    (loads,) = call(second_coarse_kernel, [copies], 3, "coarse_second")(sums, coarse_inverse, scalars)
    loads = after(loads, got)
    outs = call(
        final_kernel, [face] * 4, 19, "final", smem=(0,), scratch=(whole,)
    )(
        place, masks, *gather_rows(loads), steps, z_deck, z_joint, y_deck, y_joint,
        image_deck, image_joint, res_deck, res_joint, corner_deck, corner_joint, w[0], w[2], *got,
    )
    return tuple(out[None, None] for out in outs)


def solution(mesh):
    mesh = Mesh(mesh.devices.reshape(Z, Y, X, 2), SPAN + DECK)
    block = P(SPAN, DECK, None, None)
    in_specs = (block, block, block, P(), block, block, P(SPAN, DECK, None))
    return jax.shard_map(
        local, mesh=mesh, in_specs=in_specs, out_specs=(block,) * 4, check_vma=False
    )
```

profile of v0, /device:TPU:1, one launch (start us, length us, event | category | flops | bytes accessed | tf_op | source)
XLA Modules:
  0.0 170.5 jit_solution(15023660343800340168)
XLA Ops:
  0.6 2.6 %collective-permute-start.1 = (f32[256,256]{1,0:T(8,128)}, f32[256,256]{1,0:T(8,128)S(1)}, u32[]{:S(2)}, u32[]{:S(2)}) collective-permute-start(f32[256,256]{1,0:T(8,128)} %bitcast.25), channel_id=1, source_target_pairs={{0,1},{1,2},{2,3},{3,4},{4,5},{5,6},{6,7},{7,0},{8,9},{9,10},{10,1... | collective-permute-start | bytes 786440 | tf_op jit(solution)/shard_map/ppermute | solution.py:26
  3.2 1.3 collective-permute-start.2
  4.5 1.3 collective-permute-start
  5.9 2.2 %copy-done = f32[1,1,1024,1024]{3,2,1,0:T(8,128)S(1)} copy-done((f32[1,1,1024,1024]{3,2,1,0:T(8,128)S(1)}, f32[1,1,1024,1024]{3,2,1,0:T(8,128)}, u32[]{:S(2)}) %copy-start) | copy-done | bytes 4194328
  10.7 1.6 own.1.part
  12.3 5.0 %collective-permute-done.active_behind = s32[4]{0:T(128)S(1)} collective-permute-done((s32[4]{0:T(128)}, s32[4]{0:T(128)S(1)}, u32[]{:S(2)}, u32[]{:S(2)}) %collective-permute-start) | collective-permute-done | bytes 48 | tf_op jit(solution)/shard_map/ppermute | solution.py:26
  17.3 1.6 behind.1
  19.9 4.8 %collective-permute-start.5 = (f32[256,256]{1,0:T(8,128)S(1)}, f32[256,256]{1,0:T(8,128)S(1)}, u32[]{:S(2)}, u32[]{:S(2)}) collective-permute-start(f32[256,256]{1,0:T(8,128)S(1)} %get-tuple-element.48.f3), channel_id=1, source_target_pairs={{0,248},{8,0},{16,8},{24,16},{32,24},{40,32},{48,40},{56,48},{64,5... | collective-permute-start | bytes 786440 | tf_op jit(solution)/shard_map/ppermute | solution.py:26
  24.7 1.3 collective-permute-done.3.g0
  26.0 3.2 %collective-permute-done.6.g3 = f32[256,256]{1,0:T(8,128)S(1)} collective-permute-done((f32[256,256]{1,0:T(8,128)S(1)}, f32[256,256]{1,0:T(8,128)S(1)}, u32[]{:S(2)}, u32[]{:S(2)}) %collective-permute-start.6) | collective-permute-done | bytes 262176 | tf_op jit(solution)/shard_map/ppermute | solution.py:26
  29.2 4.1 %flex_first.1 = (f32[512,256]{1,0:T(8,128)S(1)}, f32[512,256]{1,0:T(8,128)S(1)}, f32[512,256]{1,0:T(8,128)}, f32[512,256]{1,0:T(8,128)}, f32[256,256]{1,0:T(8,12...) custom-call(s32[2]{0:T(128)S(1)} %pad_add_fusion.place, ...), custom_call_target="tpu_custom_call" | custom-call | flops 1610612736 | bytes 8388608 | tf_op jit(solution)/shard_map/flex_first/pallas_call | solution.py:300
  34.7 2.8 %collective-permute-start.7 = (f32[128,384]{1,0:T(8,128)S(1)}, f32[128,384]{1,0:T(8,128)S(1)}, u32[]{:S(2)}, u32[]{:S(2)}) collective-permute-start(f32[128,384]{1,0:T(8,128)S(1)} %get-tuple-element.50), channel_id=1, source_target_pairs={{0,1},{1,0},{2,3},{3,2},{4,5},{5,4},{6,7},{7,6},{8,9},{9,8},{10,11... | collective-permute-start | bytes 589832 | tf_op jit(solution)/shard_map/ppermute | solution.py:30
  37.5 1.7 %collective-permute-start.9 = (f32[512,256]{1,0:T(8,128)S(1)}, f32[512,256]{1,0:T(8,128)}, u32[]{:S(2)}, u32[]{:S(2)}) collective-permute-start(f32[512,256]{1,0:T(8,128)S(1)} %get-tuple-element.53.f0), channel_id=1, source_target_pairs={{0,1},{1,2},{2,3},{3,4},{4,5},{5,6},{6,7},{7,0},{8,9},{9,10},{10,1... | collective-permute-start | bytes 1572872 | tf_op jit(solution)/shard_map/ppermute | solution.py:26
  39.3 4.8 %collective-permute-start.10 = (f32[512,256]{1,0:T(8,128)}, f32[512,256]{1,0:T(8,128)}, u32[]{:S(2)}, u32[]{:S(2)}) collective-permute-start(f32[512,256]{1,0:T(8,128)} %get-tuple-element.54.f3), channel_id=1, source_target_pairs={{0,248},{8,0},{16,8},{24,16},{32,24},{40,32},{48,40},{56,48},{64,5... | collective-permute-start | bytes 1572872 | tf_op jit(solution)/shard_map/ppermute | solution.py:26
  44.1 19.6 %all_to_all.30 = f32[16,8,384]{2,1,0:T(8,128)} all-to-all(f32[16,8,384]{2,1,0:T(8,128)S(1)} %add_bitcast_fusion.1), channel_id=1, replica_groups=mesh['z'=8,'y'=4,'x'=4,'core'=2] {'y','x'}, dimensions={0} | all-to-all | bytes 393216 | tf_op jit(solution)/shard_map/all_to_all | solution.py:264
  64.7 12.8 %all_to_all.31.got = f32[8,8,384]{2,1,0:T(8,128)S(1)} all-to-all(f32[8,8,384]{2,1,0:T(8,128)S(1)} %broadcast_in_dim.18), channel_id=1, replica_groups=mesh['z'=8,'y'=4,'x'=4,'core'=2] {'z'}, dimensions={0} | all-to-all | bytes 196608 | tf_op jit(solution)/shard_map/all_to_all | solution.py:266
  77.9 10.8 %all_to_all.32 = f32[16,8,384]{2,1,0:T(8,128)S(1)} all-to-all(f32[16,8,384]{2,1,0:T(8,128)S(1)} %get-tuple-element.56), channel_id=1, replica_groups=mesh['z'=8,'y'=4,'x'=4,'core'=2] {'y','x'}, dimensions={0} | all-to-all | bytes 393216 | tf_op jit(solution)/shard_map/all_to_all | solution.py:270
  88.7 3.4 %collective-permute-start.12 = (f32[128,384]{1,0:T(8,128)S(1)}, f32[128,384]{1,0:T(8,128)S(1)}, u32[]{:S(2)}, u32[]{:S(2)}) collective-permute-start(f32[128,384]{1,0:T(8,128)S(1)} %bitcast.35), channel_id=1, source_target_pairs={{0,1},{1,0},{2,3},{3,2},{4,5},{5,4},{6,7},{7,6},{8,9},{9,8},{10,11... | collective-permute-start | bytes 589832 | tf_op jit(solution)/shard_map/ppermute | solution.py:30
  93.2 2.2 %copy-done.2 = f32[1,1,1024,1024]{3,2,1,0:T(8,128)S(1)} copy-done((f32[1,1,1024,1024]{3,2,1,0:T(8,128)S(1)}, f32[1,1,1024,1024]{3,2,1,0:T(8,128)}, u32[]{:S(2)}) %copy-start.2) | copy-done | bytes 4194328
  97.5 4.8 %precond.1 = (f32[256,256]{1,0:T(8,128)S(1)}, f32[256,256]{1,0:T(8,128)S(1)}, f32[256,256]{1,0:T(8,128)S(1)}, f32[256,256]{1,0:T(8,128)S(1)}, f32[256,256]{1,0:T...) custom-call(s32[2]{0:T(128)S(1)} %pad_add_fusion.place, ...), custom_call_target="tpu_custom_call" | custom-call | flops 1610612736 | bytes 8388608 | tf_op jit(solution)/shard_map/precond/pallas_call | solution.py:310
  103.6 4.8 %collective-permute-start.15 = (f32[256,256]{1,0:T(8,128)S(1)}, f32[256,256]{1,0:T(8,128)S(1)}, u32[]{:S(2)}, u32[]{:S(2)}) collective-permute-start(f32[256,256]{1,0:T(8,128)S(1)} %get-tuple-element.60.f3), channel_id=1, source_target_pairs={{0,248},{8,0},{16,8},{24,16},{32,24},{40,32},{48,40},{56,48},{64,5... | collective-permute-start | bytes 786440 | tf_op jit(solution)/shard_map/ppermute | solution.py:26
  108.3 1.3 collective-permute-done.13.g0
  109.6 2.5 %collective-permute-done.16.g3 = f32[256,256]{1,0:T(8,128)S(1)} collective-permute-done((f32[256,256]{1,0:T(8,128)S(1)}, f32[256,256]{1,0:T(8,128)S(1)}, u32[]{:S(2)}, u32[]{:S(2)}) %collective-permute-start.16) | collective-permute-done | bytes 262176 | tf_op jit(solution)/shard_map/ppermute | solution.py:26
  112.1 3.2 %flex_second.1 = (f32[256,256]{1,0:T(8,128)S(1)}, f32[256,256]{1,0:T(8,128)S(1)}, f32[256,256]{1,0:T(8,128)S(1)}, f32[256,256]{1,0:T(8,128)S(1)}, f32[256,256]{1...) custom-call(s32[2]{0:T(128)S(1)} %pad_add_fusion.place, ...), custom_call_target="tpu_custom_call" | custom-call | flops 1610612736 | bytes 8388608 | tf_op jit(solution)/shard_map/flex_second/pallas_call | solution.py:314
  118.8 3.9 %collective-permute-start.17 = (f32[128,384]{1,0:T(8,128)S(1)}, f32[128,384]{1,0:T(8,128)S(1)}, u32[]{:S(2)}, u32[]{:S(2)}) collective-permute-start(f32[128,384]{1,0:T(8,128)S(1)} %get-tuple-element.66), channel_id=1, source_target_pairs={{0,1},{1,0},{2,3},{3,2},{4,5},{5,4},{6,7},{7,6},{8,9},{9,8},{10,11... | collective-permute-start | bytes 589832 | tf_op jit(solution)/shard_map/ppermute | solution.py:30
  122.8 1.1 collective-permute-done.17
  124.5 4.5 %all-to-all-start.3 = ((f32[16,8,384]{2,1,0:T(8,128)}), f32[16,8,384]{2,1,0:T(8,128)S(1)}, u32[]{:S(2)}, u32[]{:S(2)}) async-start(f32[16,8,384]{2,1,0:T(8,128)} %add_bitcast_fusion), calls=%async_computation.3 | async-start | bytes 393216 | tf_op jit(solution)/shard_map/all_to_all | solution.py:264
  129.7 6.2 %collective-permute-start.19 = (f32[256,256]{1,0:T(8,128)}, f32[256,256]{1,0:T(8,128)S(1)}, u32[]{:S(2)}, u32[]{:S(2)}) collective-permute-start(f32[256,256]{1,0:T(8,128)} %copy-done.30), channel_id=1, source_target_pairs={{0,248},{8,0},{16,8},{24,16},{32,24},{40,32},{48,40},{56,48},{64,5... | collective-permute-start | bytes 786440 | tf_op jit(solution)/shard_map/ppermute | solution.py:26
  136.2 12.4 %all_to_all.33.got = f32[8,8,384]{2,1,0:T(8,128)S(1)} all-to-all(f32[8,8,384]{2,1,0:T(8,128)S(1)} %broadcast_in_dim.19), channel_id=1, replica_groups=mesh['z'=8,'y'=4,'x'=4,'core'=2] {'z'}, dimensions={0} | all-to-all | bytes 196608 | tf_op jit(solution)/shard_map/all_to_all | solution.py:266
  149.1 10.2 %all_to_all.34 = f32[16,8,384]{2,1,0:T(8,128)S(1)} all-to-all(f32[16,8,384]{2,1,0:T(8,128)S(1)} %coarse_second.1), channel_id=1, replica_groups=mesh['z'=8,'y'=4,'x'=4,'core'=2] {'y','x'}, dimensions={0} | all-to-all | bytes 393216 | tf_op jit(solution)/shard_map/all_to_all | solution.py:270
  159.3 4.4 %collective-permute-start.20 = (f32[128,384]{1,0:T(8,128)S(1)}, f32[128,384]{1,0:T(8,128)S(1)}, u32[]{:S(2)}, u32[]{:S(2)}) collective-permute-start(f32[128,384]{1,0:T(8,128)S(1)} %bitcast.33), channel_id=1, source_target_pairs={{0,1},{1,0},{2,3},{3,2},{4,5},{5,4},{6,7},{7,6},{8,9},{9,8},{10,11... | collective-permute-start | bytes 589832 | tf_op jit(solution)/shard_map/ppermute | solution.py:30
  168.6 1.9 %final.1 = (f32[256,256]{1,0:T(8,128)}, f32[256,256]{1,0:T(8,128)}, f32[256,256]{1,0:T(8,128)}, f32[256,256]{1,0:T(8,128)}) custom-call(s32[2]{0:T(128)S(1)} %pad_add_fusion.place, f32[8,256]{1,0:T(8,128)S(1)} %get-tuple-element.44.masks, f32[128,384]{1,0:T(8,128)S(1)} %bitcast.34, f32[128,384]{1,0:T(8,128)S(1)} %collective-permute-done.20.other, ...), custom_call_target="tpu_custom_call" | custom-call | tf_op jit(solution)/shard_map/final/pallas_call | solution.py:322
  (96 shorter events, 21.4 us)
Async XLA Ops:
  0.6 16.7 %collective-permute-start.1 = (f32[256,256]{1,0:T(8,128)}, f32[256,256]{1,0:T(8,128)S(1)}, u32[]{:S(2)}, u32[]{:S(2)}) collective-permute-start(f32[256,256]{1,0:T(8,128)} %bitcast.25), channel_id=1, source_target_pairs={{0,1},{1,2},{2,3},{3,4},{4,5},{5,6},{6,7},{7,0},{8,9},{9,10},{10,1... | collective-permute-start | bytes 786440 | tf_op jit(solution)/shard_map/ppermute | solution.py:26
  3.2 14.1 %collective-permute-start.2 = (f32[256,256]{1,0:T(8,128)}, f32[256,256]{1,0:T(8,128)S(1)}, u32[]{:S(2)}, u32[]{:S(2)}) collective-permute-start(f32[256,256]{1,0:T(8,128)} %bitcast.29), channel_id=1, source_target_pairs={{0,8},{8,16},{16,24},{24,32},{32,40},{40,48},{48,56},{56,64},{64,7... | collective-permute-start | bytes 786440 | tf_op jit(solution)/shard_map/ppermute | solution.py:26
  4.5 12.8 %collective-permute-start = (s32[4]{0:T(128)}, s32[4]{0:T(128)S(1)}, u32[]{:S(2)}, u32[]{:S(2)}) collective-permute-start(s32[4]{0:T(128)} %bitcast.37), channel_id=1, source_target_pairs={{0,8},{8,16},{16,24},{24,32},{32,40},{40,48},{48,56},{56,64},{64,7... | collective-permute-start | bytes 56 | tf_op jit(solution)/shard_map/ppermute | solution.py:26
  12.2 16.9 %copy-start.3 = (f32[1,1,1024,1024]{3,2,1,0:T(8,128)S(1)}, f32[1,1,1024,1024]{3,2,1,0:T(8,128)}, u32[]{:S(2)}) copy-start(f32[1,1,1024,1024]{3,2,1,0:T(8,128)} %param.7) | copy-start | bytes 12582916
  12.2 16.9 %copy-start.5 = (f32[1,1,256,1024]{3,2,1,0:T(8,128)S(1)}, f32[1,1,256,1024]{3,2,1,0:T(8,128)}, u32[]{:S(2)}) copy-start(f32[1,1,256,1024]{3,2,1,0:T(8,128)} %param.9) | copy-start | bytes 3145732
  12.2 16.9 %copy-start.7 = (f32[1,1,256,256]{3,2,1,0:T(8,128)S(1)}, f32[1,1,256,256]{3,2,1,0:T(8,128)}, u32[]{:S(2)}) copy-start(f32[1,1,256,256]{3,2,1,0:T(8,128)} %param.11) | copy-start | bytes 786436
  12.3 16.9 %copy-start.9 = (f32[1,1,256,256]{3,2,1,0:T(8,128)S(1)}, f32[1,1,256,256]{3,2,1,0:T(8,128)}, u32[]{:S(2)}) copy-start(f32[1,1,256,256]{3,2,1,0:T(8,128)} %param.12) | copy-start | bytes 786436
  18.9 5.8 %collective-permute-start.4 = (f32[256,256]{1,0:T(8,128)S(1)}, f32[256,256]{1,0:T(8,128)S(1)}, u32[]{:S(2)}, u32[]{:S(2)}) collective-permute-start(f32[256,256]{1,0:T(8,128)S(1)} %get-tuple-element.45.f0), channel_id=1, source_target_pairs={{0,1},{1,2},{2,3},{3,4},{4,5},{5,6},{6,7},{7,0},{8,9},{9,10},{10,1... | collective-permute-start | bytes 786440 | tf_op jit(solution)/shard_map/ppermute | solution.py:26
  19.9 6.1 %collective-permute-start.3 = (f32[256,256]{1,0:T(8,128)S(1)}, f32[256,256]{1,0:T(8,128)S(1)}, u32[]{:S(2)}, u32[]{:S(2)}) collective-permute-start(f32[256,256]{1,0:T(8,128)S(1)} %get-tuple-element.46.f1), channel_id=1, source_target_pairs={{0,7},{1,0},{2,1},{3,2},{4,3},{5,4},{6,5},{7,6},{8,15},{9,8},{10,9... | collective-permute-start | bytes 786440 | tf_op jit(solution)/shard_map/ppermute | solution.py:26
  19.9 9.3 %collective-permute-start.6 = (f32[256,256]{1,0:T(8,128)S(1)}, f32[256,256]{1,0:T(8,128)S(1)}, u32[]{:S(2)}, u32[]{:S(2)}) collective-permute-start(f32[256,256]{1,0:T(8,128)S(1)} %get-tuple-element.47.f2), channel_id=1, source_target_pairs={{0,8},{8,16},{16,24},{24,32},{32,40},{40,48},{48,56},{56,64},{64,7... | collective-permute-start | bytes 786440 | tf_op jit(solution)/shard_map/ppermute | solution.py:26
  19.9 9.3 %collective-permute-start.5 = (f32[256,256]{1,0:T(8,128)S(1)}, f32[256,256]{1,0:T(8,128)S(1)}, u32[]{:S(2)}, u32[]{:S(2)}) collective-permute-start(f32[256,256]{1,0:T(8,128)S(1)} %get-tuple-element.48.f3), channel_id=1, source_target_pairs={{0,248},{8,0},{16,8},{24,16},{32,24},{40,32},{48,40},{56,48},{64,5... | collective-permute-start | bytes 786440 | tf_op jit(solution)/shard_map/ppermute | solution.py:26
  29.2 48.3 %copy-start.10 = (f32[256,256]{1,0:T(8,128)S(1)}, f32[256,256]{1,0:T(8,128)}, u32[]{:S(2)}) copy-start(f32[256,256]{1,0:T(8,128)} %coarse.3) | copy-start | bytes 786436
  34.7 57.4 %copy-start.11 = (f32[512,256]{1,0:T(8,128)}, f32[512,256]{1,0:T(8,128)S(1)}, u32[]{:S(2)}) copy-start(f32[512,256]{1,0:T(8,128)S(1)} %get-tuple-element.53.f0) | copy-start | bytes 1572868
  34.7 57.4 %copy-start.13 = (f32[512,256]{1,0:T(8,128)}, f32[512,256]{1,0:T(8,128)S(1)}, u32[]{:S(2)}) copy-start(f32[512,256]{1,0:T(8,128)S(1)} %get-tuple-element.52.f1) | copy-start | bytes 1572868
  34.7 9.3 %collective-permute-start.7 = (f32[128,384]{1,0:T(8,128)S(1)}, f32[128,384]{1,0:T(8,128)S(1)}, u32[]{:S(2)}, u32[]{:S(2)}) collective-permute-start(f32[128,384]{1,0:T(8,128)S(1)} %get-tuple-element.50), channel_id=1, source_target_pairs={{0,1},{1,0},{2,3},{3,2},{4,5},{5,4},{6,7},{7,6},{8,9},{9,8},{10,11... | collective-permute-start | bytes 589832 | tf_op jit(solution)/shard_map/ppermute | solution.py:30
  37.5 40.4 %collective-permute-start.8 = (f32[512,256]{1,0:T(8,128)S(1)}, f32[512,256]{1,0:T(8,128)}, u32[]{:S(2)}, u32[]{:S(2)}) collective-permute-start(f32[512,256]{1,0:T(8,128)S(1)} %get-tuple-element.52.f1), channel_id=1, source_target_pairs={{0,7},{1,0},{2,1},{3,2},{4,3},{5,4},{6,5},{7,6},{8,15},{9,8},{10,9... | collective-permute-start | bytes 1572872 | tf_op jit(solution)/shard_map/ppermute | solution.py:26
  37.5 40.4 %collective-permute-start.9 = (f32[512,256]{1,0:T(8,128)S(1)}, f32[512,256]{1,0:T(8,128)}, u32[]{:S(2)}, u32[]{:S(2)}) collective-permute-start(f32[512,256]{1,0:T(8,128)S(1)} %get-tuple-element.53.f0), channel_id=1, source_target_pairs={{0,1},{1,2},{2,3},{3,4},{4,5},{5,6},{6,7},{7,0},{8,9},{9,10},{10,1... | collective-permute-start | bytes 1572872 | tf_op jit(solution)/shard_map/ppermute | solution.py:26
  39.3 38.6 %collective-permute-start.10 = (f32[512,256]{1,0:T(8,128)}, f32[512,256]{1,0:T(8,128)}, u32[]{:S(2)}, u32[]{:S(2)}) collective-permute-start(f32[512,256]{1,0:T(8,128)} %get-tuple-element.54.f3), channel_id=1, source_target_pairs={{0,248},{8,0},{16,8},{24,16},{32,24},{40,32},{48,40},{56,48},{64,5... | collective-permute-start | bytes 1572872 | tf_op jit(solution)/shard_map/ppermute | solution.py:26
  44.0 33.9 %collective-permute-start.11 = (f32[512,256]{1,0:T(8,128)}, f32[512,256]{1,0:T(8,128)}, u32[]{:S(2)}, u32[]{:S(2)}) collective-permute-start(f32[512,256]{1,0:T(8,128)} %get-tuple-element.55.f2), channel_id=1, source_target_pairs={{0,8},{8,16},{16,24},{24,32},{32,40},{40,48},{48,56},{56,64},{64,7... | collective-permute-start | bytes 1572872 | tf_op jit(solution)/shard_map/ppermute | solution.py:26
  88.7 4.5 %collective-permute-start.12 = (f32[128,384]{1,0:T(8,128)S(1)}, f32[128,384]{1,0:T(8,128)S(1)}, u32[]{:S(2)}, u32[]{:S(2)}) collective-permute-start(f32[128,384]{1,0:T(8,128)S(1)} %bitcast.35), channel_id=1, source_target_pairs={{0,1},{1,0},{2,3},{3,2},{4,5},{5,4},{6,7},{7,6},{8,9},{9,8},{10,11... | collective-permute-start | bytes 589832 | tf_op jit(solution)/shard_map/ppermute | solution.py:30
  103.0 5.3 %collective-permute-start.14 = (f32[256,256]{1,0:T(8,128)S(1)}, f32[256,256]{1,0:T(8,128)S(1)}, u32[]{:S(2)}, u32[]{:S(2)}) collective-permute-start(f32[256,256]{1,0:T(8,128)S(1)} %get-tuple-element.57.f0), channel_id=1, source_target_pairs={{0,1},{1,2},{2,3},{3,4},{4,5},{5,6},{6,7},{7,0},{8,9},{9,10},{10,1... | collective-permute-start | bytes 786440 | tf_op jit(solution)/shard_map/ppermute | solution.py:26
  103.5 6.1 %collective-permute-start.13 = (f32[256,256]{1,0:T(8,128)S(1)}, f32[256,256]{1,0:T(8,128)S(1)}, u32[]{:S(2)}, u32[]{:S(2)}) collective-permute-start(f32[256,256]{1,0:T(8,128)S(1)} %get-tuple-element.58.f1), channel_id=1, source_target_pairs={{0,7},{1,0},{2,1},{3,2},{4,3},{5,4},{6,5},{7,6},{8,15},{9,8},{10,9... | collective-permute-start | bytes 786440 | tf_op jit(solution)/shard_map/ppermute | solution.py:26
  103.6 8.5 %collective-permute-start.16 = (f32[256,256]{1,0:T(8,128)S(1)}, f32[256,256]{1,0:T(8,128)S(1)}, u32[]{:S(2)}, u32[]{:S(2)}) collective-permute-start(f32[256,256]{1,0:T(8,128)S(1)} %get-tuple-element.59.f2), channel_id=1, source_target_pairs={{0,8},{8,16},{16,24},{24,32},{32,40},{40,48},{48,56},{56,64},{64,7... | collective-permute-start | bytes 786440 | tf_op jit(solution)/shard_map/ppermute | solution.py:26
  103.6 8.5 %collective-permute-start.15 = (f32[256,256]{1,0:T(8,128)S(1)}, f32[256,256]{1,0:T(8,128)S(1)}, u32[]{:S(2)}, u32[]{:S(2)}) collective-permute-start(f32[256,256]{1,0:T(8,128)S(1)} %get-tuple-element.60.f3), channel_id=1, source_target_pairs={{0,248},{8,0},{16,8},{24,16},{32,24},{40,32},{48,40},{56,48},{64,5... | collective-permute-start | bytes 786440 | tf_op jit(solution)/shard_map/ppermute | solution.py:26
  112.1 52.7 %copy-start.16 = (f32[256,256]{1,0:T(8,128)S(1)}, f32[256,256]{1,0:T(8,128)}, u32[]{:S(2)}) copy-start(f32[256,256]{1,0:T(8,128)} %copy-done.15) | copy-start | bytes 786436
  112.1 52.7 %copy-start.18 = (f32[256,256]{1,0:T(8,128)S(1)}, f32[256,256]{1,0:T(8,128)}, u32[]{:S(2)}) copy-start(f32[256,256]{1,0:T(8,128)} %copy-done.17) | copy-start | bytes 786436
  112.1 52.7 %copy-start.22 = (f32[256,256]{1,0:T(8,128)S(1)}, f32[256,256]{1,0:T(8,128)}, u32[]{:S(2)}) copy-start(f32[256,256]{1,0:T(8,128)} %copy-done.21) | copy-start | bytes 786436
  118.8 5.0 %collective-permute-start.17 = (f32[128,384]{1,0:T(8,128)S(1)}, f32[128,384]{1,0:T(8,128)S(1)}, u32[]{:S(2)}, u32[]{:S(2)}) collective-permute-start(f32[128,384]{1,0:T(8,128)S(1)} %get-tuple-element.66), channel_id=1, source_target_pairs={{0,1},{1,0},{2,3},{3,2},{4,5},{5,4},{6,7},{7,6},{8,9},{9,8},{10,11... | collective-permute-start | bytes 589832 | tf_op jit(solution)/shard_map/ppermute | solution.py:30
  124.5 11.7 %all-to-all-start.3 = ((f32[16,8,384]{2,1,0:T(8,128)}), f32[16,8,384]{2,1,0:T(8,128)S(1)}, u32[]{:S(2)}, u32[]{:S(2)}) async-start(f32[16,8,384]{2,1,0:T(8,128)} %add_bitcast_fusion), calls=%async_computation.3 | async-start | bytes 393216 | tf_op jit(solution)/shard_map/all_to_all | solution.py:264
  129.0 20.1 %collective-permute-start.18 = (f32[256,256]{1,0:T(8,128)}, f32[256,256]{1,0:T(8,128)S(1)}, u32[]{:S(2)}, u32[]{:S(2)}) collective-permute-start(f32[256,256]{1,0:T(8,128)} %copy-done.31), channel_id=1, source_target_pairs={{0,7},{1,0},{2,1},{3,2},{4,3},{5,4},{6,5},{7,6},{8,15},{9,8},{10,9... | collective-permute-start | bytes 786440 | tf_op jit(solution)/shard_map/ppermute | solution.py:26
  129.7 19.4 %collective-permute-start.19 = (f32[256,256]{1,0:T(8,128)}, f32[256,256]{1,0:T(8,128)S(1)}, u32[]{:S(2)}, u32[]{:S(2)}) collective-permute-start(f32[256,256]{1,0:T(8,128)} %copy-done.30), channel_id=1, source_target_pairs={{0,248},{8,0},{16,8},{24,16},{32,24},{40,32},{48,40},{56,48},{64,5... | collective-permute-start | bytes 786440 | tf_op jit(solution)/shard_map/ppermute | solution.py:26
  159.3 5.5 %collective-permute-start.20 = (f32[128,384]{1,0:T(8,128)S(1)}, f32[128,384]{1,0:T(8,128)S(1)}, u32[]{:S(2)}, u32[]{:S(2)}) collective-permute-start(f32[128,384]{1,0:T(8,128)S(1)} %bitcast.33), channel_id=1, source_target_pairs={{0,1},{1,0},{2,3},{3,2},{4,5},{5,4},{6,7},{7,6},{8,9},{9,8},{10,11... | collective-permute-start | bytes 589832 | tf_op jit(solution)/shard_map/ppermute | solution.py:30
  (22 other events, 52.0 us)
where the time goes:
time: 171 us; the launch traced here: 170 us
  blocking collectives  65.8 us (38%)
  starting transfers between devices  48.7 us (28%)
  local copies, waits for them, and re-layouts  18.5 us (11%)
  Pallas kernels  18 us (11%)
  waiting for transfers between devices  16.8 us (10%)
  other arithmetic  1.77 us (1%)
    ppermute x17, starting transfers between devices, cyclic(): return lax.ppermute(block, axes, [(i, (i + k) % n) for i in range(n)])  29.7 us
    all_to_all x2, blocking collectives, reduce_rows(): return lax.all_to_all(jnp.broadcast_to(part, (Z, PIECE, WIDE)), 'z', 0, 0)  25.2 us
    all_to_all x2, blocking collectives, gather_rows(): mine = lax.all_to_all(copies, ('y', 'x'), 0, 0).reshape(HALF, WIDE)  21 us
    all_to_all x1, blocking collectives, reduce_rows(): got = lax.all_to_all(block.reshape(Y * X, PIECE, WIDE), ('y', 'x'), 0, 0)  19.6 us
    unnamed x64, local copies, waits for them, and re-layouts  18.4 us
    ppermute x4, starting transfers between devices, swapped(): return lax.ppermute(block, 'core', [(0, 1), (1, 0)])  14.6 us
    ppermute x17, waiting for transfers between devices, cyclic(): return lax.ppermute(block, axes, [(i, (i + k) % n) for i in range(n)])  13.3 us
    pallas_call x1, Pallas kernels, local(): call(precond_kernel, field + [face] * 6 + [(CASES, 128)], 17, 'precond',...  4.78 us
  transfers between devices with their start and end apart: 22, of which 9 were waited for; matrix products, arithmetic and copies ran while one was open for 1% of the time, Pallas kernels for 1%

commit v1 on v0

--- a/solution.py
+++ b/solution.py
@@ -62,14 +62,14 @@
     return pl.CostEstimate(flops=6 * rows * IFACE * IFACE, bytes_accessed=8 << 20, transcendentals=0)
 
 
-def call(body, outs, n_in, name, smem=(), scratch=(), estimate=None):
+def call(body, outs, n_in, name, smem=(), scratch=(), estimate=None, grant=2):
     return pl.pallas_call(
         body,
         out_shape=tuple(jax.ShapeDtypeStruct(s, F32) for s in outs),
         in_specs=[SMEM if i in smem else VMEM for i in range(n_in)],
         out_specs=tuple(VMEM for _ in outs),
         scratch_shapes=list(scratch),
-        compiler_params=pltpu.CompilerParams(vmem_limit_bytes=24 << 20),
+        compiler_params=pltpu.CompilerParams(vmem_limit_bytes=grant << 20),
         cost_estimate=estimate,
         name=name,
     )
@@ -87,6 +87,11 @@
 
 
 U_SCRATCH = (pltpu.VMEM((CASES, IFACE), BF16), pltpu.VMEM((CASES, IFACE), BF16))
+
+
+def position():
+    span = lax.axis_index("z") * Y + lax.axis_index("y")
+    return span, lax.axis_index("x") * 2 + lax.axis_index("core")
 
 
 def live_row(ref, on):
@@ -104,17 +109,17 @@
     )
 
 
-def own_kernel(place, active, deck, joint, matrix, part):
-    span, across = place[0], place[1]
+def own_kernel(active, deck, joint, matrix, part):
+    span, across = position()
     first = parts((across < DECKS - 1).astype(F32) * deck[...])
     third = parts(live_row(active, span < SPANS - 1) * joint[...])
     for i in range(4):
         part[:, i * FACE : (i + 1) * FACE] = faces_times(first, third, matrix, 0, i)
 
 
-def behind_kernel(place, active, active_behind, deck_behind, joint_behind, part, matrix,
+def behind_kernel(active, active_behind, deck_behind, joint_behind, part, matrix,
                   v0, v1, v2, v3, masks):
-    span, across = place[0], place[1]
+    span, across = position()
     ones = jnp.ones((1, FACE), F32)
     lives = (
         ones * (across < DECKS - 1).astype(F32),
@@ -132,10 +137,10 @@
     return masks[i : i + 1, :] * (own[i][: CASES, :] - got[i][: CASES, :])
 
 
-def flex_kernel(n_faces, place, masks, f0, f1, f2, f3, g0, g1, g2, g3, matrix, corners, *refs):
+def flex_kernel(n_faces, masks, f0, f1, f2, f3, g0, g1, g2, g3, matrix, corners, *refs):
     pairs, refs = refs[: 2 * n_faces], refs[2 * n_faces :]
     outs, (first, third, sent, held, u_high, u_low, u_full, table) = refs[:4], refs[4:]
-    core = lax.rem(place[1], 2)
+    core = lax.axis_index("core")
     own, got = (f0, f1, f2, f3), (g0, g1, g2, g3)
     for i in range(4):
         value = jump(masks, own, got, i)
@@ -199,17 +204,17 @@
         out[k] = row
 
 
-def place_rows(place, mine, other, whole):
-    core = lax.rem(place[1], 2)
+def place_rows(mine, other, whole):
+    core = lax.axis_index("core")
     whole[pl.ds(pl.multiple_of(core * HALF, HALF), HALF), :] = mine[...]
     whole[pl.ds(pl.multiple_of((1 - core) * HALF, HALF), HALF), :] = other[...]
 
 
-def precond_kernel(place, masks, mine, other, f0, f1, f2, f3, g0, g1, g2, g3,
+def precond_kernel(masks, mine, other, f0, f1, f2, f3, g0, g1, g2, g3,
                    deck, joint, deck_behind, joint_behind, matrix,
                    v0, v1, v2, v3, image_deck, image_joint, res_deck, res_joint,
                    corner_deck, corner_joint, steps, u_high, u_low, whole):
-    place_rows(place, mine, other, whole)
+    place_rows(mine, other, whole)
     load = parts(whole[:, :NC])
     step = whole[:, NC : NC + 1]
     steps[...] = whole[:, NC:]
@@ -233,10 +238,10 @@
     times_matrix(u_high, u_low, matrix, store)
 
 
-def final_kernel(place, masks, mine, other, steps, z_deck, z_joint, y_deck, y_joint,
+def final_kernel(masks, mine, other, steps, z_deck, z_joint, y_deck, y_joint,
                  image_deck, image_joint, res_deck, res_joint, corner_deck, corner_joint,
                  f0, f2, g0, g2, sol_deck, sol_joint, out_deck, out_joint, whole):
-    place_rows(place, mine, other, whole)
+    place_rows(mine, other, whole)
     load = parts(whole[:, :NC])
     second, mixed = whole[:, NC : NC + 1], whole[:, NC + 1 : NC + 2]
     first = steps[:, 0:1] + mixed
@@ -259,11 +264,25 @@
     return left_got, right_got, behind_got, ahead_got
 
 
+def add_kernel(held, got, out):
+    for k in range(Y * X):
+        at = slice(k * PIECE, (k + 1) * PIECE)
+        out[k] = held[at, :] + got[at, :]
+
+
+def spread_kernel(got, out):
+    part = got[0]
+    for k in range(1, Y * X):
+        part = part + got[k]
+    for k in range(Z):
+        out[k] = part
+
+
 def reduce_rows(sent, held):
-    block = held + swapped(sent)
-    got = lax.all_to_all(block.reshape(Y * X, PIECE, WIDE), ("y", "x"), 0, 0)
-    part = jnp.sum(got, axis=0)
-    return lax.all_to_all(jnp.broadcast_to(part, (Z, PIECE, WIDE)), "z", 0, 0)
+    (block,) = call(add_kernel, [(Y * X, PIECE, WIDE)], 2, "add")(held, swapped(sent))
+    got = lax.all_to_all(block, ("y", "x"), 0, 0)
+    (copies,) = call(spread_kernel, [(Z, PIECE, WIDE)], 1, "spread")(got)
+    return lax.all_to_all(copies, "z", 0, 0)
 
 
 def gather_rows(copies):
@@ -278,10 +297,6 @@
 def local(flex, precond, corner_map, coarse_inverse, gap_deck, gap_joint, active):
     flex, precond, corners = flex[0, 0], precond[0, 0], corner_map[0, 0]
     deck, joint, active = gap_deck[0, 0], gap_joint[0, 0], active[0, 0]
-    span = lax.axis_index("z") * Y + lax.axis_index("y")
-    across = lax.axis_index("x") * 2 + lax.axis_index("core")
-    place = jnp.stack([span, across]).astype(jnp.int32)
-
     face, field, stacked = (CASES, FACE), [(CASES, FACE)] * 4, [(2 * CASES, FACE)] * 4
     half, copies = (HALF, WIDE), (Y * X, PIECE, WIDE)
     full = pltpu.VMEM((CASES, IFACE), F32)
@@ -292,15 +307,15 @@
     active_behind = cyclic(active, SPAN, 1)
     gaps = (deck, joint, deck_behind, joint_behind)
     (part,) = call(
-        own_kernel, [(CASES, IFACE)], 5, "own", smem=(0, 1), estimate=cost(CASES // 2)
-    )(place, active, deck, joint, precond)
+        own_kernel, [(CASES, IFACE)], 4, "own", smem=(0,), estimate=cost(CASES // 2), grant=10
+    )(active, deck, joint, precond)
     *v, masks = call(
-        behind_kernel, field + [(8, FACE)], 7, "behind", smem=(0, 1, 2), estimate=cost(CASES // 2)
-    )(place, active, active_behind, deck_behind, joint_behind, part, precond)
+        behind_kernel, field + [(8, FACE)], 6, "behind", smem=(0, 1), estimate=cost(CASES // 2), grant=10
+    )(active, active_behind, deck_behind, joint_behind, part, precond)
     *w, z_deck, z_joint, sent, held = call(
-        functools.partial(flex_kernel, 1), stacked + [face, face, half, half], 14, "flex_first",
-        smem=(0,), scratch=U_SCRATCH + (full, whole), estimate=cost(CASES),
-    )(place, masks, *v, *exchange(v), flex, corners, deck, joint)
+        functools.partial(flex_kernel, 1), stacked + [face, face, half, half], 13, "flex_first",
+        scratch=U_SCRATCH + (full, whole), estimate=cost(CASES), grant=10,
+    )(masks, *v, *exchange(v), flex, corners, deck, joint)
     got = exchange(w)
     sums = reduce_rows(sent, held)
     loads, scalars = call(first_coarse_kernel, [copies, (PIECE, 128)], 2, "coarse_first")(
@@ -308,21 +323,21 @@
     )
     loads = after(loads, got)
     *v, image_deck, image_joint, res_deck, res_joint, corner_deck, corner_joint, steps = call(
-        precond_kernel, field + [face] * 6 + [(CASES, 128)], 17, "precond",
-        smem=(0,), scratch=U_SCRATCH + (whole,), estimate=cost(CASES),
-    )(place, masks, *gather_rows(loads), *w, *got, *gaps, precond)
+        precond_kernel, field + [face] * 6 + [(CASES, 128)], 16, "precond",
+        scratch=U_SCRATCH + (whole,), estimate=cost(CASES), grant=10,
+    )(masks, *gather_rows(loads), *w, *got, *gaps, precond)
     *w, y_deck, y_joint, sent, held = call(
-        functools.partial(flex_kernel, 2), field + [face, face, half, half], 16, "flex_second",
-        smem=(0,), scratch=U_SCRATCH + (full, whole), estimate=cost(CASES),
-    )(place, masks, *v, *exchange(v), flex, corners, res_deck, res_joint, image_deck, image_joint)
+        functools.partial(flex_kernel, 2), field + [face, face, half, half], 15, "flex_second",
+        scratch=U_SCRATCH + (full, whole), estimate=cost(CASES), grant=10,
+    )(masks, *v, *exchange(v), flex, corners, res_deck, res_joint, image_deck, image_joint)
     got = cyclic(w[1], DECK, -1), cyclic(w[3], SPAN, -1)
     sums = reduce_rows(sent, held)
     (loads,) = call(second_coarse_kernel, [copies], 3, "coarse_second")(sums, coarse_inverse, scalars)
     loads = after(loads, got)
     outs = call(
-        final_kernel, [face] * 4, 19, "final", smem=(0,), scratch=(whole,)
+        final_kernel, [face] * 4, 18, "final", scratch=(whole,), grant=6
     )(
-        place, masks, *gather_rows(loads), steps, z_deck, z_joint, y_deck, y_joint,
+        masks, *gather_rows(loads), steps, z_deck, z_joint, y_deck, y_joint,
         image_deck, image_joint, res_deck, res_joint, corner_deck, corner_joint, w[0], w[2], *got,
     )
     return tuple(out[None, None] for out in outs)

time: 171 us -> 154 us (0.901)
  local copies, waits for them, and re-layouts: 18.5 us -> 6.44 us
  Pallas kernels: 18 us -> 15.1 us
  other arithmetic: 1.77 us -> 0 us
    unnamed x64 -> x28, local copies, waits for them, and re-layouts: 18.4 us -> 6.44 us
    pallas_call x4 -> x8, Pallas kernels: 9.8 us -> 8.96 us  [the longest x1 2.72 us: local(): call(precond_kernel, field + [face] * 6 + [(CASES, 128)], 16, 'precond',...]
  transfers between devices with their start and end apart: 22 -> 22, of which waited for: 9 -> 9; matrix products, arithmetic and copies ran while one was open for 1% -> 0% of each run, Pallas kernels for 1% -> 2%
where the time goes in v1:
time: 154 us
  blocking collectives  65.5 us (43%)
  starting transfers between devices  48.8 us (32%)
  waiting for transfers between devices  16.9 us (11%)
  Pallas kernels  15.1 us (10%)
  local copies, waits for them, and re-layouts  6.44 us (4%)
    ppermute x17, starting transfers between devices, cyclic(): return lax.ppermute(block, axes, [(i, (i + k) % n) for i in range(n)])  29.7 us
    all_to_all x2, blocking collectives, reduce_rows(): return lax.all_to_all(copies, 'z', 0, 0)  25.2 us
    all_to_all x2, blocking collectives, gather_rows(): mine = lax.all_to_all(copies, ('y', 'x'), 0, 0).reshape(HALF, WIDE)  21 us
    all_to_all x1, blocking collectives, reduce_rows(): got = lax.all_to_all(block, ('y', 'x'), 0, 0)  19.3 us
    ppermute x4, starting transfers between devices, swapped(): return lax.ppermute(block, 'core', [(0, 1), (1, 0)])  14.6 us
    ppermute x17, waiting for transfers between devices, cyclic(): return lax.ppermute(block, axes, [(i, (i + k) % n) for i in range(n)])  13.4 us
    unnamed x28, local copies, waits for them, and re-layouts  6.44 us
    all_to_all x1, starting transfers between devices, reduce_rows(): got = lax.all_to_all(block, ('y', 'x'), 0, 0)  4.48 us
  transfers between devices with their start and end apart: 22, of which 9 were waited for; matrix products, arithmetic and copies ran while one was open for 0% of the time, Pallas kernels for 2%

profile of v1, /device:TPU:1, one launch (start us, length us, event | category | flops | bytes accessed | tf_op | source)
XLA Modules:
  0.0 153.7 jit_solution(4702436625835095930)
XLA Ops:
  0.6 2.6 %collective-permute-start.1 = (f32[256,256]{1,0:T(8,128)}, f32[256,256]{1,0:T(8,128)S(1)}, u32[]{:S(2)}, u32[]{:S(2)}) collective-permute-start(f32[256,256]{1,0:T(8,128)} %bitcast.19), channel_id=1, source_target_pairs={{0,1},{1,2},{2,3},{3,4},{4,5},{5,6},{6,7},{7,0},{8,9},{9,10},{10,1... | collective-permute-start | bytes 786440 | tf_op jit(solution)/shard_map/ppermute | solution.py:26
  3.2 1.3 collective-permute-start.2
  4.5 1.3 collective-permute-start
  5.8 2.2 %copy-done = f32[1,1,1024,1024]{3,2,1,0:T(8,128)S(1)} copy-done((f32[1,1,1024,1024]{3,2,1,0:T(8,128)S(1)}, f32[1,1,1024,1024]{3,2,1,0:T(8,128)}, u32[]{:S(2)}) %copy-start) | copy-done | bytes 4194328
  10.6 1.6 %own.1.part = f32[256,1024]{1,0:T(8,128)S(1)} custom-call(s32[4]{0:T(128)S(1)} %bitcast.32, f32[256,256]{1,0:T(8,128)S(1)} %bitcast.20, f32[256,256]{1,0:T(8,128)S(1)} %bitcast.24, f32[1024,1024]{1,0:T(8,128)S(1)} %bitcast.12), custom_call_target="tpu_custom_call" | custom-call | flops 805306368 | bytes 8388608 | tf_op jit(solution)/shard_map/own/pallas_call | solution.py:309
  12.2 5.1 %collective-permute-done.active_behind = s32[4]{0:T(128)S(1)} collective-permute-done((s32[4]{0:T(128)}, s32[4]{0:T(128)S(1)}, u32[]{:S(2)}, u32[]{:S(2)}) %collective-permute-start) | collective-permute-done | bytes 48 | tf_op jit(solution)/shard_map/ppermute | solution.py:26
  17.3 1.6 %behind.1 = (f32[256,256]{1,0:T(8,128)S(1)}, f32[256,256]{1,0:T(8,128)S(1)}, f32[256,256]{1,0:T(8,128)S(1)}, f32[256,256]{1,0:T(8,128)S(1)}, f32[8,256]{1,0:T(8,128)S(1)}) custom-call(s32[4]{0:T(128)S(1)} %bitcast.33, s32[4]{0:T(128)S(1)} %collective-permute-done.active_behind, f32[256,256]{1,0:T(8,128)S(1)} %collective-permute-done.1.deck_behind, ...), custom_call_target="tpu_custom_call" | custom-call | flops 805306368 | bytes 8388608 | tf_op jit(solution)/shard_map/behind/pallas_call | solution.py:312
  19.9 4.8 %collective-permute-start.5 = (f32[256,256]{1,0:T(8,128)S(1)}, f32[256,256]{1,0:T(8,128)S(1)}, u32[]{:S(2)}, u32[]{:S(2)}) collective-permute-start(f32[256,256]{1,0:T(8,128)S(1)} %get-tuple-element.48.f3), channel_id=1, source_target_pairs={{0,248},{8,0},{16,8},{24,16},{32,24},{40,32},{48,40},{56,48},{64,5... | collective-permute-start | bytes 786440 | tf_op jit(solution)/shard_map/ppermute | solution.py:26
  24.7 1.3 collective-permute-done.3.g0
  26.0 3.2 %collective-permute-done.6.g3 = f32[256,256]{1,0:T(8,128)S(1)} collective-permute-done((f32[256,256]{1,0:T(8,128)S(1)}, f32[256,256]{1,0:T(8,128)S(1)}, u32[]{:S(2)}, u32[]{:S(2)}) %collective-permute-start.6) | collective-permute-done | bytes 262176 | tf_op jit(solution)/shard_map/ppermute | solution.py:26
  29.2 2.7 %flex_first.1 = (f32[512,256]{1,0:T(8,128)S(1)}, f32[512,256]{1,0:T(8,128)S(1)}, f32[512,256]{1,0:T(8,128)S(1)}, f32[512,256]{1,0:T(8,128)S(1)}, f32[256,256]{1,...) custom-call(f32[8,256]{1,0:T(8,128)S(1)} %get-tuple-element.44.masks, ...), custom_call_target="tpu_custom_call" | custom-call | flops 1610612736 | bytes 8388608 | tf_op jit(solution)/shard_map/flex_first/pallas_call | solution.py:315
  31.9 2.9 %collective-permute-start.7 = (f32[128,384]{1,0:T(8,128)S(1)}, f32[128,384]{1,0:T(8,128)S(1)}, u32[]{:S(2)}, u32[]{:S(2)}) collective-permute-start(f32[128,384]{1,0:T(8,128)S(1)} %get-tuple-element.50), channel_id=1, source_target_pairs={{0,1},{1,0},{2,3},{3,2},{4,5},{5,4},{6,7},{7,6},{8,9},{9,8},{10,11... | collective-permute-start | bytes 589832 | tf_op jit(solution)/shard_map/ppermute | solution.py:30
  34.7 1.7 %collective-permute-start.9 = (f32[512,256]{1,0:T(8,128)S(1)}, f32[512,256]{1,0:T(8,128)S(1)}, u32[]{:S(2)}, u32[]{:S(2)}) collective-permute-start(f32[512,256]{1,0:T(8,128)S(1)} %get-tuple-element.53.f0), channel_id=1, source_target_pairs={{0,1},{1,2},{2,3},{3,4},{4,5},{5,6},{6,7},{7,0},{8,9},{9,10},{10,1... | collective-permute-start | bytes 1572872 | tf_op jit(solution)/shard_map/ppermute | solution.py:26
  36.5 4.8 %collective-permute-start.10 = (f32[512,256]{1,0:T(8,128)S(1)}, f32[512,256]{1,0:T(8,128)S(1)}, u32[]{:S(2)}, u32[]{:S(2)}) collective-permute-start(f32[512,256]{1,0:T(8,128)S(1)} %get-tuple-element.54.f3), channel_id=1, source_target_pairs={{0,248},{8,0},{16,8},{24,16},{32,24},{40,32},{48,40},{56,48},{64,5... | collective-permute-start | bytes 1572872 | tf_op jit(solution)/shard_map/ppermute | solution.py:26
  41.3 19.3 %all_to_all.30.got = f32[16,8,384]{2,1,0:T(8,128)S(1)} all-to-all(f32[16,8,384]{2,1,0:T(8,128)S(1)} %add.2), channel_id=1, replica_groups=mesh['z'=8,'y'=4,'x'=4,'core'=2] {'y','x'}, dimensions={0} | all-to-all | bytes 393216 | tf_op jit(solution)/shard_map/all_to_all | solution.py:283
  60.6 12.8 %all_to_all.31.got = f32[8,8,384]{2,1,0:T(8,128)S(1)} all-to-all(f32[8,8,384]{2,1,0:T(8,128)S(1)} %spread.2), channel_id=1, replica_groups=mesh['z'=8,'y'=4,'x'=4,'core'=2] {'z'}, dimensions={0} | all-to-all | bytes 196608 | tf_op jit(solution)/shard_map/all_to_all | solution.py:285
  73.9 10.8 %all_to_all.32 = f32[16,8,384]{2,1,0:T(8,128)S(1)} all-to-all(f32[16,8,384]{2,1,0:T(8,128)S(1)} %get-tuple-element.56), channel_id=1, replica_groups=mesh['z'=8,'y'=4,'x'=4,'core'=2] {'y','x'}, dimensions={0} | all-to-all | bytes 393216 | tf_op jit(solution)/shard_map/all_to_all | solution.py:289
  84.7 3.4 %collective-permute-start.12 = (f32[128,384]{1,0:T(8,128)S(1)}, f32[128,384]{1,0:T(8,128)S(1)}, u32[]{:S(2)}, u32[]{:S(2)}) collective-permute-start(f32[128,384]{1,0:T(8,128)S(1)} %bitcast.29), channel_id=1, source_target_pairs={{0,1},{1,0},{2,3},{3,2},{4,5},{5,4},{6,7},{7,6},{8,9},{9,8},{10,11... | collective-permute-start | bytes 589832 | tf_op jit(solution)/shard_map/ppermute | solution.py:30
  88.1 1.1 collective-permute-done.12.other
  89.2 2.7 %precond.1 = (f32[256,256]{1,0:T(8,128)S(1)}, f32[256,256]{1,0:T(8,128)S(1)}, f32[256,256]{1,0:T(8,128)S(1)}, f32[256,256]{1,0:T(8,128)S(1)}, f32[256,256]{1,0:T...) custom-call(f32[8,256]{1,0:T(8,128)S(1)} %get-tuple-element.44.masks, ...), custom_call_target="tpu_custom_call" | custom-call | flops 1610612736 | bytes 8388608 | tf_op jit(solution)/shard_map/precond/pallas_call | solution.py:325
  92.5 4.8 %collective-permute-start.15 = (f32[256,256]{1,0:T(8,128)S(1)}, f32[256,256]{1,0:T(8,128)S(1)}, u32[]{:S(2)}, u32[]{:S(2)}) collective-permute-start(f32[256,256]{1,0:T(8,128)S(1)} %get-tuple-element.60.f3), channel_id=1, source_target_pairs={{0,248},{8,0},{16,8},{24,16},{32,24},{40,32},{48,40},{56,48},{64,5... | collective-permute-start | bytes 786440 | tf_op jit(solution)/shard_map/ppermute | solution.py:26
  97.2 1.3 collective-permute-done.13.g0
  98.5 2.5 %collective-permute-done.16.g3 = f32[256,256]{1,0:T(8,128)S(1)} collective-permute-done((f32[256,256]{1,0:T(8,128)S(1)}, f32[256,256]{1,0:T(8,128)S(1)}, u32[]{:S(2)}, u32[]{:S(2)}) %collective-permute-start.16) | collective-permute-done | bytes 262176 | tf_op jit(solution)/shard_map/ppermute | solution.py:26
  101.0 2.7 %flex_second.1 = (f32[256,256]{1,0:T(8,128)S(1)}, f32[256,256]{1,0:T(8,128)S(1)}, f32[256,256]{1,0:T(8,128)S(1)}, f32[256,256]{1,0:T(8,128)S(1)}, f32[256,256]{1...) custom-call(f32[8,256]{1,0:T(8,128)S(1)} %get-tuple-element.44.masks, ...), custom_call_target="tpu_custom_call" | custom-call | flops 1610612736 | bytes 8388608 | tf_op jit(solution)/shard_map/flex_second/pallas_call | solution.py:329
  104.4 3.9 %collective-permute-start.17 = (f32[128,384]{1,0:T(8,128)S(1)}, f32[128,384]{1,0:T(8,128)S(1)}, u32[]{:S(2)}, u32[]{:S(2)}) collective-permute-start(f32[128,384]{1,0:T(8,128)S(1)} %get-tuple-element.66), channel_id=1, source_target_pairs={{0,1},{1,0},{2,3},{3,2},{4,5},{5,4},{6,7},{7,6},{8,9},{9,8},{10,11... | collective-permute-start | bytes 589832 | tf_op jit(solution)/shard_map/ppermute | solution.py:30
  108.3 1.1 collective-permute-done.17.got
  110.1 4.5 %all-to-all-start.3 = ((f32[16,8,384]{2,1,0:T(8,128)}), f32[16,8,384]{2,1,0:T(8,128)S(1)}, u32[]{:S(2)}, u32[]{:S(2)}) async-start(f32[16,8,384]{2,1,0:T(8,128)} %add.3), calls=%async_computation.3 | async-start | bytes 393216 | tf_op jit(solution)/shard_map/all_to_all | solution.py:283
  115.3 6.2 %collective-permute-start.19 = (f32[256,256]{1,0:T(8,128)}, f32[256,256]{1,0:T(8,128)}, u32[]{:S(2)}, u32[]{:S(2)}) collective-permute-start(f32[256,256]{1,0:T(8,128)} %copy-done.12), channel_id=1, source_target_pairs={{0,248},{8,0},{16,8},{24,16},{32,24},{40,32},{48,40},{56,48},{64,5... | collective-permute-start | bytes 786440 | tf_op jit(solution)/shard_map/ppermute | solution.py:26
  121.8 12.4 %all_to_all.33.got = f32[8,8,384]{2,1,0:T(8,128)S(1)} all-to-all(f32[8,8,384]{2,1,0:T(8,128)S(1)} %spread.3), channel_id=1, replica_groups=mesh['z'=8,'y'=4,'x'=4,'core'=2] {'z'}, dimensions={0} | all-to-all | bytes 196608 | tf_op jit(solution)/shard_map/all_to_all | solution.py:285
  134.7 10.2 %all_to_all.34 = f32[16,8,384]{2,1,0:T(8,128)S(1)} all-to-all(f32[16,8,384]{2,1,0:T(8,128)S(1)} %coarse_second.1), channel_id=1, replica_groups=mesh['z'=8,'y'=4,'x'=4,'core'=2] {'y','x'}, dimensions={0} | all-to-all | bytes 393216 | tf_op jit(solution)/shard_map/all_to_all | solution.py:289
  144.9 4.4 %collective-permute-start.20 = (f32[128,384]{1,0:T(8,128)S(1)}, f32[128,384]{1,0:T(8,128)S(1)}, u32[]{:S(2)}, u32[]{:S(2)}) collective-permute-start(f32[128,384]{1,0:T(8,128)S(1)} %bitcast.27), channel_id=1, source_target_pairs={{0,1},{1,0},{2,3},{3,2},{4,5},{5,4},{6,7},{7,6},{8,9},{9,8},{10,11... | collective-permute-start | bytes 589832 | tf_op jit(solution)/shard_map/ppermute | solution.py:30
  151.3 2.4 %final.1 = (f32[256,256]{1,0:T(8,128)}, f32[256,256]{1,0:T(8,128)}, f32[256,256]{1,0:T(8,128)}, f32[256,256]{1,0:T(8,128)}) custom-call(f32[8,256]{1,0:T(8,128)S(1)} %get-tuple-element.44.masks, f32[128,384]{1,0:T(8,128)S(1)} %bitcast.28, f32[128,384]{1,0:T(8,128)S(1)} %collective-permute-done.20.other, f32[256,128]{1,0:T(8,128)S(1)} %get-tuple-element.71.steps, ...), custom_call_target="tpu_custom_call" | custom-call | tf_op jit(solution)/shard_map/final/pallas_call | solution.py:337
  (57 shorter events, 9.5 us)
Async XLA Ops:
  0.6 16.7 %collective-permute-start.1 = (f32[256,256]{1,0:T(8,128)}, f32[256,256]{1,0:T(8,128)S(1)}, u32[]{:S(2)}, u32[]{:S(2)}) collective-permute-start(f32[256,256]{1,0:T(8,128)} %bitcast.19), channel_id=1, source_target_pairs={{0,1},{1,2},{2,3},{3,4},{4,5},{5,6},{6,7},{7,0},{8,9},{9,10},{10,1... | collective-permute-start | bytes 786440 | tf_op jit(solution)/shard_map/ppermute | solution.py:26
  3.2 14.1 %collective-permute-start.2 = (f32[256,256]{1,0:T(8,128)}, f32[256,256]{1,0:T(8,128)S(1)}, u32[]{:S(2)}, u32[]{:S(2)}) collective-permute-start(f32[256,256]{1,0:T(8,128)} %bitcast.23), channel_id=1, source_target_pairs={{0,8},{8,16},{16,24},{24,32},{32,40},{40,48},{48,56},{56,64},{64,7... | collective-permute-start | bytes 786440 | tf_op jit(solution)/shard_map/ppermute | solution.py:26
  4.5 12.8 %collective-permute-start = (s32[4]{0:T(128)}, s32[4]{0:T(128)S(1)}, u32[]{:S(2)}, u32[]{:S(2)}) collective-permute-start(s32[4]{0:T(128)} %bitcast.31), channel_id=1, source_target_pairs={{0,8},{8,16},{16,24},{24,32},{32,40},{40,48},{48,56},{56,64},{64,7... | collective-permute-start | bytes 56 | tf_op jit(solution)/shard_map/ppermute | solution.py:26
  5.8 2.2 %copy-start = (f32[1,1,1024,1024]{3,2,1,0:T(8,128)S(1)}, f32[1,1,1024,1024]{3,2,1,0:T(8,128)}, u32[]{:S(2)}) copy-start(f32[1,1,1024,1024]{3,2,1,0:T(8,128)} %param.8) | copy-start | bytes 12582916
  8.0 0.9 copy-start.4
  10.6 6.7 %copy-start.1 = (f32[1,1,1024,1024]{3,2,1,0:T(8,128)S(1)}, f32[1,1,1024,1024]{3,2,1,0:T(8,128)}, u32[]{:S(2)}) copy-start(f32[1,1,1024,1024]{3,2,1,0:T(8,128)} %param.8) | copy-start | bytes 12582916
  12.1 17.0 %copy-start.2 = (f32[1,1,1024,1024]{3,2,1,0:T(8,128)S(1)}, f32[1,1,1024,1024]{3,2,1,0:T(8,128)}, u32[]{:S(2)}) copy-start(f32[1,1,1024,1024]{3,2,1,0:T(8,128)} %param.7) | copy-start | bytes 12582916
  12.2 17.0 %copy-start.3 = (f32[1,1,256,1024]{3,2,1,0:T(8,128)S(1)}, f32[1,1,256,1024]{3,2,1,0:T(8,128)}, u32[]{:S(2)}) copy-start(f32[1,1,256,1024]{3,2,1,0:T(8,128)} %param.9) | copy-start | bytes 3145732
  12.2 17.0 %copy-start.5 = (f32[1,1,256,256]{3,2,1,0:T(8,128)S(1)}, f32[1,1,256,256]{3,2,1,0:T(8,128)}, u32[]{:S(2)}) copy-start(f32[1,1,256,256]{3,2,1,0:T(8,128)} %param.11) | copy-start | bytes 786436
  12.2 17.0 %copy-start.7 = (f32[1,1,256,256]{3,2,1,0:T(8,128)S(1)}, f32[1,1,256,256]{3,2,1,0:T(8,128)}, u32[]{:S(2)}) copy-start(f32[1,1,256,256]{3,2,1,0:T(8,128)} %param.12) | copy-start | bytes 786436
  18.9 5.8 %collective-permute-start.4 = (f32[256,256]{1,0:T(8,128)S(1)}, f32[256,256]{1,0:T(8,128)S(1)}, u32[]{:S(2)}, u32[]{:S(2)}) collective-permute-start(f32[256,256]{1,0:T(8,128)S(1)} %get-tuple-element.45.f0), channel_id=1, source_target_pairs={{0,1},{1,2},{2,3},{3,4},{4,5},{5,6},{6,7},{7,0},{8,9},{9,10},{10,1... | collective-permute-start | bytes 786440 | tf_op jit(solution)/shard_map/ppermute | solution.py:26
  19.9 6.1 %collective-permute-start.3 = (f32[256,256]{1,0:T(8,128)S(1)}, f32[256,256]{1,0:T(8,128)S(1)}, u32[]{:S(2)}, u32[]{:S(2)}) collective-permute-start(f32[256,256]{1,0:T(8,128)S(1)} %get-tuple-element.46.f1), channel_id=1, source_target_pairs={{0,7},{1,0},{2,1},{3,2},{4,3},{5,4},{6,5},{7,6},{8,15},{9,8},{10,9... | collective-permute-start | bytes 786440 | tf_op jit(solution)/shard_map/ppermute | solution.py:26
  19.9 9.3 %collective-permute-start.6 = (f32[256,256]{1,0:T(8,128)S(1)}, f32[256,256]{1,0:T(8,128)S(1)}, u32[]{:S(2)}, u32[]{:S(2)}) collective-permute-start(f32[256,256]{1,0:T(8,128)S(1)} %get-tuple-element.47.f2), channel_id=1, source_target_pairs={{0,8},{8,16},{16,24},{24,32},{32,40},{40,48},{48,56},{56,64},{64,7... | collective-permute-start | bytes 786440 | tf_op jit(solution)/shard_map/ppermute | solution.py:26
  19.9 9.3 %collective-permute-start.5 = (f32[256,256]{1,0:T(8,128)S(1)}, f32[256,256]{1,0:T(8,128)S(1)}, u32[]{:S(2)}, u32[]{:S(2)}) collective-permute-start(f32[256,256]{1,0:T(8,128)S(1)} %get-tuple-element.48.f3), channel_id=1, source_target_pairs={{0,248},{8,0},{16,8},{24,16},{32,24},{40,32},{48,40},{56,48},{64,5... | collective-permute-start | bytes 786440 | tf_op jit(solution)/shard_map/ppermute | solution.py:26
  29.2 44.3 %copy-start.8 = (f32[256,256]{1,0:T(8,128)S(1)}, f32[256,256]{1,0:T(8,128)}, u32[]{:S(2)}) copy-start(f32[256,256]{1,0:T(8,128)} %coarse.3) | copy-start | bytes 786436
  31.9 9.4 %collective-permute-start.7 = (f32[128,384]{1,0:T(8,128)S(1)}, f32[128,384]{1,0:T(8,128)S(1)}, u32[]{:S(2)}, u32[]{:S(2)}) collective-permute-start(f32[128,384]{1,0:T(8,128)S(1)} %get-tuple-element.50), channel_id=1, source_target_pairs={{0,1},{1,0},{2,3},{3,2},{4,5},{5,4},{6,7},{7,6},{8,9},{9,8},{10,11... | collective-permute-start | bytes 589832 | tf_op jit(solution)/shard_map/ppermute | solution.py:30
  34.7 39.1 %collective-permute-start.8 = (f32[512,256]{1,0:T(8,128)S(1)}, f32[512,256]{1,0:T(8,128)S(1)}, u32[]{:S(2)}, u32[]{:S(2)}) collective-permute-start(f32[512,256]{1,0:T(8,128)S(1)} %get-tuple-element.52.f1), channel_id=1, source_target_pairs={{0,7},{1,0},{2,1},{3,2},{4,3},{5,4},{6,5},{7,6},{8,15},{9,8},{10,9... | collective-permute-start | bytes 1572872 | tf_op jit(solution)/shard_map/ppermute | solution.py:26
  34.7 39.1 %collective-permute-start.9 = (f32[512,256]{1,0:T(8,128)S(1)}, f32[512,256]{1,0:T(8,128)S(1)}, u32[]{:S(2)}, u32[]{:S(2)}) collective-permute-start(f32[512,256]{1,0:T(8,128)S(1)} %get-tuple-element.53.f0), channel_id=1, source_target_pairs={{0,1},{1,2},{2,3},{3,4},{4,5},{5,6},{6,7},{7,0},{8,9},{9,10},{10,1... | collective-permute-start | bytes 1572872 | tf_op jit(solution)/shard_map/ppermute | solution.py:26
  36.5 37.4 %collective-permute-start.10 = (f32[512,256]{1,0:T(8,128)S(1)}, f32[512,256]{1,0:T(8,128)S(1)}, u32[]{:S(2)}, u32[]{:S(2)}) collective-permute-start(f32[512,256]{1,0:T(8,128)S(1)} %get-tuple-element.54.f3), channel_id=1, source_target_pairs={{0,248},{8,0},{16,8},{24,16},{32,24},{40,32},{48,40},{56,48},{64,5... | collective-permute-start | bytes 1572872 | tf_op jit(solution)/shard_map/ppermute | solution.py:26
  41.2 32.6 %collective-permute-start.11 = (f32[512,256]{1,0:T(8,128)S(1)}, f32[512,256]{1,0:T(8,128)S(1)}, u32[]{:S(2)}, u32[]{:S(2)}) collective-permute-start(f32[512,256]{1,0:T(8,128)S(1)} %get-tuple-element.55.f2), channel_id=1, source_target_pairs={{0,8},{8,16},{16,24},{24,32},{32,40},{40,48},{48,56},{56,64},{64,7... | collective-permute-start | bytes 1572872 | tf_op jit(solution)/shard_map/ppermute | solution.py:26
  84.7 4.5 %collective-permute-start.12 = (f32[128,384]{1,0:T(8,128)S(1)}, f32[128,384]{1,0:T(8,128)S(1)}, u32[]{:S(2)}, u32[]{:S(2)}) collective-permute-start(f32[128,384]{1,0:T(8,128)S(1)} %bitcast.29), channel_id=1, source_target_pairs={{0,1},{1,0},{2,3},{3,2},{4,5},{5,4},{6,7},{7,6},{8,9},{9,8},{10,11... | collective-permute-start | bytes 589832 | tf_op jit(solution)/shard_map/ppermute | solution.py:30
  91.9 5.3 %collective-permute-start.14 = (f32[256,256]{1,0:T(8,128)S(1)}, f32[256,256]{1,0:T(8,128)S(1)}, u32[]{:S(2)}, u32[]{:S(2)}) collective-permute-start(f32[256,256]{1,0:T(8,128)S(1)} %get-tuple-element.57.f0), channel_id=1, source_target_pairs={{0,1},{1,2},{2,3},{3,4},{4,5},{5,6},{6,7},{7,0},{8,9},{9,10},{10,1... | collective-permute-start | bytes 786440 | tf_op jit(solution)/shard_map/ppermute | solution.py:26
  92.5 6.1 %collective-permute-start.13 = (f32[256,256]{1,0:T(8,128)S(1)}, f32[256,256]{1,0:T(8,128)S(1)}, u32[]{:S(2)}, u32[]{:S(2)}) collective-permute-start(f32[256,256]{1,0:T(8,128)S(1)} %get-tuple-element.58.f1), channel_id=1, source_target_pairs={{0,7},{1,0},{2,1},{3,2},{4,3},{5,4},{6,5},{7,6},{8,15},{9,8},{10,9... | collective-permute-start | bytes 786440 | tf_op jit(solution)/shard_map/ppermute | solution.py:26
  92.5 8.5 %collective-permute-start.16 = (f32[256,256]{1,0:T(8,128)S(1)}, f32[256,256]{1,0:T(8,128)S(1)}, u32[]{:S(2)}, u32[]{:S(2)}) collective-permute-start(f32[256,256]{1,0:T(8,128)S(1)} %get-tuple-element.59.f2), channel_id=1, source_target_pairs={{0,8},{8,16},{16,24},{24,32},{32,40},{40,48},{48,56},{56,64},{64,7... | collective-permute-start | bytes 786440 | tf_op jit(solution)/shard_map/ppermute | solution.py:26
  92.5 8.5 %collective-permute-start.15 = (f32[256,256]{1,0:T(8,128)S(1)}, f32[256,256]{1,0:T(8,128)S(1)}, u32[]{:S(2)}, u32[]{:S(2)}) collective-permute-start(f32[256,256]{1,0:T(8,128)S(1)} %get-tuple-element.60.f3), channel_id=1, source_target_pairs={{0,248},{8,0},{16,8},{24,16},{32,24},{40,32},{48,40},{56,48},{64,5... | collective-permute-start | bytes 786440 | tf_op jit(solution)/shard_map/ppermute | solution.py:26
  104.4 5.0 %copy-start.12 = (f32[256,256]{1,0:T(8,128)}, f32[256,256]{1,0:T(8,128)S(1)}, u32[]{:S(2)}) copy-start(f32[256,256]{1,0:T(8,128)S(1)} %get-tuple-element.69) | copy-start | bytes 786436
  104.4 5.0 %copy-start.13 = (f32[256,256]{1,0:T(8,128)}, f32[256,256]{1,0:T(8,128)S(1)}, u32[]{:S(2)}) copy-start(f32[256,256]{1,0:T(8,128)S(1)} %get-tuple-element.68) | copy-start | bytes 786436
  104.4 5.0 %collective-permute-start.17 = (f32[128,384]{1,0:T(8,128)S(1)}, f32[128,384]{1,0:T(8,128)S(1)}, u32[]{:S(2)}, u32[]{:S(2)}) collective-permute-start(f32[128,384]{1,0:T(8,128)S(1)} %get-tuple-element.66), channel_id=1, source_target_pairs={{0,1},{1,0},{2,3},{3,2},{4,5},{5,4},{6,7},{7,6},{8,9},{9,8},{10,11... | collective-permute-start | bytes 589832 | tf_op jit(solution)/shard_map/ppermute | solution.py:30
  110.1 11.7 %all-to-all-start.3 = ((f32[16,8,384]{2,1,0:T(8,128)}), f32[16,8,384]{2,1,0:T(8,128)S(1)}, u32[]{:S(2)}, u32[]{:S(2)}) async-start(f32[16,8,384]{2,1,0:T(8,128)} %add.3), calls=%async_computation.3 | async-start | bytes 393216 | tf_op jit(solution)/shard_map/all_to_all | solution.py:283
  114.6 20.1 %collective-permute-start.18 = (f32[256,256]{1,0:T(8,128)}, f32[256,256]{1,0:T(8,128)}, u32[]{:S(2)}, u32[]{:S(2)}) collective-permute-start(f32[256,256]{1,0:T(8,128)} %copy-done.13), channel_id=1, source_target_pairs={{0,7},{1,0},{2,1},{3,2},{4,3},{5,4},{6,5},{7,6},{8,15},{9,8},{10,9... | collective-permute-start | bytes 786440 | tf_op jit(solution)/shard_map/ppermute | solution.py:26
  115.3 19.4 %collective-permute-start.19 = (f32[256,256]{1,0:T(8,128)}, f32[256,256]{1,0:T(8,128)}, u32[]{:S(2)}, u32[]{:S(2)}) collective-permute-start(f32[256,256]{1,0:T(8,128)} %copy-done.12), channel_id=1, source_target_pairs={{0,248},{8,0},{16,8},{24,16},{32,24},{40,32},{48,40},{56,48},{64,5... | collective-permute-start | bytes 786440 | tf_op jit(solution)/shard_map/ppermute | solution.py:26
  144.9 5.5 %collective-permute-start.20 = (f32[128,384]{1,0:T(8,128)S(1)}, f32[128,384]{1,0:T(8,128)S(1)}, u32[]{:S(2)}, u32[]{:S(2)}) collective-permute-start(f32[128,384]{1,0:T(8,128)S(1)} %bitcast.27), channel_id=1, source_target_pairs={{0,1},{1,0},{2,3},{3,2},{4,5},{5,4},{6,7},{7,6},{8,9},{9,8},{10,11... | collective-permute-start | bytes 589832 | tf_op jit(solution)/shard_map/ppermute | solution.py:30
  (4 other events, 3.3 us)

commit v2 on v1

--- a/solution.py
+++ b/solution.py
@@ -65,7 +65,7 @@
 def call(body, outs, n_in, name, smem=(), scratch=(), estimate=None, grant=2):
     return pl.pallas_call(
         body,
-        out_shape=tuple(jax.ShapeDtypeStruct(s, F32) for s in outs),
+        out_shape=tuple(s if isinstance(s, jax.ShapeDtypeStruct) else jax.ShapeDtypeStruct(s, F32) for s in outs),
         in_specs=[SMEM if i in smem else VMEM for i in range(n_in)],
         out_specs=tuple(VMEM for _ in outs),
         scratch_shapes=list(scratch),
@@ -75,18 +75,10 @@
     )
 
 
-def times_matrix(u_high, u_low, matrix_ref, store):
-    for i in range(4):
-        store(i, product((u_high[...], u_low[...]), parts(quarter(matrix_ref, i))))
-
-
 def keep(u_high, u_low, i, value):
     high, low = parts(value)
     u_high[:, i * FACE : (i + 1) * FACE] = high
     u_low[:, i * FACE : (i + 1) * FACE] = low
-
-
-U_SCRATCH = (pltpu.VMEM((CASES, IFACE), BF16), pltpu.VMEM((CASES, IFACE), BF16))
 
 
 def position():
@@ -117,8 +109,7 @@
         part[:, i * FACE : (i + 1) * FACE] = faces_times(first, third, matrix, 0, i)
 
 
-def behind_kernel(active, active_behind, deck_behind, joint_behind, part, matrix,
-                  v0, v1, v2, v3, masks):
+def behind_kernel(which, active, active_behind, deck_behind, joint_behind, part, matrix, *outs):
     span, across = position()
     ones = jnp.ones((1, FACE), F32)
     lives = (
@@ -127,9 +118,10 @@
         live_row(active, span < SPANS - 1),
         live_row(active_behind, span > 0),
     )
-    masks[...] = jnp.concatenate(lives + (jnp.zeros((4, FACE), F32),), axis=0)
+    if len(outs) == 3:
+        outs[2][...] = jnp.concatenate(lives + (jnp.zeros((4, FACE), F32),), axis=0)
     second, fourth = parts(lives[1] * deck_behind[...]), parts(lives[3] * joint_behind[...])
-    for i, out in enumerate((v0, v1, v2, v3)):
+    for i, out in zip(which, outs):
         out[...] = 0.5 * (quarter(part, i) - faces_times(second, fourth, matrix, FACE, i))
 
 
@@ -137,21 +129,32 @@
     return masks[i : i + 1, :] * (own[i][: CASES, :] - got[i][: CASES, :])
 
 
-def flex_kernel(n_faces, masks, f0, f1, f2, f3, g0, g1, g2, g3, matrix, corners, *refs):
+def two_quarters(masks, own, got, matrix, corners, at):
+    jumps = [jump(masks, own, got, i) for i in range(2)]
+    high, low = parts(jnp.concatenate(jumps, axis=1))
+    rows = slice(at, at + 2 * FACE)
+    fields = [product((high, low), parts(matrix[rows, i * FACE : (i + 1) * FACE])) for i in range(4)]
+    return jumps, fields, product((high, low), parts(corners[:, rows]), TRANS)
+
+
+def flex_span_kernel(masks, f2, f3, g2, g3, matrix, corners, part, corner_part):
+    _, fields, corner = two_quarters(masks[2:4, :], (f2, f3), (g2, g3), matrix, corners, 2 * FACE)
+    for i in range(4):
+        part[:, i * FACE : (i + 1) * FACE] = fields[i]
+    corner_part[...] = corner
+
+
+def flex_kernel(n_faces, masks, f0, f1, f2, f3, g0, g1, g2, g3, part, corner_part, matrix, corners, *refs):
     pairs, refs = refs[: 2 * n_faces], refs[2 * n_faces :]
-    outs, (first, third, sent, held, u_high, u_low, u_full, table) = refs[:4], refs[4:]
+    outs, (first, third, sent, held, table) = refs[:4], refs[4:]
     core = lax.axis_index("core")
-    own, got = (f0, f1, f2, f3), (g0, g1, g2, g3)
-    for i in range(4):
-        value = jump(masks, own, got, i)
-        keep(u_high, u_low, i, value)
-        u_full[:, i * FACE : (i + 1) * FACE] = value
-    first[...] = quarter(u_full, 0)
-    third[...] = quarter(u_full, 2)
+    late, fields, corner = two_quarters(masks[0:2, :], (f0, f1), (g0, g1), matrix, corners, 0)
+    jumps = late + [jump(masks[2:4, :], (f2, f3), (g2, g3), i) for i in range(2)]
+    first[...], third[...] = jumps[0], jumps[2]
     total = jnp.zeros((CASES, 1), F32)
     for i in range(4):
-        value = product((u_high[...], u_low[...]), parts(quarter(matrix, i)))
-        total = total + row_sum(quarter(u_full, i) * value)
+        value = quarter(part, i) + fields[i]
+        total = total + row_sum(jumps[i] * value)
         if outs[i].shape[0] == CASES:
             outs[i][...] = value
         else:
@@ -161,7 +164,7 @@
         row_sum(masks[0:1, :] * pairs[2 * k][...] * first[...] + masks[2:3, :] * pairs[2 * k + 1][...] * third[...])
         for k in range(n_faces)
     ]
-    table[:, :NC] = product((u_high[...], u_low[...]), parts(corners[...]), TRANS)
+    table[:, :NC] = corner_part[...] + corner
     lane = lax.broadcasted_iota(jnp.int32, (CASES, 128), 1)
     table[:, NC:] = column(lane, total, *sums)
     held[...] = table[pl.ds(pl.multiple_of(core * HALF, HALF), HALF), :]
@@ -212,8 +215,8 @@
 
 def precond_kernel(masks, mine, other, f0, f1, f2, f3, g0, g1, g2, g3,
                    deck, joint, deck_behind, joint_behind, matrix,
-                   v0, v1, v2, v3, image_deck, image_joint, res_deck, res_joint,
-                   corner_deck, corner_joint, steps, u_high, u_low, whole):
+                   v2, v3, u_high, u_low, image_deck, image_joint, res_deck, res_joint,
+                   corner_deck, corner_joint, steps, whole):
     place_rows(mine, other, whole)
     load = parts(whole[:, :NC])
     step = whole[:, NC : NC + 1]
@@ -232,10 +235,20 @@
             corner_joint[...], image_joint[...], res_joint[...] = corner, image, res
         keep(u_high, u_low, i, res)
 
-    def store(i, value):
-        (v0, v1, v2, v3)[i][...] = 0.5 * value
-
-    times_matrix(u_high, u_low, matrix, store)
+    span_quarters(u_high, u_low, matrix, v2, v3)
+
+
+def two_of(first, u_high, u_low, matrix, outs):
+    for i, out in enumerate(outs):
+        out[...] = 0.5 * product((u_high[...], u_low[...]), parts(quarter(matrix, first + i)))
+
+
+def span_quarters(u_high, u_low, matrix, v2, v3):
+    two_of(2, u_high, u_low, matrix, (v2, v3))
+
+
+def deck_quarters(u_high, u_low, matrix, v0, v1):
+    two_of(0, u_high, u_low, matrix, (v0, v1))
 
 
 def final_kernel(masks, mine, other, steps, z_deck, z_joint, y_deck, y_joint,
@@ -278,9 +291,12 @@
         out[k] = part
 
 
-def reduce_rows(sent, held):
+def scatter_rows(sent, held):
     (block,) = call(add_kernel, [(Y * X, PIECE, WIDE)], 2, "add")(held, swapped(sent))
-    got = lax.all_to_all(block, ("y", "x"), 0, 0)
+    return lax.all_to_all(block, ("y", "x"), 0, 0)
+
+
+def along_z(got):
     (copies,) = call(spread_kernel, [(Z, PIECE, WIDE)], 1, "spread")(got)
     return lax.all_to_all(copies, "z", 0, 0)
 
@@ -297,42 +313,60 @@
 def local(flex, precond, corner_map, coarse_inverse, gap_deck, gap_joint, active):
     flex, precond, corners = flex[0, 0], precond[0, 0], corner_map[0, 0]
     deck, joint, active = gap_deck[0, 0], gap_joint[0, 0], active[0, 0]
-    face, field, stacked = (CASES, FACE), [(CASES, FACE)] * 4, [(2 * CASES, FACE)] * 4
-    half, copies = (HALF, WIDE), (Y * X, PIECE, WIDE)
-    full = pltpu.VMEM((CASES, IFACE), F32)
+    face, pair, field, stacked = (CASES, FACE), [(CASES, FACE)] * 2, [(CASES, FACE)] * 4, [(2 * CASES, FACE)] * 4
+    wide, half, copies = (CASES, IFACE), (HALF, WIDE), (Y * X, PIECE, WIDE)
+    narrow = [jax.ShapeDtypeStruct(wide, BF16)] * 2
     whole = pltpu.VMEM((CASES, WIDE), F32)
+
+    def flexed(n_faces, v, name, shapes, *pairs):
+        got = exchange(v)
+        part, corner = call(
+            flex_span_kernel, [wide, (CASES, NC)], 7, name + "_span", estimate=cost(CASES // 2), grant=10
+        )(masks, *v[2:], *got[2:], flex, corners)
+        return call(
+            functools.partial(flex_kernel, n_faces), shapes + [face, face, half, half], 13 + 2 * n_faces,
+            name, scratch=(whole,), estimate=cost(CASES // 2), grant=10,
+        )(masks, *v, *got, part, corner, flex, corners, *pairs)
 
     joint_behind = cyclic(joint, SPAN, 1)
     deck_behind = cyclic(deck, DECK, 1)
     active_behind = cyclic(active, SPAN, 1)
     gaps = (deck, joint, deck_behind, joint_behind)
     (part,) = call(
-        own_kernel, [(CASES, IFACE)], 4, "own", smem=(0,), estimate=cost(CASES // 2), grant=10
+        own_kernel, [wide], 4, "own", smem=(0,), estimate=cost(CASES // 2), grant=10
     )(active, deck, joint, precond)
-    *v, masks = call(
-        behind_kernel, field + [(8, FACE)], 6, "behind", smem=(0, 1), estimate=cost(CASES // 2), grant=10
-    )(active, active_behind, deck_behind, joint_behind, part, precond)
-    *w, z_deck, z_joint, sent, held = call(
-        functools.partial(flex_kernel, 1), stacked + [face, face, half, half], 13, "flex_first",
-        scratch=U_SCRATCH + (full, whole), estimate=cost(CASES), grant=10,
-    )(masks, *v, *exchange(v), flex, corners, deck, joint)
-    got = exchange(w)
-    sums = reduce_rows(sent, held)
+    behind = (active, active_behind, deck_behind, joint_behind, part, precond)
+    v2, v3, masks = call(
+        functools.partial(behind_kernel, (2, 3)), pair + [(8, FACE)], 6, "behind_span",
+        smem=(0, 1), estimate=cost(CASES // 4), grant=10,
+    )(*behind)
+    v0, v1 = call(
+        functools.partial(behind_kernel, (0, 1)), pair, 6, "behind_deck",
+        smem=(0, 1), estimate=cost(CASES // 4), grant=10,
+    )(*behind)
+    *w, z_deck, z_joint, sent, held = flexed(1, (v0, v1, v2, v3), "flex_first", stacked, deck, joint)
+    rows = scatter_rows(sent, held)
+    got = exchange(after(w, rows))
     loads, scalars = call(first_coarse_kernel, [copies, (PIECE, 128)], 2, "coarse_first")(
-        sums, coarse_inverse
+        along_z(rows), coarse_inverse
     )
     loads = after(loads, got)
-    *v, image_deck, image_joint, res_deck, res_joint, corner_deck, corner_joint, steps = call(
-        precond_kernel, field + [face] * 6 + [(CASES, 128)], 16, "precond",
-        scratch=U_SCRATCH + (whole,), estimate=cost(CASES), grant=10,
+    v2, v3, *u, image_deck, image_joint, res_deck, res_joint, corner_deck, corner_joint, steps = call(
+        precond_kernel, pair + narrow + [face] * 6 + [(CASES, 128)], 16, "precond_span",
+        scratch=(whole,), estimate=cost(CASES // 2), grant=10,
     )(masks, *gather_rows(loads), *w, *got, *gaps, precond)
-    *w, y_deck, y_joint, sent, held = call(
-        functools.partial(flex_kernel, 2), field + [face, face, half, half], 15, "flex_second",
-        scratch=U_SCRATCH + (full, whole), estimate=cost(CASES), grant=10,
-    )(masks, *v, *exchange(v), flex, corners, res_deck, res_joint, image_deck, image_joint)
-    got = cyclic(w[1], DECK, -1), cyclic(w[3], SPAN, -1)
-    sums = reduce_rows(sent, held)
-    (loads,) = call(second_coarse_kernel, [copies], 3, "coarse_second")(sums, coarse_inverse, scalars)
+    v0, v1 = call(
+        deck_quarters, pair, 3, "precond_deck", estimate=cost(CASES // 2), grant=10
+    )(*u, precond)
+    *w, y_deck, y_joint, sent, held = flexed(
+        2, (v0, v1, v2, v3), "flex_second", field, res_deck, res_joint, image_deck, image_joint
+    )
+    rows = scatter_rows(sent, held)
+    left, behind = after((w[1], w[3]), rows)
+    got = cyclic(left, DECK, -1), cyclic(behind, SPAN, -1)
+    (loads,) = call(second_coarse_kernel, [copies], 3, "coarse_second")(
+        along_z(rows), coarse_inverse, scalars
+    )
     loads = after(loads, got)
     outs = call(
         final_kernel, [face] * 4, 18, "final", scratch=(whole,), grant=6

time: 154 us -> 148 us (0.961)
  starting transfers between devices: 48.8 us -> 33.6 us
  blocking collectives: 65.5 us -> 72.5 us
  waiting for transfers between devices: 16.9 us -> 21.7 us
  local copies, waits for them, and re-layouts: 6.44 us -> 4.77 us
    ppermute x4, starting transfers between devices: 14.6 us -> 6.11 us  [swapped(): return lax.ppermute(block, 'core', [(0, 1), (1, 0)])]
    all_to_all x3 -> x4, blocking collectives: 44.5 us -> 50.4 us  [the longest x2 26.7 us: along_z(): return lax.all_to_all(copies, 'z', 0, 0)]
    all_to_all x1 -> x0, starting transfers between devices: 4.48 us -> none  [reduce_rows(): got = lax.all_to_all(block, ('y', 'x'), 0, 0)]
    ppermute x17, waiting for transfers between devices: 13.4 us -> 17.1 us  [cyclic(): return lax.ppermute(block, axes, [(i, (i + k) % n) for i in range(n)])]
    ppermute x17, starting transfers between devices: 29.7 us -> 27.5 us  [cyclic(): return lax.ppermute(block, axes, [(i, (i + k) % n) for i in range(n)])]
    unnamed x28 -> x20, local copies, waits for them, and re-layouts: 6.44 us -> 4.77 us
    pallas_call x9 -> x13, Pallas kernels: 11.9 us -> 12.4 us  [the longest x2 3.09 us: flexed(): call(functools.partial(flex_kernel, n_faces), shapes + [face, face, half,...]
  transfers between devices with their start and end apart: 22 -> 21, of which waited for: 9 -> 10; matrix products, arithmetic and copies ran while one was open for 0% -> 0% of each run, Pallas kernels for 2% -> 5%
where the time goes in v2:
time: 148 us
  blocking collectives  72.5 us (49%)
  starting transfers between devices  33.6 us (23%)
  waiting for transfers between devices  21.7 us (15%)
  Pallas kernels  14.6 us (10%)
  local copies, waits for them, and re-layouts  4.77 us (3%)
    ppermute x17, starting transfers between devices, cyclic(): return lax.ppermute(block, axes, [(i, (i + k) % n) for i in range(n)])  27.5 us
    all_to_all x2, blocking collectives, along_z(): return lax.all_to_all(copies, 'z', 0, 0)  26.7 us
    all_to_all x2, blocking collectives, scatter_rows(): return lax.all_to_all(block, ('y', 'x'), 0, 0)  23.7 us
    all_to_all x2, blocking collectives, gather_rows(): mine = lax.all_to_all(copies, ('y', 'x'), 0, 0).reshape(HALF, WIDE)  22.1 us
    ppermute x17, waiting for transfers between devices, cyclic(): return lax.ppermute(block, axes, [(i, (i + k) % n) for i in range(n)])  17.1 us
    ppermute x4, starting transfers between devices, swapped(): return lax.ppermute(block, 'core', [(0, 1), (1, 0)])  6.11 us
    unnamed x20, local copies, waits for them, and re-layouts  4.77 us
    ppermute x4, waiting for transfers between devices, swapped(): return lax.ppermute(block, 'core', [(0, 1), (1, 0)])  4.52 us
  transfers between devices with their start and end apart: 21, of which 10 were waited for; matrix products, arithmetic and copies ran while one was open for 0% of the time, Pallas kernels for 5%

profile of v2, /device:TPU:1, one launch (start us, length us, event | category | flops | bytes accessed | tf_op | source)
XLA Modules:
  0.0 148.0 jit_solution(1292419091489639360)
XLA Ops:
  0.6 2.6 %collective-permute-start.1 = (f32[256,256]{1,0:T(8,128)}, f32[256,256]{1,0:T(8,128)S(1)}, u32[]{:S(2)}, u32[]{:S(2)}) collective-permute-start(f32[256,256]{1,0:T(8,128)} %bitcast.25), channel_id=1, source_target_pairs={{0,1},{1,2},{2,3},{3,4},{4,5},{5,6},{6,7},{7,0},{8,9},{9,10},{10,1... | collective-permute-start | bytes 786440 | tf_op jit(solution)/shard_map/ppermute | solution.py:26
  3.2 1.3 collective-permute-start.2
  4.5 1.3 collective-permute-start
  5.8 2.2 %copy-done = f32[1,1,1024,1024]{3,2,1,0:T(8,128)S(1)} copy-done((f32[1,1,1024,1024]{3,2,1,0:T(8,128)S(1)}, f32[1,1,1024,1024]{3,2,1,0:T(8,128)}, u32[]{:S(2)}) %copy-start) | copy-done | bytes 4194328
  10.6 1.6 %own.1.part = f32[256,1024]{1,0:T(8,128)S(1)} custom-call(s32[4]{0:T(128)S(1)} %bitcast.38, f32[256,256]{1,0:T(8,128)S(1)} %bitcast.26, f32[256,256]{1,0:T(8,128)S(1)} %bitcast.30, f32[1024,1024]{1,0:T(8,128)S(1)} %bitcast.12), custom_call_target="tpu_custom_call" | custom-call | flops 805306368 | bytes 8388608 | tf_op jit(solution)/shard_map/own/pallas_call | solution.py:335
  12.1 5.1 %collective-permute-done.active_behind = s32[4]{0:T(128)S(1)} collective-permute-done((s32[4]{0:T(128)}, s32[4]{0:T(128)S(1)}, u32[]{:S(2)}, u32[]{:S(2)}) %collective-permute-start) | collective-permute-done | bytes 48 | tf_op jit(solution)/shard_map/ppermute | solution.py:26
  18.6 4.8 %collective-permute-start.5 = (f32[256,256]{1,0:T(8,128)S(1)}, f32[256,256]{1,0:T(8,128)S(1)}, u32[]{:S(2)}, u32[]{:S(2)}) collective-permute-start(f32[256,256]{1,0:T(8,128)S(1)} %get-tuple-element.60.f3), channel_id=1, source_target_pairs={{0,248},{8,0},{16,8},{24,16},{32,24},{40,32},{48,40},{56,48},{64,5... | collective-permute-start | bytes 786440 | tf_op jit(solution)/shard_map/ppermute | solution.py:26
  23.4 1.1 behind_deck.1
  24.5 1.6 %collective-permute-start.4 = (f32[256,256]{1,0:T(8,128)S(1)}, f32[256,256]{1,0:T(8,128)S(1)}, u32[]{:S(2)}, u32[]{:S(2)}) collective-permute-start(f32[256,256]{1,0:T(8,128)S(1)} %get-tuple-element.57.f0), channel_id=1, source_target_pairs={{0,1},{1,2},{2,3},{3,4},{4,5},{5,6},{6,7},{7,0},{8,9},{9,10},{10,1... | collective-permute-start | bytes 786440 | tf_op jit(solution)/shard_map/ppermute | solution.py:26
  26.1 3.9 %collective-permute-done.6.g3 = f32[256,256]{1,0:T(8,128)S(1)} collective-permute-done((f32[256,256]{1,0:T(8,128)S(1)}, f32[256,256]{1,0:T(8,128)S(1)}, u32[]{:S(2)}, u32[]{:S(2)}) %collective-permute-start.6) | collective-permute-done | bytes 262176 | tf_op jit(solution)/shard_map/ppermute | solution.py:26
  30.0 1.3 flex_first_span.1
  31.9 1.6 %flex_first.1 = (f32[512,256]{1,0:T(8,128)S(1)}, f32[512,256]{1,0:T(8,128)S(1)}, f32[512,256]{1,0:T(8,128)S(1)}, f32[512,256]{1,0:T(8,128)S(1)}, f32[256,256]{1,...) custom-call(f32[8,256]{1,0:T(8,128)S(1)} %get-tuple-element.56.masks, ...), custom_call_target="tpu_custom_call" | custom-call | flops 805306368 | bytes 8388608 | tf_op jit(solution)/shard_map/flex_first/pallas_call | solution.py:326
  33.7 1.3 collective-permute-done.7.got
  35.0 11.9 %all_to_all.30.got = f32[16,8,384]{2,1,0:T(8,128)S(1)} all-to-all(f32[16,8,384]{2,1,0:T(8,128)S(1)} %add.2), channel_id=1, replica_groups=mesh['z'=8,'y'=4,'x'=4,'core'=2] {'y','x'}, dimensions={0} | all-to-all | bytes 393216 | tf_op jit(solution)/shard_map/all_to_all | solution.py:296
  46.9 1.3 collective-permute-start.8
  48.6 4.3 %collective-permute-start.10 = (f32[512,256]{1,0:T(8,128)S(1)}, f32[512,256]{1,0:T(8,128)S(1)}, u32[]{:S(2)}, u32[]{:S(2)}) collective-permute-start(f32[512,256]{1,0:T(8,128)S(1)} %get-tuple-element.72.f3), channel_id=1, source_target_pairs={{0,248},{8,0},{16,8},{24,16},{32,24},{40,32},{48,40},{56,48},{64,5... | collective-permute-start | bytes 1572872 | tf_op jit(solution)/shard_map/ppermute | solution.py:26
  52.9 14.2 %all_to_all.31.got = f32[8,8,384]{2,1,0:T(8,128)S(1)} all-to-all(f32[8,8,384]{2,1,0:T(8,128)S(1)} %spread.2), channel_id=1, replica_groups=mesh['z'=8,'y'=4,'x'=4,'core'=2] {'z'}, dimensions={0} | all-to-all | bytes 196608 | tf_op jit(solution)/shard_map/all_to_all | solution.py:301
  67.6 2.7 %collective-permute-done.11.g3 = f32[512,256]{1,0:T(8,128)S(1)} collective-permute-done((f32[512,256]{1,0:T(8,128)S(1)}, f32[512,256]{1,0:T(8,128)S(1)}, u32[]{:S(2)}, u32[]{:S(2)}) %collective-permute-start.11) | collective-permute-done | bytes 524320 | tf_op jit(solution)/shard_map/ppermute | solution.py:26
  70.3 12.4 %all_to_all.32 = f32[16,8,384]{2,1,0:T(8,128)S(1)} all-to-all(f32[16,8,384]{2,1,0:T(8,128)S(1)} %get-tuple-element.74), channel_id=1, replica_groups=mesh['z'=8,'y'=4,'x'=4,'core'=2] {'y','x'}, dimensions={0} | all-to-all | bytes 393216 | tf_op jit(solution)/shard_map/all_to_all | solution.py:305
  82.6 1.9 %collective-permute-start.12 = (f32[128,384]{1,0:T(8,128)S(1)}, f32[128,384]{1,0:T(8,128)S(1)}, u32[]{:S(2)}, u32[]{:S(2)}) collective-permute-start(f32[128,384]{1,0:T(8,128)S(1)} %bitcast.35), channel_id=1, source_target_pairs={{0,1},{1,0},{2,3},{3,2},{4,5},{5,4},{6,7},{7,6},{8,9},{9,8},{10,11... | collective-permute-start | bytes 589832 | tf_op jit(solution)/shard_map/ppermute | solution.py:30
  85.7 1.8 %precond_span.1 = (f32[256,256]{1,0:T(8,128)S(1)}, f32[256,256]{1,0:T(8,128)S(1)}, bf16[256,1024]{1,0:T(8,128)(2,1)S(1)}, bf16[256,1024]{1,0:T(8,128)(2,1)S(1)},...) custom-call(f32[8,256]{1,0:T(8,128)S(1)} %get-tuple-element.56.masks, ...), custom_call_target="tpu_custom_call" | custom-call | flops 805306368 | bytes 8388608 | tf_op jit(solution)/shard_map/precond_span/pallas_call | solution.py:354
  87.6 4.8 %collective-permute-start.15 = (f32[256,256]{1,0:T(8,128)S(1)}, f32[256,256]{1,0:T(8,128)S(1)}, u32[]{:S(2)}, u32[]{:S(2)}) collective-permute-start(f32[256,256]{1,0:T(8,128)S(1)} %get-tuple-element.80.f3), channel_id=1, source_target_pairs={{0,248},{8,0},{16,8},{24,16},{32,24},{40,32},{48,40},{56,48},{64,5... | collective-permute-start | bytes 786440 | tf_op jit(solution)/shard_map/ppermute | solution.py:26
  94.5 3.9 %collective-permute-done.16.g3 = f32[256,256]{1,0:T(8,128)S(1)} collective-permute-done((f32[256,256]{1,0:T(8,128)S(1)}, f32[256,256]{1,0:T(8,128)S(1)}, u32[]{:S(2)}, u32[]{:S(2)}) %collective-permute-start.16) | collective-permute-done | bytes 262176 | tf_op jit(solution)/shard_map/ppermute | solution.py:26
  98.4 1.3 flex_second_span.1
  100.6 1.5 %flex_second.1 = (f32[256,256]{1,0:T(8,128)S(1)}, f32[256,256]{1,0:T(8,128)S(1)}, f32[256,256]{1,0:T(8,128)S(1)}, f32[256,256]{1,0:T(8,128)S(1)}, f32[256,256]{1...) custom-call(f32[8,256]{1,0:T(8,128)S(1)} %get-tuple-element.56.masks, ...), custom_call_target="tpu_custom_call" | custom-call | flops 805306368 | bytes 8388608 | tf_op jit(solution)/shard_map/flex_second/pallas_call | solution.py:326
  104.1 11.8 %all_to_all.33.got = f32[16,8,384]{2,1,0:T(8,128)S(1)} all-to-all(f32[16,8,384]{2,1,0:T(8,128)S(1)} %add.3), channel_id=1, replica_groups=mesh['z'=8,'y'=4,'x'=4,'core'=2] {'y','x'}, dimensions={0} | all-to-all | bytes 393216 | tf_op jit(solution)/shard_map/all_to_all | solution.py:296
  115.8 1.3 collective-permute-start.18
  117.1 2.6 %collective-permute-start.19 = (f32[256,256]{1,0:T(8,128)S(1)}, f32[256,256]{1,0:T(8,128)S(1)}, u32[]{:S(2)}, u32[]{:S(2)}) collective-permute-start(f32[256,256]{1,0:T(8,128)S(1)} %get-tuple-element.93), channel_id=1, source_target_pairs={{0,248},{8,0},{16,8},{24,16},{32,24},{40,32},{48,40},{56,48},{64,5... | collective-permute-start | bytes 786440 | tf_op jit(solution)/shard_map/ppermute | solution.py:26
  119.8 12.5 %all_to_all.34.got = f32[8,8,384]{2,1,0:T(8,128)S(1)} all-to-all(f32[8,8,384]{2,1,0:T(8,128)S(1)} %spread.3), channel_id=1, replica_groups=mesh['z'=8,'y'=4,'x'=4,'core'=2] {'z'}, dimensions={0} | all-to-all | bytes 196608 | tf_op jit(solution)/shard_map/all_to_all | solution.py:301
  132.7 9.8 %all_to_all.35 = f32[16,8,384]{2,1,0:T(8,128)S(1)} all-to-all(f32[16,8,384]{2,1,0:T(8,128)S(1)} %coarse_second.1), channel_id=1, replica_groups=mesh['z'=8,'y'=4,'x'=4,'core'=2] {'y','x'}, dimensions={0} | all-to-all | bytes 393216 | tf_op jit(solution)/shard_map/all_to_all | solution.py:305
  142.5 3.1 %collective-permute-start.20 = (f32[128,384]{1,0:T(8,128)S(1)}, f32[128,384]{1,0:T(8,128)S(1)}, u32[]{:S(2)}, u32[]{:S(2)}) collective-permute-start(f32[128,384]{1,0:T(8,128)S(1)} %bitcast.33), channel_id=1, source_target_pairs={{0,1},{1,0},{2,3},{3,2},{4,5},{5,4},{6,7},{7,6},{8,9},{9,8},{10,11... | collective-permute-start | bytes 589832 | tf_op jit(solution)/shard_map/ppermute | solution.py:30
  146.7 1.3 final.1
  (52 shorter events, 13.3 us)
Async XLA Ops:
  0.6 16.7 %collective-permute-start.1 = (f32[256,256]{1,0:T(8,128)}, f32[256,256]{1,0:T(8,128)S(1)}, u32[]{:S(2)}, u32[]{:S(2)}) collective-permute-start(f32[256,256]{1,0:T(8,128)} %bitcast.25), channel_id=1, source_target_pairs={{0,1},{1,2},{2,3},{3,4},{4,5},{5,6},{6,7},{7,0},{8,9},{9,10},{10,1... | collective-permute-start | bytes 786440 | tf_op jit(solution)/shard_map/ppermute | solution.py:26
  3.2 14.1 %collective-permute-start.2 = (f32[256,256]{1,0:T(8,128)}, f32[256,256]{1,0:T(8,128)S(1)}, u32[]{:S(2)}, u32[]{:S(2)}) collective-permute-start(f32[256,256]{1,0:T(8,128)} %bitcast.29), channel_id=1, source_target_pairs={{0,8},{8,16},{16,24},{24,32},{32,40},{40,48},{48,56},{56,64},{64,7... | collective-permute-start | bytes 786440 | tf_op jit(solution)/shard_map/ppermute | solution.py:26
  4.5 12.8 %collective-permute-start = (s32[4]{0:T(128)}, s32[4]{0:T(128)S(1)}, u32[]{:S(2)}, u32[]{:S(2)}) collective-permute-start(s32[4]{0:T(128)} %bitcast.37), channel_id=1, source_target_pairs={{0,8},{8,16},{16,24},{24,32},{32,40},{40,48},{48,56},{56,64},{64,7... | collective-permute-start | bytes 56 | tf_op jit(solution)/shard_map/ppermute | solution.py:26
  5.8 2.2 %copy-start = (f32[1,1,1024,1024]{3,2,1,0:T(8,128)S(1)}, f32[1,1,1024,1024]{3,2,1,0:T(8,128)}, u32[]{:S(2)}) copy-start(f32[1,1,1024,1024]{3,2,1,0:T(8,128)} %param.8) | copy-start | bytes 12582916
  8.0 0.9 copy-start.4
  9.0 0.9 copy-start.6
  9.9 0.7 copy-start.9
  10.6 6.7 %copy-start.1 = (f32[1,1,1024,1024]{3,2,1,0:T(8,128)S(1)}, f32[1,1,1024,1024]{3,2,1,0:T(8,128)}, u32[]{:S(2)}) copy-start(f32[1,1,1024,1024]{3,2,1,0:T(8,128)} %param.8) | copy-start | bytes 12582916
  18.5 11.5 %copy-start.2 = (f32[1,1,1024,1024]{3,2,1,0:T(8,128)S(1)}, f32[1,1,1024,1024]{3,2,1,0:T(8,128)}, u32[]{:S(2)}) copy-start(f32[1,1,1024,1024]{3,2,1,0:T(8,128)} %param.7) | copy-start | bytes 12582916
  18.5 11.5 %copy-start.3 = (f32[1,1,256,1024]{3,2,1,0:T(8,128)S(1)}, f32[1,1,256,1024]{3,2,1,0:T(8,128)}, u32[]{:S(2)}) copy-start(f32[1,1,256,1024]{3,2,1,0:T(8,128)} %param.9) | copy-start | bytes 3145732
  18.5 11.5 %collective-permute-start.6 = (f32[256,256]{1,0:T(8,128)S(1)}, f32[256,256]{1,0:T(8,128)S(1)}, u32[]{:S(2)}, u32[]{:S(2)}) collective-permute-start(f32[256,256]{1,0:T(8,128)S(1)} %get-tuple-element.59.f2), channel_id=1, source_target_pairs={{0,8},{8,16},{16,24},{24,32},{32,40},{40,48},{48,56},{56,64},{64,7... | collective-permute-start | bytes 786440 | tf_op jit(solution)/shard_map/ppermute | solution.py:26
  18.6 11.4 %collective-permute-start.5 = (f32[256,256]{1,0:T(8,128)S(1)}, f32[256,256]{1,0:T(8,128)S(1)}, u32[]{:S(2)}, u32[]{:S(2)}) collective-permute-start(f32[256,256]{1,0:T(8,128)S(1)} %get-tuple-element.60.f3), channel_id=1, source_target_pairs={{0,248},{8,0},{16,8},{24,16},{32,24},{40,32},{48,40},{56,48},{64,5... | collective-permute-start | bytes 786440 | tf_op jit(solution)/shard_map/ppermute | solution.py:26
  24.5 7.4 %copy-start.5 = (f32[1,1,256,256]{3,2,1,0:T(8,128)S(1)}, f32[1,1,256,256]{3,2,1,0:T(8,128)}, u32[]{:S(2)}) copy-start(f32[1,1,256,256]{3,2,1,0:T(8,128)} %param.11) | copy-start | bytes 786436
  24.5 7.4 %copy-start.7 = (f32[1,1,256,256]{3,2,1,0:T(8,128)S(1)}, f32[1,1,256,256]{3,2,1,0:T(8,128)}, u32[]{:S(2)}) copy-start(f32[1,1,256,256]{3,2,1,0:T(8,128)} %param.12) | copy-start | bytes 786436
  24.5 6.7 %collective-permute-start.4 = (f32[256,256]{1,0:T(8,128)S(1)}, f32[256,256]{1,0:T(8,128)S(1)}, u32[]{:S(2)}, u32[]{:S(2)}) collective-permute-start(f32[256,256]{1,0:T(8,128)S(1)} %get-tuple-element.57.f0), channel_id=1, source_target_pairs={{0,1},{1,2},{2,3},{3,4},{4,5},{5,6},{6,7},{7,0},{8,9},{9,10},{10,1... | collective-permute-start | bytes 786440 | tf_op jit(solution)/shard_map/ppermute | solution.py:26
  26.1 5.8 %collective-permute-start.3 = (f32[256,256]{1,0:T(8,128)S(1)}, f32[256,256]{1,0:T(8,128)S(1)}, u32[]{:S(2)}, u32[]{:S(2)}) collective-permute-start(f32[256,256]{1,0:T(8,128)S(1)} %get-tuple-element.58.f1), channel_id=1, source_target_pairs={{0,7},{1,0},{2,1},{3,2},{4,3},{5,4},{6,5},{7,6},{8,15},{9,8},{10,9... | collective-permute-start | bytes 786440 | tf_op jit(solution)/shard_map/ppermute | solution.py:26
  31.9 35.3 %copy-start.8 = (f32[256,256]{1,0:T(8,128)S(1)}, f32[256,256]{1,0:T(8,128)}, u32[]{:S(2)}) copy-start(f32[256,256]{1,0:T(8,128)} %coarse.3) | copy-start | bytes 786436
  33.4 1.5 %collective-permute-start.7 = (f32[128,384]{1,0:T(8,128)S(1)}, f32[128,384]{1,0:T(8,128)S(1)}, u32[]{:S(2)}, u32[]{:S(2)}) collective-permute-start(f32[128,384]{1,0:T(8,128)S(1)} %get-tuple-element.64), channel_id=1, source_target_pairs={{0,1},{1,0},{2,3},{3,2},{4,5},{5,4},{6,7},{7,6},{8,9},{9,8},{10,11... | collective-permute-start | bytes 589832 | tf_op jit(solution)/shard_map/ppermute | solution.py:30
  46.9 20.7 %collective-permute-start.8 = (f32[512,256]{1,0:T(8,128)S(1)}, f32[512,256]{1,0:T(8,128)S(1)}, u32[]{:S(2)}, u32[]{:S(2)}) collective-permute-start(f32[512,256]{1,0:T(8,128)S(1)} %get-tuple-element.70.f1), channel_id=1, source_target_pairs={{0,7},{1,0},{2,1},{3,2},{4,3},{5,4},{6,5},{7,6},{8,15},{9,8},{10,9... | collective-permute-start | bytes 1572872 | tf_op jit(solution)/shard_map/ppermute | solution.py:26
  48.2 19.4 %collective-permute-start.9 = (f32[512,256]{1,0:T(8,128)S(1)}, f32[512,256]{1,0:T(8,128)S(1)}, u32[]{:S(2)}, u32[]{:S(2)}) collective-permute-start(f32[512,256]{1,0:T(8,128)S(1)} %get-tuple-element.71.f0), channel_id=1, source_target_pairs={{0,1},{1,2},{2,3},{3,4},{4,5},{5,6},{6,7},{7,0},{8,9},{9,10},{10,1... | collective-permute-start | bytes 1572872 | tf_op jit(solution)/shard_map/ppermute | solution.py:26
  48.6 19.0 %collective-permute-start.10 = (f32[512,256]{1,0:T(8,128)S(1)}, f32[512,256]{1,0:T(8,128)S(1)}, u32[]{:S(2)}, u32[]{:S(2)}) collective-permute-start(f32[512,256]{1,0:T(8,128)S(1)} %get-tuple-element.72.f3), channel_id=1, source_target_pairs={{0,248},{8,0},{16,8},{24,16},{32,24},{40,32},{48,40},{56,48},{64,5... | collective-permute-start | bytes 1572872 | tf_op jit(solution)/shard_map/ppermute | solution.py:26
  52.9 17.4 %collective-permute-start.11 = (f32[512,256]{1,0:T(8,128)S(1)}, f32[512,256]{1,0:T(8,128)S(1)}, u32[]{:S(2)}, u32[]{:S(2)}) collective-permute-start(f32[512,256]{1,0:T(8,128)S(1)} %get-tuple-element.73.f2), channel_id=1, source_target_pairs={{0,8},{8,16},{16,24},{24,32},{32,40},{40,48},{48,56},{56,64},{64,7... | collective-permute-start | bytes 1572872 | tf_op jit(solution)/shard_map/ppermute | solution.py:26
  82.6 3.0 %collective-permute-start.12 = (f32[128,384]{1,0:T(8,128)S(1)}, f32[128,384]{1,0:T(8,128)S(1)}, u32[]{:S(2)}, u32[]{:S(2)}) collective-permute-start(f32[128,384]{1,0:T(8,128)S(1)} %bitcast.35), channel_id=1, source_target_pairs={{0,1},{1,0},{2,3},{3,2},{4,5},{5,4},{6,7},{7,6},{8,9},{9,8},{10,11... | collective-permute-start | bytes 589832 | tf_op jit(solution)/shard_map/ppermute | solution.py:30
  87.5 10.9 %collective-permute-start.16 = (f32[256,256]{1,0:T(8,128)S(1)}, f32[256,256]{1,0:T(8,128)S(1)}, u32[]{:S(2)}, u32[]{:S(2)}) collective-permute-start(f32[256,256]{1,0:T(8,128)S(1)} %get-tuple-element.79.f2), channel_id=1, source_target_pairs={{0,8},{8,16},{16,24},{24,32},{32,40},{40,48},{48,56},{56,64},{64,7... | collective-permute-start | bytes 786440 | tf_op jit(solution)/shard_map/ppermute | solution.py:26
  87.6 10.8 %collective-permute-start.15 = (f32[256,256]{1,0:T(8,128)S(1)}, f32[256,256]{1,0:T(8,128)S(1)}, u32[]{:S(2)}, u32[]{:S(2)}) collective-permute-start(f32[256,256]{1,0:T(8,128)S(1)} %get-tuple-element.80.f3), channel_id=1, source_target_pairs={{0,248},{8,0},{16,8},{24,16},{32,24},{40,32},{48,40},{56,48},{64,5... | collective-permute-start | bytes 786440 | tf_op jit(solution)/shard_map/ppermute | solution.py:26
  93.4 6.3 %collective-permute-start.14 = (f32[256,256]{1,0:T(8,128)S(1)}, f32[256,256]{1,0:T(8,128)S(1)}, u32[]{:S(2)}, u32[]{:S(2)}) collective-permute-start(f32[256,256]{1,0:T(8,128)S(1)} %get-tuple-element.77.f0), channel_id=1, source_target_pairs={{0,1},{1,2},{2,3},{3,4},{4,5},{5,6},{6,7},{7,0},{8,9},{9,10},{10,1... | collective-permute-start | bytes 786440 | tf_op jit(solution)/shard_map/ppermute | solution.py:26
  94.5 6.1 %collective-permute-start.13 = (f32[256,256]{1,0:T(8,128)S(1)}, f32[256,256]{1,0:T(8,128)S(1)}, u32[]{:S(2)}, u32[]{:S(2)}) collective-permute-start(f32[256,256]{1,0:T(8,128)S(1)} %get-tuple-element.78.f1), channel_id=1, source_target_pairs={{0,7},{1,0},{2,1},{3,2},{4,3},{5,4},{6,5},{7,6},{8,15},{9,8},{10,9... | collective-permute-start | bytes 786440 | tf_op jit(solution)/shard_map/ppermute | solution.py:26
  102.1 1.9 %collective-permute-start.17 = (f32[128,384]{1,0:T(8,128)S(1)}, f32[128,384]{1,0:T(8,128)S(1)}, u32[]{:S(2)}, u32[]{:S(2)}) collective-permute-start(f32[128,384]{1,0:T(8,128)S(1)} %get-tuple-element.88), channel_id=1, source_target_pairs={{0,1},{1,0},{2,3},{3,2},{4,5},{5,4},{6,7},{7,6},{8,9},{9,8},{10,11... | collective-permute-start | bytes 589832 | tf_op jit(solution)/shard_map/ppermute | solution.py:30
  115.8 16.8 %collective-permute-start.18 = (f32[256,256]{1,0:T(8,128)S(1)}, f32[256,256]{1,0:T(8,128)S(1)}, u32[]{:S(2)}, u32[]{:S(2)}) collective-permute-start(f32[256,256]{1,0:T(8,128)S(1)} %get-tuple-element.92), channel_id=1, source_target_pairs={{0,7},{1,0},{2,1},{3,2},{4,3},{5,4},{6,5},{7,6},{8,15},{9,8},{10,9... | collective-permute-start | bytes 786440 | tf_op jit(solution)/shard_map/ppermute | solution.py:26
  117.1 15.6 %collective-permute-start.19 = (f32[256,256]{1,0:T(8,128)S(1)}, f32[256,256]{1,0:T(8,128)S(1)}, u32[]{:S(2)}, u32[]{:S(2)}) collective-permute-start(f32[256,256]{1,0:T(8,128)S(1)} %get-tuple-element.93), channel_id=1, source_target_pairs={{0,248},{8,0},{16,8},{24,16},{32,24},{40,32},{48,40},{56,48},{64,5... | collective-permute-start | bytes 786440 | tf_op jit(solution)/shard_map/ppermute | solution.py:26
  142.5 4.2 %collective-permute-start.20 = (f32[128,384]{1,0:T(8,128)S(1)}, f32[128,384]{1,0:T(8,128)S(1)}, u32[]{:S(2)}, u32[]{:S(2)}) collective-permute-start(f32[128,384]{1,0:T(8,128)S(1)} %bitcast.33), channel_id=1, source_target_pairs={{0,1},{1,0},{2,3},{3,2},{4,5},{5,4},{6,7},{7,6},{8,9},{9,8},{10,11... | collective-permute-start | bytes 589832 | tf_op jit(solution)/shard_map/ppermute | solution.py:30

commit v3 on v2

--- a/solution.py
+++ b/solution.py
@@ -101,10 +101,13 @@
     )
 
 
-def own_kernel(active, deck, joint, matrix, part):
-    span, across = position()
-    first = parts((across < DECKS - 1).astype(F32) * deck[...])
-    third = parts(live_row(active, span < SPANS - 1) * joint[...])
+def lives_kernel(active, out):
+    out[...] = jnp.broadcast_to(live_row(active, position()[0] < SPANS - 1), (8, FACE))
+
+
+def own_kernel(lives, deck, joint, matrix, part):
+    first = parts((position()[1] < DECKS - 1).astype(F32) * deck[...])
+    third = parts(lives[0:1, :] * joint[...])
     for i in range(4):
         part[:, i * FACE : (i + 1) * FACE] = faces_times(first, third, matrix, 0, i)
 
@@ -332,9 +335,10 @@
     deck_behind = cyclic(deck, DECK, 1)
     active_behind = cyclic(active, SPAN, 1)
     gaps = (deck, joint, deck_behind, joint_behind)
+    (lives,) = call(lives_kernel, [(8, FACE)], 1, "lives", smem=(0,), estimate=cost(4 * CASES))(active)
     (part,) = call(
-        own_kernel, [wide], 4, "own", smem=(0,), estimate=cost(CASES // 2), grant=10
-    )(active, deck, joint, precond)
+        own_kernel, [wide], 4, "own", estimate=cost(CASES // 2), grant=10
+    )(lives, deck, joint, precond)
     behind = (active, active_behind, deck_behind, joint_behind, part, precond)
     v2, v3, masks = call(
         functools.partial(behind_kernel, (2, 3)), pair + [(8, FACE)], 6, "behind_span",
@@ -346,11 +350,10 @@
     )(*behind)
     *w, z_deck, z_joint, sent, held = flexed(1, (v0, v1, v2, v3), "flex_first", stacked, deck, joint)
     rows = scatter_rows(sent, held)
-    got = exchange(after(w, rows))
     loads, scalars = call(first_coarse_kernel, [copies, (PIECE, 128)], 2, "coarse_first")(
         along_z(rows), coarse_inverse
     )
-    loads = after(loads, got)
+    got = exchange(after(w, loads))
     v2, v3, *u, image_deck, image_joint, res_deck, res_joint, corner_deck, corner_joint, steps = call(
         precond_kernel, pair + narrow + [face] * 6 + [(CASES, 128)], 16, "precond_span",
         scratch=(whole,), estimate=cost(CASES // 2), grant=10,

time: 148 us -> 150 us (1.014)
  blocking collectives: 72.5 us -> 78.2 us
  local copies, waits for them, and re-layouts: 4.77 us -> 0.8 us
    all_to_all x2, blocking collectives: 22.1 us -> 28.2 us  [gather_rows(): mine = lax.all_to_all(copies, ('y', 'x'), 0, 0).reshape(HALF, WIDE)]
    unnamed x20 -> x16, local copies, waits for them, and re-layouts: 4.77 us -> 0.8 us
    ppermute x4, starting transfers between devices: 6.11 us -> 4.37 us  [swapped(): return lax.ppermute(block, 'core', [(0, 1), (1, 0)])]
where the time goes in v3:
time: 150 us; the launch traced here: 149 us
  blocking collectives  78.2 us (52%)
  starting transfers between devices  32.2 us (21%)
  waiting for transfers between devices  22.6 us (15%)
  Pallas kernels  14.7 us (10%)
    all_to_all x2, blocking collectives, gather_rows(): mine = lax.all_to_all(copies, ('y', 'x'), 0, 0).reshape(HALF, WIDE)  28.2 us
    ppermute x17, starting transfers between devices, cyclic(): return lax.ppermute(block, axes, [(i, (i + k) % n) for i in range(n)])  27.8 us
    all_to_all x2, blocking collectives, along_z(): return lax.all_to_all(copies, 'z', 0, 0)  26.3 us
    all_to_all x2, blocking collectives, scatter_rows(): return lax.all_to_all(block, ('y', 'x'), 0, 0)  23.7 us
    ppermute x17, waiting for transfers between devices, cyclic(): return lax.ppermute(block, axes, [(i, (i + k) % n) for i in range(n)])  18.1 us
    ppermute x4, waiting for transfers between devices, swapped(): return lax.ppermute(block, 'core', [(0, 1), (1, 0)])  4.53 us
    ppermute x4, starting transfers between devices, swapped(): return lax.ppermute(block, 'core', [(0, 1), (1, 0)])  4.37 us
    pallas_call x2, Pallas kernels, flexed(): call(functools.partial(flex_kernel, n_faces), shapes + [face, face, half,...  3.11 us
  transfers between devices with their start and end apart: 21, of which 10 were waited for; matrix products, arithmetic and copies ran while one was open for 0% of the time, Pallas kernels for 5%

profile of v3, /device:TPU:1, one launch (start us, length us, event | category | flops | bytes accessed | tf_op | source)
XLA Modules:
  0.0 149.3 jit_solution(1959960591781558028)
XLA Ops:
  0.6 2.2 %collective-permute-start = (s32[4]{0:T(128)}, s32[4]{0:T(128)S(1)}, u32[]{:S(2)}, u32[]{:S(2)}) collective-permute-start(s32[4]{0:T(128)} %bitcast.37), channel_id=1, source_target_pairs={{0,8},{8,16},{16,24},{24,32},{32,40},{40,48},{48,56},{56,64},{64,7... | collective-permute-start | bytes 56 | tf_op jit(solution)/shard_map/ppermute | solution.py:26
  2.8 2.1 %collective-permute-start.1 = (f32[256,256]{1,0:T(8,128)}, f32[256,256]{1,0:T(8,128)S(1)}, u32[]{:S(2)}, u32[]{:S(2)}) collective-permute-start(f32[256,256]{1,0:T(8,128)} %bitcast.25), channel_id=1, source_target_pairs={{0,1},{1,2},{2,3},{3,4},{4,5},{5,6},{6,7},{7,0},{8,9},{9,10},{10,1... | collective-permute-start | bytes 786440 | tf_op jit(solution)/shard_map/ppermute | solution.py:26
  4.9 1.3 collective-permute-start.2
  8.6 2.0 %collective-permute-done.active_behind = s32[4]{0:T(128)S(1)} collective-permute-done((s32[4]{0:T(128)}, s32[4]{0:T(128)S(1)}, u32[]{:S(2)}, u32[]{:S(2)}) %collective-permute-start) | collective-permute-done | bytes 48 | tf_op jit(solution)/shard_map/ppermute | solution.py:26
  10.6 6.7 %collective-permute-done.2.joint_behind = f32[256,256]{1,0:T(8,128)S(1)} collective-permute-done((f32[256,256]{1,0:T(8,128)}, f32[256,256]{1,0:T(8,128)S(1)}, u32[]{:S(2)}, u32[]{:S(2)}) %collective-permute-start.2) | collective-permute-done | bytes 262176 | tf_op jit(solution)/shard_map/ppermute | solution.py:26
  17.3 1.1 behind_span.1
  18.6 4.8 %collective-permute-start.5 = (f32[256,256]{1,0:T(8,128)S(1)}, f32[256,256]{1,0:T(8,128)S(1)}, u32[]{:S(2)}, u32[]{:S(2)}) collective-permute-start(f32[256,256]{1,0:T(8,128)S(1)} %get-tuple-element.59.f3), channel_id=1, source_target_pairs={{0,248},{8,0},{16,8},{24,16},{32,24},{40,32},{48,40},{56,48},{64,5... | collective-permute-start | bytes 786440 | tf_op jit(solution)/shard_map/ppermute | solution.py:26
  23.4 1.1 behind_deck.1
  24.5 1.5 %collective-permute-start.4 = (f32[256,256]{1,0:T(8,128)S(1)}, f32[256,256]{1,0:T(8,128)S(1)}, u32[]{:S(2)}, u32[]{:S(2)}) collective-permute-start(f32[256,256]{1,0:T(8,128)S(1)} %get-tuple-element.56.f0), channel_id=1, source_target_pairs={{0,1},{1,2},{2,3},{3,4},{4,5},{5,6},{6,7},{7,0},{8,9},{9,10},{10,1... | collective-permute-start | bytes 786440 | tf_op jit(solution)/shard_map/ppermute | solution.py:26
  26.1 3.8 %collective-permute-done.6.g3 = f32[256,256]{1,0:T(8,128)S(1)} collective-permute-done((f32[256,256]{1,0:T(8,128)S(1)}, f32[256,256]{1,0:T(8,128)S(1)}, u32[]{:S(2)}, u32[]{:S(2)}) %collective-permute-start.6) | collective-permute-done | bytes 262176 | tf_op jit(solution)/shard_map/ppermute | solution.py:26
  29.9 1.3 flex_first_span.1
  31.9 1.6 %flex_first.1 = (f32[512,256]{1,0:T(8,128)S(1)}, f32[512,256]{1,0:T(8,128)S(1)}, f32[512,256]{1,0:T(8,128)S(1)}, f32[512,256]{1,0:T(8,128)S(1)}, f32[256,256]{1,...) custom-call(f32[8,256]{1,0:T(8,128)S(1)} %get-tuple-element.55.masks, ...), custom_call_target="tpu_custom_call" | custom-call | flops 805306368 | bytes 8388608 | tf_op jit(solution)/shard_map/flex_first/pallas_call | solution.py:329
  33.7 1.3 collective-permute-done.7.got
  35.0 11.9 %all_to_all.30.got = f32[16,8,384]{2,1,0:T(8,128)S(1)} all-to-all(f32[16,8,384]{2,1,0:T(8,128)S(1)} %add.2), channel_id=1, replica_groups=mesh['z'=8,'y'=4,'x'=4,'core'=2] {'y','x'}, dimensions={0} | all-to-all | bytes 393216 | tf_op jit(solution)/shard_map/all_to_all | solution.py:299
  47.0 15.6 %all_to_all.31.got = f32[8,8,384]{2,1,0:T(8,128)S(1)} all-to-all(f32[8,8,384]{2,1,0:T(8,128)S(1)} %spread.2), channel_id=1, replica_groups=mesh['z'=8,'y'=4,'x'=4,'core'=2] {'z'}, dimensions={0} | all-to-all | bytes 196608 | tf_op jit(solution)/shard_map/all_to_all | solution.py:304
  62.9 3.1 %collective-permute-start.9 = (f32[512,256]{1,0:T(8,128)S(1)}, f32[512,256]{1,0:T(8,128)S(1)}, u32[]{:S(2)}, u32[]{:S(2)}) collective-permute-start(f32[512,256]{1,0:T(8,128)S(1)} %get-tuple-element.69.f1), channel_id=1, source_target_pairs={{0,7},{1,0},{2,1},{3,2},{4,3},{5,4},{6,5},{7,6},{8,15},{9,8},{10,9... | collective-permute-start | bytes 1572872 | tf_op jit(solution)/shard_map/ppermute | solution.py:26
  67.7 18.4 %all_to_all.32 = f32[16,8,384]{2,1,0:T(8,128)S(1)} all-to-all(f32[16,8,384]{2,1,0:T(8,128)S(1)} %get-tuple-element.64), channel_id=1, replica_groups=mesh['z'=8,'y'=4,'x'=4,'core'=2] {'y','x'}, dimensions={0} | all-to-all | bytes 393216 | tf_op jit(solution)/shard_map/all_to_all | solution.py:308
  87.7 1.8 %precond_span.1 = (f32[256,256]{1,0:T(8,128)S(1)}, f32[256,256]{1,0:T(8,128)S(1)}, bf16[256,1024]{1,0:T(8,128)(2,1)S(1)}, bf16[256,1024]{1,0:T(8,128)(2,1)S(1)},...) custom-call(f32[8,256]{1,0:T(8,128)S(1)} %get-tuple-element.55.masks, ...), custom_call_target="tpu_custom_call" | custom-call | flops 805306368 | bytes 8388608 | tf_op jit(solution)/shard_map/precond_span/pallas_call | solution.py:357
  89.6 4.8 %collective-permute-start.15 = (f32[256,256]{1,0:T(8,128)S(1)}, f32[256,256]{1,0:T(8,128)S(1)}, u32[]{:S(2)}, u32[]{:S(2)}) collective-permute-start(f32[256,256]{1,0:T(8,128)S(1)} %get-tuple-element.78.f3), channel_id=1, source_target_pairs={{0,248},{8,0},{16,8},{24,16},{32,24},{40,32},{48,40},{56,48},{64,5... | collective-permute-start | bytes 786440 | tf_op jit(solution)/shard_map/ppermute | solution.py:26
  95.4 1.3 collective-permute-start.14
  96.7 3.7 %collective-permute-done.16.g3 = f32[256,256]{1,0:T(8,128)S(1)} collective-permute-done((f32[256,256]{1,0:T(8,128)S(1)}, f32[256,256]{1,0:T(8,128)S(1)}, u32[]{:S(2)}, u32[]{:S(2)}) %collective-permute-start.16) | collective-permute-done | bytes 262176 | tf_op jit(solution)/shard_map/ppermute | solution.py:26
  100.4 1.3 flex_second_span.1
  101.7 1.1 collective-permute-done.13.g0
  102.8 1.5 %flex_second.1 = (f32[256,256]{1,0:T(8,128)S(1)}, f32[256,256]{1,0:T(8,128)S(1)}, f32[256,256]{1,0:T(8,128)S(1)}, f32[256,256]{1,0:T(8,128)S(1)}, f32[256,256]{1...) custom-call(f32[8,256]{1,0:T(8,128)S(1)} %get-tuple-element.55.masks, ...), custom_call_target="tpu_custom_call" | custom-call | flops 805306368 | bytes 8388608 | tf_op jit(solution)/shard_map/flex_second/pallas_call | solution.py:329
  105.0 1.1 collective-permute-done.17.got
  106.1 11.8 %all_to_all.33.got = f32[16,8,384]{2,1,0:T(8,128)S(1)} all-to-all(f32[16,8,384]{2,1,0:T(8,128)S(1)} %add.3), channel_id=1, replica_groups=mesh['z'=8,'y'=4,'x'=4,'core'=2] {'y','x'}, dimensions={0} | all-to-all | bytes 393216 | tf_op jit(solution)/shard_map/all_to_all | solution.py:299
  117.9 1.3 collective-permute-start.18
  119.1 3.6 %collective-permute-start.19 = (f32[256,256]{1,0:T(8,128)S(1)}, f32[256,256]{1,0:T(8,128)S(1)}, u32[]{:S(2)}, u32[]{:S(2)}) collective-permute-start(f32[256,256]{1,0:T(8,128)S(1)} %get-tuple-element.91), channel_id=1, source_target_pairs={{0,248},{8,0},{16,8},{24,16},{32,24},{40,32},{48,40},{56,48},{64,5... | collective-permute-start | bytes 786440 | tf_op jit(solution)/shard_map/ppermute | solution.py:26
  122.8 10.8 %all_to_all.34.got = f32[8,8,384]{2,1,0:T(8,128)S(1)} all-to-all(f32[8,8,384]{2,1,0:T(8,128)S(1)} %spread.3), channel_id=1, replica_groups=mesh['z'=8,'y'=4,'x'=4,'core'=2] {'z'}, dimensions={0} | all-to-all | bytes 196608 | tf_op jit(solution)/shard_map/all_to_all | solution.py:304
  134.0 9.8 %all_to_all.35 = f32[16,8,384]{2,1,0:T(8,128)S(1)} all-to-all(f32[16,8,384]{2,1,0:T(8,128)S(1)} %coarse_second.1), channel_id=1, replica_groups=mesh['z'=8,'y'=4,'x'=4,'core'=2] {'y','x'}, dimensions={0} | all-to-all | bytes 393216 | tf_op jit(solution)/shard_map/all_to_all | solution.py:308
  143.8 3.1 %collective-permute-start.20 = (f32[128,384]{1,0:T(8,128)S(1)}, f32[128,384]{1,0:T(8,128)S(1)}, u32[]{:S(2)}, u32[]{:S(2)}) collective-permute-start(f32[128,384]{1,0:T(8,128)S(1)} %bitcast.33), channel_id=1, source_target_pairs={{0,1},{1,0},{2,3},{3,2},{4,5},{5,4},{6,7},{7,6},{8,9},{9,8},{10,11... | collective-permute-start | bytes 589832 | tf_op jit(solution)/shard_map/ppermute | solution.py:30
  148.0 1.3 final.1
  (49 shorter events, 10.3 us)
Async XLA Ops:
  0.6 10.0 %collective-permute-start = (s32[4]{0:T(128)}, s32[4]{0:T(128)S(1)}, u32[]{:S(2)}, u32[]{:S(2)}) collective-permute-start(s32[4]{0:T(128)} %bitcast.37), channel_id=1, source_target_pairs={{0,8},{8,16},{16,24},{24,32},{32,40},{40,48},{48,56},{56,64},{64,7... | collective-permute-start | bytes 56 | tf_op jit(solution)/shard_map/ppermute | solution.py:26
  2.8 7.8 %collective-permute-start.1 = (f32[256,256]{1,0:T(8,128)}, f32[256,256]{1,0:T(8,128)S(1)}, u32[]{:S(2)}, u32[]{:S(2)}) collective-permute-start(f32[256,256]{1,0:T(8,128)} %bitcast.25), channel_id=1, source_target_pairs={{0,1},{1,2},{2,3},{3,4},{4,5},{5,6},{6,7},{7,0},{8,9},{9,10},{10,1... | collective-permute-start | bytes 786440 | tf_op jit(solution)/shard_map/ppermute | solution.py:26
  4.9 2.6 %copy-start = (f32[1,1,1024,1024]{3,2,1,0:T(8,128)S(1)}, f32[1,1,1024,1024]{3,2,1,0:T(8,128)}, u32[]{:S(2)}) copy-start(f32[1,1,1024,1024]{3,2,1,0:T(8,128)} %param.8) | copy-start | bytes 12582916
  4.9 2.6 %copy-start.3 = (f32[1,1,256,256]{3,2,1,0:T(8,128)S(1)}, f32[1,1,256,256]{3,2,1,0:T(8,128)}, u32[]{:S(2)}) copy-start(f32[1,1,256,256]{3,2,1,0:T(8,128)} %param.11) | copy-start | bytes 786436
  4.9 2.7 %copy-start.4 = (f32[1,1,256,256]{3,2,1,0:T(8,128)S(1)}, f32[1,1,256,256]{3,2,1,0:T(8,128)}, u32[]{:S(2)}) copy-start(f32[1,1,256,256]{3,2,1,0:T(8,128)} %param.12) | copy-start | bytes 786436
  4.9 12.5 %collective-permute-start.2 = (f32[256,256]{1,0:T(8,128)}, f32[256,256]{1,0:T(8,128)S(1)}, u32[]{:S(2)}, u32[]{:S(2)}) collective-permute-start(f32[256,256]{1,0:T(8,128)} %bitcast.29), channel_id=1, source_target_pairs={{0,8},{8,16},{16,24},{24,32},{32,40},{40,48},{48,56},{56,64},{64,7... | collective-permute-start | bytes 786440 | tf_op jit(solution)/shard_map/ppermute | solution.py:26
  6.2 0.8 copy-start.6
  8.6 14.8 %copy-start.7 = (s32[1,1,4]{2,1,0:T(1,128)S(1)}, s32[1,1,4]{2,1,0:T(1,128)}, u32[]{:S(2)}) copy-start(s32[1,1,4]{2,1,0:T(1,128)} %param.13) | copy-start | bytes 52
  18.5 11.4 %copy-start.1 = (f32[1,1,1024,1024]{3,2,1,0:T(8,128)S(1)}, f32[1,1,1024,1024]{3,2,1,0:T(8,128)}, u32[]{:S(2)}) copy-start(f32[1,1,1024,1024]{3,2,1,0:T(8,128)} %param.7) | copy-start | bytes 12582916
  18.5 11.4 %copy-start.2 = (f32[1,1,256,1024]{3,2,1,0:T(8,128)S(1)}, f32[1,1,256,1024]{3,2,1,0:T(8,128)}, u32[]{:S(2)}) copy-start(f32[1,1,256,1024]{3,2,1,0:T(8,128)} %param.9) | copy-start | bytes 3145732
  18.5 11.4 %collective-permute-start.6 = (f32[256,256]{1,0:T(8,128)S(1)}, f32[256,256]{1,0:T(8,128)S(1)}, u32[]{:S(2)}, u32[]{:S(2)}) collective-permute-start(f32[256,256]{1,0:T(8,128)S(1)} %get-tuple-element.58.f2), channel_id=1, source_target_pairs={{0,8},{8,16},{16,24},{24,32},{32,40},{40,48},{48,56},{56,64},{64,7... | collective-permute-start | bytes 786440 | tf_op jit(solution)/shard_map/ppermute | solution.py:26
  18.6 11.3 %collective-permute-start.5 = (f32[256,256]{1,0:T(8,128)S(1)}, f32[256,256]{1,0:T(8,128)S(1)}, u32[]{:S(2)}, u32[]{:S(2)}) collective-permute-start(f32[256,256]{1,0:T(8,128)S(1)} %get-tuple-element.59.f3), channel_id=1, source_target_pairs={{0,248},{8,0},{16,8},{24,16},{32,24},{40,32},{48,40},{56,48},{64,5... | collective-permute-start | bytes 786440 | tf_op jit(solution)/shard_map/ppermute | solution.py:26
  24.5 6.7 %collective-permute-start.4 = (f32[256,256]{1,0:T(8,128)S(1)}, f32[256,256]{1,0:T(8,128)S(1)}, u32[]{:S(2)}, u32[]{:S(2)}) collective-permute-start(f32[256,256]{1,0:T(8,128)S(1)} %get-tuple-element.56.f0), channel_id=1, source_target_pairs={{0,1},{1,2},{2,3},{3,4},{4,5},{5,6},{6,7},{7,0},{8,9},{9,10},{10,1... | collective-permute-start | bytes 786440 | tf_op jit(solution)/shard_map/ppermute | solution.py:26
  26.1 5.8 %collective-permute-start.3 = (f32[256,256]{1,0:T(8,128)S(1)}, f32[256,256]{1,0:T(8,128)S(1)}, u32[]{:S(2)}, u32[]{:S(2)}) collective-permute-start(f32[256,256]{1,0:T(8,128)S(1)} %get-tuple-element.57.f1), channel_id=1, source_target_pairs={{0,7},{1,0},{2,1},{3,2},{4,3},{5,4},{6,5},{7,6},{8,15},{9,8},{10,9... | collective-permute-start | bytes 786440 | tf_op jit(solution)/shard_map/ppermute | solution.py:26
  31.9 30.6 %copy-start.5 = (f32[256,256]{1,0:T(8,128)S(1)}, f32[256,256]{1,0:T(8,128)}, u32[]{:S(2)}) copy-start(f32[256,256]{1,0:T(8,128)} %coarse.3) | copy-start | bytes 786436
  33.5 1.5 %collective-permute-start.7 = (f32[128,384]{1,0:T(8,128)S(1)}, f32[128,384]{1,0:T(8,128)S(1)}, u32[]{:S(2)}, u32[]{:S(2)}) collective-permute-start(f32[128,384]{1,0:T(8,128)S(1)} %get-tuple-element.63), channel_id=1, source_target_pairs={{0,1},{1,0},{2,3},{3,2},{4,5},{5,4},{6,7},{7,6},{8,9},{9,8},{10,11... | collective-permute-start | bytes 589832 | tf_op jit(solution)/shard_map/ppermute | solution.py:30
  62.9 24.7 %collective-permute-start.9 = (f32[512,256]{1,0:T(8,128)S(1)}, f32[512,256]{1,0:T(8,128)S(1)}, u32[]{:S(2)}, u32[]{:S(2)}) collective-permute-start(f32[512,256]{1,0:T(8,128)S(1)} %get-tuple-element.69.f1), channel_id=1, source_target_pairs={{0,7},{1,0},{2,1},{3,2},{4,3},{5,4},{6,5},{7,6},{8,15},{9,8},{10,9... | collective-permute-start | bytes 1572872 | tf_op jit(solution)/shard_map/ppermute | solution.py:26
  66.1 21.6 %collective-permute-start.10 = (f32[512,256]{1,0:T(8,128)S(1)}, f32[512,256]{1,0:T(8,128)S(1)}, u32[]{:S(2)}, u32[]{:S(2)}) collective-permute-start(f32[512,256]{1,0:T(8,128)S(1)} %get-tuple-element.70.f0), channel_id=1, source_target_pairs={{0,1},{1,2},{2,3},{3,4},{4,5},{5,6},{6,7},{7,0},{8,9},{9,10},{10,1... | collective-permute-start | bytes 1572872 | tf_op jit(solution)/shard_map/ppermute | solution.py:26
  66.2 21.4 %collective-permute-start.11 = (f32[512,256]{1,0:T(8,128)S(1)}, f32[512,256]{1,0:T(8,128)S(1)}, u32[]{:S(2)}, u32[]{:S(2)}) collective-permute-start(f32[512,256]{1,0:T(8,128)S(1)} %get-tuple-element.71.f3), channel_id=1, source_target_pairs={{0,248},{8,0},{16,8},{24,16},{32,24},{40,32},{48,40},{56,48},{64,5... | collective-permute-start | bytes 1572872 | tf_op jit(solution)/shard_map/ppermute | solution.py:26
  66.8 20.9 %collective-permute-start.12 = (f32[512,256]{1,0:T(8,128)S(1)}, f32[512,256]{1,0:T(8,128)S(1)}, u32[]{:S(2)}, u32[]{:S(2)}) collective-permute-start(f32[512,256]{1,0:T(8,128)S(1)} %get-tuple-element.72.f2), channel_id=1, source_target_pairs={{0,8},{8,16},{16,24},{24,32},{32,40},{40,48},{48,56},{56,64},{64,7... | collective-permute-start | bytes 1572872 | tf_op jit(solution)/shard_map/ppermute | solution.py:26
  86.2 1.5 %collective-permute-start.8 = (f32[128,384]{1,0:T(8,128)S(1)}, f32[128,384]{1,0:T(8,128)S(1)}, u32[]{:S(2)}, u32[]{:S(2)}) collective-permute-start(f32[128,384]{1,0:T(8,128)S(1)} %bitcast.35), channel_id=1, source_target_pairs={{0,1},{1,0},{2,3},{3,2},{4,5},{5,4},{6,7},{7,6},{8,9},{9,8},{10,11... | collective-permute-start | bytes 589832 | tf_op jit(solution)/shard_map/ppermute | solution.py:30
  89.5 10.9 %collective-permute-start.16 = (f32[256,256]{1,0:T(8,128)S(1)}, f32[256,256]{1,0:T(8,128)S(1)}, u32[]{:S(2)}, u32[]{:S(2)}) collective-permute-start(f32[256,256]{1,0:T(8,128)S(1)} %get-tuple-element.77.f2), channel_id=1, source_target_pairs={{0,8},{8,16},{16,24},{24,32},{32,40},{40,48},{48,56},{56,64},{64,7... | collective-permute-start | bytes 786440 | tf_op jit(solution)/shard_map/ppermute | solution.py:26
  89.6 10.8 %collective-permute-start.15 = (f32[256,256]{1,0:T(8,128)S(1)}, f32[256,256]{1,0:T(8,128)S(1)}, u32[]{:S(2)}, u32[]{:S(2)}) collective-permute-start(f32[256,256]{1,0:T(8,128)S(1)} %get-tuple-element.78.f3), channel_id=1, source_target_pairs={{0,248},{8,0},{16,8},{24,16},{32,24},{40,32},{48,40},{56,48},{64,5... | collective-permute-start | bytes 786440 | tf_op jit(solution)/shard_map/ppermute | solution.py:26
  95.4 6.3 %collective-permute-start.14 = (f32[256,256]{1,0:T(8,128)S(1)}, f32[256,256]{1,0:T(8,128)S(1)}, u32[]{:S(2)}, u32[]{:S(2)}) collective-permute-start(f32[256,256]{1,0:T(8,128)S(1)} %get-tuple-element.75.f0), channel_id=1, source_target_pairs={{0,1},{1,2},{2,3},{3,4},{4,5},{5,6},{6,7},{7,0},{8,9},{9,10},{10,1... | collective-permute-start | bytes 786440 | tf_op jit(solution)/shard_map/ppermute | solution.py:26
  96.7 6.1 %collective-permute-start.13 = (f32[256,256]{1,0:T(8,128)S(1)}, f32[256,256]{1,0:T(8,128)S(1)}, u32[]{:S(2)}, u32[]{:S(2)}) collective-permute-start(f32[256,256]{1,0:T(8,128)S(1)} %get-tuple-element.76.f1), channel_id=1, source_target_pairs={{0,7},{1,0},{2,1},{3,2},{4,3},{5,4},{6,5},{7,6},{8,15},{9,8},{10,9... | collective-permute-start | bytes 786440 | tf_op jit(solution)/shard_map/ppermute | solution.py:26
  104.4 1.7 %collective-permute-start.17 = (f32[128,384]{1,0:T(8,128)S(1)}, f32[128,384]{1,0:T(8,128)S(1)}, u32[]{:S(2)}, u32[]{:S(2)}) collective-permute-start(f32[128,384]{1,0:T(8,128)S(1)} %get-tuple-element.86), channel_id=1, source_target_pairs={{0,1},{1,0},{2,3},{3,2},{4,5},{5,4},{6,7},{7,6},{8,9},{9,8},{10,11... | collective-permute-start | bytes 589832 | tf_op jit(solution)/shard_map/ppermute | solution.py:30
  117.9 16.1 %collective-permute-start.18 = (f32[256,256]{1,0:T(8,128)S(1)}, f32[256,256]{1,0:T(8,128)S(1)}, u32[]{:S(2)}, u32[]{:S(2)}) collective-permute-start(f32[256,256]{1,0:T(8,128)S(1)} %get-tuple-element.90), channel_id=1, source_target_pairs={{0,7},{1,0},{2,1},{3,2},{4,3},{5,4},{6,5},{7,6},{8,15},{9,8},{10,9... | collective-permute-start | bytes 786440 | tf_op jit(solution)/shard_map/ppermute | solution.py:26
  119.1 14.9 %collective-permute-start.19 = (f32[256,256]{1,0:T(8,128)S(1)}, f32[256,256]{1,0:T(8,128)S(1)}, u32[]{:S(2)}, u32[]{:S(2)}) collective-permute-start(f32[256,256]{1,0:T(8,128)S(1)} %get-tuple-element.91), channel_id=1, source_target_pairs={{0,248},{8,0},{16,8},{24,16},{32,24},{40,32},{48,40},{56,48},{64,5... | collective-permute-start | bytes 786440 | tf_op jit(solution)/shard_map/ppermute | solution.py:26
  143.8 4.2 %collective-permute-start.20 = (f32[128,384]{1,0:T(8,128)S(1)}, f32[128,384]{1,0:T(8,128)S(1)}, u32[]{:S(2)}, u32[]{:S(2)}) collective-permute-start(f32[128,384]{1,0:T(8,128)S(1)} %bitcast.33), channel_id=1, source_target_pairs={{0,1},{1,0},{2,3},{3,2},{4,5},{5,4},{6,7},{7,6},{8,9},{9,8},{10,11... | collective-permute-start | bytes 589832 | tf_op jit(solution)/shard_map/ppermute | solution.py:30

commit v4 on v3

--- a/solution.py
+++ b/solution.py
@@ -26,6 +26,14 @@
     return lax.ppermute(block, axes, [(i, (i + k) % n) for i in range(n)])
 
 
+def near(block):
+    return lax.ppermute(block, SPAN, [(i, i ^ 1) for i in range(SPANS)])
+
+
+def far(block):
+    return lax.ppermute(block, SPAN, [(i, (i + (1 if i % 2 else -1)) % SPANS) for i in range(SPANS)])
+
+
 def swapped(block):
     return lax.ppermute(block, "core", [(0, 1), (1, 0)])
 
@@ -101,6 +109,11 @@
     )
 
 
+def by_span(near_value, far_value):
+    odd = lax.rem(position()[0], 2) == 1
+    return jnp.where(odd, far_value, near_value), jnp.where(odd, near_value, far_value)
+
+
 def lives_kernel(active, out):
     out[...] = jnp.broadcast_to(live_row(active, position()[0] < SPANS - 1), (8, FACE))
 
@@ -112,7 +125,7 @@
         part[:, i * FACE : (i + 1) * FACE] = faces_times(first, third, matrix, 0, i)
 
 
-def behind_kernel(which, active, active_behind, deck_behind, joint_behind, part, matrix, *outs):
+def behind_kernel(which, active, joint_behind, deck_behind, active_behind, part, matrix, *outs):
     span, across = position()
     ones = jnp.ones((1, FACE), F32)
     lives = (
@@ -124,45 +137,58 @@
     if len(outs) == 3:
         outs[2][...] = jnp.concatenate(lives + (jnp.zeros((4, FACE), F32),), axis=0)
     second, fourth = parts(lives[1] * deck_behind[...]), parts(lives[3] * joint_behind[...])
-    for i, out in zip(which, outs):
-        out[...] = 0.5 * (quarter(part, i) - faces_times(second, fourth, matrix, FACE, i))
-
-
-def jump(masks, own, got, i):
-    return masks[i : i + 1, :] * (own[i][: CASES, :] - got[i][: CASES, :])
-
-
-def two_quarters(masks, own, got, matrix, corners, at):
-    jumps = [jump(masks, own, got, i) for i in range(2)]
-    high, low = parts(jnp.concatenate(jumps, axis=1))
+    values = [0.5 * (quarter(part, i) - faces_times(second, fourth, matrix, FACE, i)) for i in which]
+    if which[0] == 2:
+        values = by_span(*values)
+    outs[0][...], outs[1][...] = values
+
+
+def deck_jumps(masks, own, got, rows=slice(0, CASES)):
+    return [masks[i : i + 1, :] * (own[i][rows, :] - got[i][rows, :]) for i in range(2)]
+
+
+def span_jumps(masks, own, got, rows=slice(0, CASES)):
+    ahead, behind = by_span(own[0][rows, :] - got[0][rows, :], own[1][rows, :] - got[1][rows, :])
+    return [masks[2:3, :] * ahead, masks[3:4, :] * behind]
+
+
+def two_quarters(jumps, matrix, corners, at):
+    pair = parts(jnp.concatenate(jumps, axis=1))
     rows = slice(at, at + 2 * FACE)
-    fields = [product((high, low), parts(matrix[rows, i * FACE : (i + 1) * FACE])) for i in range(4)]
-    return jumps, fields, product((high, low), parts(corners[:, rows]), TRANS)
-
-
-def flex_span_kernel(masks, f2, f3, g2, g3, matrix, corners, part, corner_part):
-    _, fields, corner = two_quarters(masks[2:4, :], (f2, f3), (g2, g3), matrix, corners, 2 * FACE)
+    fields = [product(pair, parts(matrix[rows, i * FACE : (i + 1) * FACE])) for i in range(4)]
+    return fields, product(pair, parts(corners[:, rows]), TRANS)
+
+
+def flex_span_kernel(masks, f2, f3, g2, g3, matrix, corners, part, corner_part, third, fourth):
+    third[...], fourth[...] = span_jumps(masks, (f2, f3), (g2, g3))
+    fields, corner = two_quarters([third[...], fourth[...]], matrix, corners, 2 * FACE)
     for i in range(4):
         part[:, i * FACE : (i + 1) * FACE] = fields[i]
     corner_part[...] = corner
 
 
-def flex_kernel(n_faces, masks, f0, f1, f2, f3, g0, g1, g2, g3, part, corner_part, matrix, corners, *refs):
+def flex_kernel(n_faces, masks, f0, f1, g0, g1, part, corner_part, third, fourth, matrix, corners, *refs):
     pairs, refs = refs[: 2 * n_faces], refs[2 * n_faces :]
-    outs, (first, third, sent, held, table) = refs[:4], refs[4:]
+    outs, (first, sent, held, table) = refs[:4], refs[4:]
     core = lax.axis_index("core")
-    late, fields, corner = two_quarters(masks[0:2, :], (f0, f1), (g0, g1), matrix, corners, 0)
-    jumps = late + [jump(masks[2:4, :], (f2, f3), (g2, g3), i) for i in range(2)]
-    first[...], third[...] = jumps[0], jumps[2]
+    jumps = deck_jumps(masks, (f0, f1), (g0, g1))
+    fields, corner = two_quarters(jumps, matrix, corners, 0)
+    first[...] = jumps[0]
+    jumps = jumps + [third[...], fourth[...]]
     total = jnp.zeros((CASES, 1), F32)
+    values = [quarter(part, i) + fields[i] for i in range(4)]
     for i in range(4):
-        value = quarter(part, i) + fields[i]
-        total = total + row_sum(jumps[i] * value)
-        if outs[i].shape[0] == CASES:
-            outs[i][...] = value
-        else:
-            outs[i][: CASES, :] = value
-            outs[i][CASES:, :] = quarter(corners, i)
+        total = total + row_sum(jumps[i] * values[i])
+    if n_faces == 1:
+        corner_quarters = [quarter(corners, i) for i in range(4)]
+        corner_quarters[2:] = by_span(*corner_quarters[2:])
+        values[2:] = by_span(*values[2:])
+        for i in range(4):
+            outs[i][: CASES, :] = values[i]
+            outs[i][CASES:, :] = corner_quarters[i]
+    else:
+        for i in range(4):
+            outs[i][...] = values[i]
     sums = [
         row_sum(masks[0:1, :] * pairs[2 * k][...] * first[...] + masks[2:3, :] * pairs[2 * k + 1][...] * third[...])
         for k in range(n_faces)
@@ -224,34 +250,34 @@
     load = parts(whole[:, :NC])
     step = whole[:, NC : NC + 1]
     steps[...] = whole[:, NC:]
-    own, got = (f0, f1, f2, f3), (g0, g1, g2, g3)
     gaps = (deck, deck_behind, joint, joint_behind)
+    low = slice(CASES, 2 * CASES)
+    images = deck_jumps(masks, (f0, f1), (g0, g1)) + span_jumps(masks, (f2, f3), (g2, g3))
+    corner = deck_jumps(masks, (f0, f1), (g0, g1), low) + span_jumps(masks, (f2, f3), (g2, g3), low)
     for i in range(4):
-        live = masks[i : i + 1, :]
-        corner = live * (own[i][CASES:, :] - got[i][CASES:, :])
-        image = jump(masks, own, got, i) + product(load, parts(corner))
-        gap = live * gaps[i][...]
+        image = images[i] + product(load, parts(corner[i]))
+        gap = masks[i : i + 1, :] * gaps[i][...]
         res = (gap if i % 2 == 0 else -gap) - step * image
         if i == 0:
-            corner_deck[...], image_deck[...], res_deck[...] = corner, image, res
+            corner_deck[...], image_deck[...], res_deck[...] = corner[i], image, res
         if i == 2:
-            corner_joint[...], image_joint[...], res_joint[...] = corner, image, res
+            corner_joint[...], image_joint[...], res_joint[...] = corner[i], image, res
         keep(u_high, u_low, i, res)
 
     span_quarters(u_high, u_low, matrix, v2, v3)
 
 
-def two_of(first, u_high, u_low, matrix, outs):
-    for i, out in enumerate(outs):
-        out[...] = 0.5 * product((u_high[...], u_low[...]), parts(quarter(matrix, first + i)))
+def two_of(first, u_high, u_low, matrix):
+    pair = u_high[...], u_low[...]
+    return [0.5 * product(pair, parts(quarter(matrix, first + i))) for i in range(2)]
 
 
 def span_quarters(u_high, u_low, matrix, v2, v3):
-    two_of(2, u_high, u_low, matrix, (v2, v3))
+    v2[...], v3[...] = by_span(*two_of(2, u_high, u_low, matrix))
 
 
 def deck_quarters(u_high, u_low, matrix, v0, v1):
-    two_of(0, u_high, u_low, matrix, (v0, v1))
+    v0[...], v1[...] = two_of(0, u_high, u_low, matrix)
 
 
 def final_kernel(masks, mine, other, steps, z_deck, z_joint, y_deck, y_joint,
@@ -274,10 +300,9 @@
 
 
 def exchange(field):
-    right, left, ahead, behind = field
-    ahead_got, behind_got = cyclic(ahead, SPAN, 1), cyclic(behind, SPAN, -1)
+    right, left, to_near, to_far = field
     right_got, left_got = cyclic(right, DECK, 1), cyclic(left, DECK, -1)
-    return left_got, right_got, behind_got, ahead_got
+    return left_got, right_got, near(to_near), far(to_far)
 
 
 def add_kernel(held, got, out):
@@ -323,13 +348,15 @@
 
     def flexed(n_faces, v, name, shapes, *pairs):
         got = exchange(v)
-        part, corner = call(
-            flex_span_kernel, [wide, (CASES, NC)], 7, name + "_span", estimate=cost(CASES // 2), grant=10
+        part, corner, third, fourth = call(
+            flex_span_kernel, [wide, (CASES, NC), face, face], 7, name + "_span",
+            estimate=cost(CASES // 2), grant=10,
         )(masks, *v[2:], *got[2:], flex, corners)
-        return call(
-            functools.partial(flex_kernel, n_faces), shapes + [face, face, half, half], 13 + 2 * n_faces,
+        *w, first, sent, held = call(
+            functools.partial(flex_kernel, n_faces), shapes + [face, half, half], 11 + 2 * n_faces,
             name, scratch=(whole,), estimate=cost(CASES // 2), grant=10,
-        )(masks, *v, *got, part, corner, flex, corners, *pairs)
+        )(masks, *v[:2], *got[:2], part, corner, third, fourth, flex, corners, *pairs)
+        return *w, first, third, sent, held
 
     joint_behind = cyclic(joint, SPAN, 1)
     deck_behind = cyclic(deck, DECK, 1)
@@ -339,14 +366,14 @@
     (part,) = call(
         own_kernel, [wide], 4, "own", estimate=cost(CASES // 2), grant=10
     )(lives, deck, joint, precond)
-    behind = (active, active_behind, deck_behind, joint_behind, part, precond)
+    behind = (active, joint_behind, deck_behind, active_behind, part, precond)
     v2, v3, masks = call(
         functools.partial(behind_kernel, (2, 3)), pair + [(8, FACE)], 6, "behind_span",
-        smem=(0, 1), estimate=cost(CASES // 4), grant=10,
+        smem=(0, 3), estimate=cost(CASES // 4), grant=10,
     )(*behind)
     v0, v1 = call(
         functools.partial(behind_kernel, (0, 1)), pair, 6, "behind_deck",
-        smem=(0, 1), estimate=cost(CASES // 4), grant=10,
+        smem=(0, 3), estimate=cost(CASES // 4), grant=10,
     )(*behind)
     *w, z_deck, z_joint, sent, held = flexed(1, (v0, v1, v2, v3), "flex_first", stacked, deck, joint)
     rows = scatter_rows(sent, held)

time: 150 us -> 143 us (0.953)
  starting transfers between devices: 32.2 us -> 26.3 us
  blocking collectives: 78.2 us -> 74.6 us
  waiting for transfers between devices: 22.6 us -> 25.8 us
    ppermute x0 -> x6, waiting for transfers between devices: none -> 12.7 us  [the longest x3 7.02 us: far(): lax.ppermute(block, SPAN, [(i, (i + (1 if i % 2 else -1)) % SPANS) for i...]
    ppermute x17 -> x11, starting transfers between devices: 27.8 us -> 15.1 us  [cyclic(): return lax.ppermute(block, axes, [(i, (i + k) % n) for i in range(n)])]
    ppermute x17 -> x11, waiting for transfers between devices: 18.1 us -> 8.78 us  [cyclic(): return lax.ppermute(block, axes, [(i, (i + k) % n) for i in range(n)])]
    ppermute x0 -> x6, starting transfers between devices: none -> 5.58 us  [the longest x3 5.39 us: far(): lax.ppermute(block, SPAN, [(i, (i + (1 if i % 2 else -1)) % SPANS) for i...]
    all_to_all x2, blocking collectives: 23.7 us -> 21.4 us  [scatter_rows(): return lax.all_to_all(block, ('y', 'x'), 0, 0)]
where the time goes in v4:
time: 143 us
  blocking collectives  74.6 us (52%)
  starting transfers between devices  26.3 us (18%)
  waiting for transfers between devices  25.8 us (18%)
  Pallas kernels  14.8 us (10%)
    all_to_all x2, blocking collectives, gather_rows(): mine = lax.all_to_all(copies, ('y', 'x'), 0, 0).reshape(HALF, WIDE)  28.3 us
    all_to_all x2, blocking collectives, along_z(): return lax.all_to_all(copies, 'z', 0, 0)  24.9 us
    all_to_all x2, blocking collectives, scatter_rows(): return lax.all_to_all(block, ('y', 'x'), 0, 0)  21.4 us
    ppermute x11, starting transfers between devices, cyclic(): return lax.ppermute(block, axes, [(i, (i + k) % n) for i in range(n)])  15.1 us
    ppermute x11, waiting for transfers between devices, cyclic(): return lax.ppermute(block, axes, [(i, (i + k) % n) for i in range(n)])  8.78 us
    ppermute x3, waiting for transfers between devices, far(): lax.ppermute(block, SPAN, [(i, (i + (1 if i % 2 else -1)) % SPANS) for i...  7.02 us
    ppermute x3, waiting for transfers between devices, near(): return lax.ppermute(block, SPAN, [(i, i ^ 1) for i in range(SPANS)])  5.68 us
    ppermute x4, starting transfers between devices, swapped(): return lax.ppermute(block, 'core', [(0, 1), (1, 0)])  5.62 us
  transfers between devices with their start and end apart: 21, of which 10 were waited for; matrix products, arithmetic and copies ran while one was open for 0% of the time, Pallas kernels for 5%

profile of v4, /device:TPU:1, one launch (start us, length us, event | category | flops | bytes accessed | tf_op | source)
XLA Modules:
  0.0 143.1 jit_solution(11099815784516103793)
XLA Ops:
  0.6 2.2 %collective-permute-start.2 = (s32[4]{0:T(128)}, s32[4]{0:T(128)S(1)}, u32[]{:S(2)}, u32[]{:S(2)}) collective-permute-start(s32[4]{0:T(128)} %bitcast.37), channel_id=1, source_target_pairs={{0,8},{8,16},{16,24},{24,32},{32,40},{40,48},{48,56},{56,64},{64,7... | collective-permute-start | bytes 56 | tf_op jit(solution)/shard_map/ppermute | solution.py:26
  2.8 2.1 %collective-permute-start.1 = (f32[256,256]{1,0:T(8,128)}, f32[256,256]{1,0:T(8,128)S(1)}, u32[]{:S(2)}, u32[]{:S(2)}) collective-permute-start(f32[256,256]{1,0:T(8,128)} %bitcast.29), channel_id=1, source_target_pairs={{0,1},{1,2},{2,3},{3,4},{4,5},{5,6},{6,7},{7,0},{8,9},{9,10},{10,1... | collective-permute-start | bytes 786440 | tf_op jit(solution)/shard_map/ppermute | solution.py:26
  4.9 1.3 collective-permute-start
  8.6 2.0 %collective-permute-done.2.active_behind = s32[4]{0:T(128)S(1)} collective-permute-done((s32[4]{0:T(128)}, s32[4]{0:T(128)S(1)}, u32[]{:S(2)}, u32[]{:S(2)}) %collective-permute-start.2) | collective-permute-done | bytes 48 | tf_op jit(solution)/shard_map/ppermute | solution.py:26
  10.6 6.7 %collective-permute-done.joint_behind = f32[256,256]{1,0:T(8,128)S(1)} collective-permute-done((f32[256,256]{1,0:T(8,128)}, f32[256,256]{1,0:T(8,128)S(1)}, u32[]{:S(2)}, u32[]{:S(2)}) %collective-permute-start) | collective-permute-done | bytes 262176 | tf_op jit(solution)/shard_map/ppermute | solution.py:26
  17.3 1.1 behind_span.1
  18.6 3.4 %collective-permute-start.6 = (f32[256,256]{1,0:T(8,128)S(1)}, f32[256,256]{1,0:T(8,128)S(1)}, u32[]{:S(2)}, u32[]{:S(2)}) collective-permute-start(f32[256,256]{1,0:T(8,128)S(1)} %get-tuple-element.61.f3), channel_id=1, source_target_pairs={{0,248},{8,16},{16,8},{24,32},{32,24},{40,48},{48,40},{56,64},{64,... | collective-permute-start | bytes 786440 | tf_op jit(solution)/shard_map/ppermute | solution.py:34
  22.0 1.1 behind_deck.1
  23.2 1.9 %collective-permute-start.4 = (f32[256,256]{1,0:T(8,128)S(1)}, f32[256,256]{1,0:T(8,128)S(1)}, u32[]{:S(2)}, u32[]{:S(2)}) collective-permute-start(f32[256,256]{1,0:T(8,128)S(1)} %get-tuple-element.58.f0), channel_id=1, source_target_pairs={{0,1},{1,2},{2,3},{3,4},{4,5},{5,6},{6,7},{7,0},{8,9},{9,10},{10,1... | collective-permute-start | bytes 786440 | tf_op jit(solution)/shard_map/ppermute | solution.py:26
  25.1 1.5 %collective-permute-done.5.g2 = f32[256,256]{1,0:T(8,128)S(1)} collective-permute-done((f32[256,256]{1,0:T(8,128)S(1)}, f32[256,256]{1,0:T(8,128)S(1)}, u32[]{:S(2)}, u32[]{:S(2)}) %collective-permute-start.5) | collective-permute-done | bytes 262176 | tf_op jit(solution)/shard_map/ppermute | solution.py:30
  26.6 3.4 %collective-permute-done.6.g3 = f32[256,256]{1,0:T(8,128)S(1)} collective-permute-done((f32[256,256]{1,0:T(8,128)S(1)}, f32[256,256]{1,0:T(8,128)S(1)}, u32[]{:S(2)}, u32[]{:S(2)}) %collective-permute-start.6) | collective-permute-done | bytes 262176 | tf_op jit(solution)/shard_map/ppermute | solution.py:34
  30.0 1.3 flex_first_span.1
  31.3 1.6 %flex_first.1 = (f32[512,256]{1,0:T(8,128)S(1)}, f32[512,256]{1,0:T(8,128)S(1)}, f32[512,256]{1,0:T(8,128)S(1)}, f32[512,256]{1,0:T(8,128)S(1)}, f32[256,256]{1,...) custom-call(f32[8,256]{1,0:T(8,128)S(1)} %get-tuple-element.57.masks, ...), custom_call_target="tpu_custom_call" | custom-call | flops 805306368 | bytes 8388608 | tf_op jit(solution)/shard_map/flex_first/pallas_call | solution.py:355
  34.8 11.1 %all_to_all.30.got = f32[16,8,384]{2,1,0:T(8,128)S(1)} all-to-all(f32[16,8,384]{2,1,0:T(8,128)S(1)} %add.2), channel_id=1, replica_groups=mesh['z'=8,'y'=4,'x'=4,'core'=2] {'y','x'}, dimensions={0} | all-to-all | bytes 393216 | tf_op jit(solution)/shard_map/all_to_all | solution.py:324
  46.0 14.3 %all_to_all.31.got = f32[8,8,384]{2,1,0:T(8,128)S(1)} all-to-all(f32[8,8,384]{2,1,0:T(8,128)S(1)} %spread.2), channel_id=1, replica_groups=mesh['z'=8,'y'=4,'x'=4,'core'=2] {'z'}, dimensions={0} | all-to-all | bytes 196608 | tf_op jit(solution)/shard_map/all_to_all | solution.py:329
  60.6 3.1 %collective-permute-start.9 = (f32[512,256]{1,0:T(8,128)S(1)}, f32[512,256]{1,0:T(8,128)S(1)}, u32[]{:S(2)}, u32[]{:S(2)}) collective-permute-start(f32[512,256]{1,0:T(8,128)S(1)} %get-tuple-element.73.f1), channel_id=1, source_target_pairs={{0,7},{1,0},{2,1},{3,2},{4,3},{5,4},{6,5},{7,6},{8,15},{9,8},{10,9... | collective-permute-start | bytes 1572872 | tf_op jit(solution)/shard_map/ppermute | solution.py:26
  64.8 18.5 %all_to_all.32 = f32[16,8,384]{2,1,0:T(8,128)S(1)} all-to-all(f32[16,8,384]{2,1,0:T(8,128)S(1)} %get-tuple-element.68), channel_id=1, replica_groups=mesh['z'=8,'y'=4,'x'=4,'core'=2] {'y','x'}, dimensions={0} | all-to-all | bytes 393216 | tf_op jit(solution)/shard_map/all_to_all | solution.py:333
  84.8 1.9 %precond_span.1 = (f32[256,256]{1,0:T(8,128)S(1)}, f32[256,256]{1,0:T(8,128)S(1)}, bf16[256,1024]{1,0:T(8,128)(2,1)S(1)}, bf16[256,1024]{1,0:T(8,128)(2,1)S(1)},...) custom-call(f32[8,256]{1,0:T(8,128)S(1)} %get-tuple-element.57.masks, ...), custom_call_target="tpu_custom_call" | custom-call | flops 805306368 | bytes 8388608 | tf_op jit(solution)/shard_map/precond_span/pallas_call | solution.py:384
  86.8 1.1 collective-permute-start.16
  89.0 1.2 collective-permute-start.14
  90.2 4.2 %collective-permute-done.15.g2 = f32[256,256]{1,0:T(8,128)S(1)} collective-permute-done((f32[256,256]{1,0:T(8,128)S(1)}, f32[256,256]{1,0:T(8,128)S(1)}, u32[]{:S(2)}, u32[]{:S(2)}) %collective-permute-start.15) | collective-permute-done | bytes 262176 | tf_op jit(solution)/shard_map/ppermute | solution.py:30
  94.3 3.6 %collective-permute-done.16.g3 = f32[256,256]{1,0:T(8,128)S(1)} collective-permute-done((f32[256,256]{1,0:T(8,128)S(1)}, f32[256,256]{1,0:T(8,128)S(1)}, u32[]{:S(2)}, u32[]{:S(2)}) %collective-permute-start.16) | collective-permute-done | bytes 262176 | tf_op jit(solution)/shard_map/ppermute | solution.py:34
  97.9 1.3 flex_second_span.1
  99.2 1.6 %flex_second.1 = (f32[256,256]{1,0:T(8,128)S(1)}, f32[256,256]{1,0:T(8,128)S(1)}, f32[256,256]{1,0:T(8,128)S(1)}, f32[256,256]{1,0:T(8,128)S(1)}, f32[256,256]{1...) custom-call(f32[8,256]{1,0:T(8,128)S(1)} %get-tuple-element.57.masks, ...), custom_call_target="tpu_custom_call" | custom-call | flops 805306368 | bytes 8388608 | tf_op jit(solution)/shard_map/flex_second/pallas_call | solution.py:355
  100.8 1.3 collective-permute-start.17
  103.2 10.3 %all_to_all.33.got = f32[16,8,384]{2,1,0:T(8,128)S(1)} all-to-all(f32[16,8,384]{2,1,0:T(8,128)S(1)} %add.3), channel_id=1, replica_groups=mesh['z'=8,'y'=4,'x'=4,'core'=2] {'y','x'}, dimensions={0} | all-to-all | bytes 393216 | tf_op jit(solution)/shard_map/all_to_all | solution.py:324
  113.4 1.8 %collective-permute-start.18 = (f32[256,256]{1,0:T(8,128)S(1)}, f32[256,256]{1,0:T(8,128)S(1)}, u32[]{:S(2)}, u32[]{:S(2)}) collective-permute-start(f32[256,256]{1,0:T(8,128)S(1)} %get-tuple-element.96), channel_id=1, source_target_pairs={{0,7},{1,0},{2,1},{3,2},{4,3},{5,4},{6,5},{7,6},{8,15},{9,8},{10,9... | collective-permute-start | bytes 786440 | tf_op jit(solution)/shard_map/ppermute | solution.py:26
  115.2 1.4 collective-permute-start.19
  116.7 10.7 %all_to_all.34.got = f32[8,8,384]{2,1,0:T(8,128)S(1)} all-to-all(f32[8,8,384]{2,1,0:T(8,128)S(1)} %spread.3), channel_id=1, replica_groups=mesh['z'=8,'y'=4,'x'=4,'core'=2] {'z'}, dimensions={0} | all-to-all | bytes 196608 | tf_op jit(solution)/shard_map/all_to_all | solution.py:329
  127.8 9.8 %all_to_all.35 = f32[16,8,384]{2,1,0:T(8,128)S(1)} all-to-all(f32[16,8,384]{2,1,0:T(8,128)S(1)} %coarse_second.1), channel_id=1, replica_groups=mesh['z'=8,'y'=4,'x'=4,'core'=2] {'y','x'}, dimensions={0} | all-to-all | bytes 393216 | tf_op jit(solution)/shard_map/all_to_all | solution.py:333
  137.6 3.1 %collective-permute-start.20 = (f32[128,384]{1,0:T(8,128)S(1)}, f32[128,384]{1,0:T(8,128)S(1)}, u32[]{:S(2)}, u32[]{:S(2)}) collective-permute-start(f32[128,384]{1,0:T(8,128)S(1)} %bitcast.33), channel_id=1, source_target_pairs={{0,1},{1,0},{2,3},{3,2},{4,5},{5,4},{6,7},{7,6},{8,9},{9,8},{10,11... | collective-permute-start | bytes 589832 | tf_op jit(solution)/shard_map/ppermute | solution.py:38
  141.8 1.3 final.1
  (47 shorter events, 11.1 us)
Async XLA Ops:
  0.6 10.0 %collective-permute-start.2 = (s32[4]{0:T(128)}, s32[4]{0:T(128)S(1)}, u32[]{:S(2)}, u32[]{:S(2)}) collective-permute-start(s32[4]{0:T(128)} %bitcast.37), channel_id=1, source_target_pairs={{0,8},{8,16},{16,24},{24,32},{32,40},{40,48},{48,56},{56,64},{64,7... | collective-permute-start | bytes 56 | tf_op jit(solution)/shard_map/ppermute | solution.py:26
  2.8 7.8 %collective-permute-start.1 = (f32[256,256]{1,0:T(8,128)}, f32[256,256]{1,0:T(8,128)S(1)}, u32[]{:S(2)}, u32[]{:S(2)}) collective-permute-start(f32[256,256]{1,0:T(8,128)} %bitcast.29), channel_id=1, source_target_pairs={{0,1},{1,2},{2,3},{3,4},{4,5},{5,6},{6,7},{7,0},{8,9},{9,10},{10,1... | collective-permute-start | bytes 786440 | tf_op jit(solution)/shard_map/ppermute | solution.py:26
  4.9 2.6 %copy-start = (f32[1,1,1024,1024]{3,2,1,0:T(8,128)S(1)}, f32[1,1,1024,1024]{3,2,1,0:T(8,128)}, u32[]{:S(2)}) copy-start(f32[1,1,1024,1024]{3,2,1,0:T(8,128)} %param.8) | copy-start | bytes 12582916
  4.9 2.6 %copy-start.3 = (f32[1,1,256,256]{3,2,1,0:T(8,128)S(1)}, f32[1,1,256,256]{3,2,1,0:T(8,128)}, u32[]{:S(2)}) copy-start(f32[1,1,256,256]{3,2,1,0:T(8,128)} %param.12) | copy-start | bytes 786436
  4.9 2.7 %copy-start.4 = (f32[1,1,256,256]{3,2,1,0:T(8,128)S(1)}, f32[1,1,256,256]{3,2,1,0:T(8,128)}, u32[]{:S(2)}) copy-start(f32[1,1,256,256]{3,2,1,0:T(8,128)} %param.11) | copy-start | bytes 786436
  4.9 12.5 %collective-permute-start = (f32[256,256]{1,0:T(8,128)}, f32[256,256]{1,0:T(8,128)S(1)}, u32[]{:S(2)}, u32[]{:S(2)}) collective-permute-start(f32[256,256]{1,0:T(8,128)} %bitcast.25), channel_id=1, source_target_pairs={{0,8},{8,16},{16,24},{24,32},{32,40},{40,48},{48,56},{56,64},{64,7... | collective-permute-start | bytes 786440 | tf_op jit(solution)/shard_map/ppermute | solution.py:26
  6.2 0.8 copy-start.6
  18.5 11.5 %copy-start.1 = (f32[1,1,1024,1024]{3,2,1,0:T(8,128)S(1)}, f32[1,1,1024,1024]{3,2,1,0:T(8,128)}, u32[]{:S(2)}) copy-start(f32[1,1,1024,1024]{3,2,1,0:T(8,128)} %param.7) | copy-start | bytes 12582916
  18.5 11.5 %copy-start.2 = (f32[1,1,256,1024]{3,2,1,0:T(8,128)S(1)}, f32[1,1,256,1024]{3,2,1,0:T(8,128)}, u32[]{:S(2)}) copy-start(f32[1,1,256,1024]{3,2,1,0:T(8,128)} %param.9) | copy-start | bytes 3145732
  18.5 8.1 %collective-permute-start.5 = (f32[256,256]{1,0:T(8,128)S(1)}, f32[256,256]{1,0:T(8,128)S(1)}, u32[]{:S(2)}, u32[]{:S(2)}) collective-permute-start(f32[256,256]{1,0:T(8,128)S(1)} %get-tuple-element.60.f2), channel_id=1, source_target_pairs={{0,8},{8,0},{16,24},{24,16},{32,40},{40,32},{48,56},{56,48},{64,72... | collective-permute-start | bytes 786440 | tf_op jit(solution)/shard_map/ppermute | solution.py:30
  18.6 11.4 %collective-permute-start.6 = (f32[256,256]{1,0:T(8,128)S(1)}, f32[256,256]{1,0:T(8,128)S(1)}, u32[]{:S(2)}, u32[]{:S(2)}) collective-permute-start(f32[256,256]{1,0:T(8,128)S(1)} %get-tuple-element.61.f3), channel_id=1, source_target_pairs={{0,248},{8,16},{16,8},{24,32},{32,24},{40,48},{48,40},{56,64},{64,... | collective-permute-start | bytes 786440 | tf_op jit(solution)/shard_map/ppermute | solution.py:34
  23.2 8.1 %collective-permute-start.4 = (f32[256,256]{1,0:T(8,128)S(1)}, f32[256,256]{1,0:T(8,128)S(1)}, u32[]{:S(2)}, u32[]{:S(2)}) collective-permute-start(f32[256,256]{1,0:T(8,128)S(1)} %get-tuple-element.58.f0), channel_id=1, source_target_pairs={{0,1},{1,2},{2,3},{3,4},{4,5},{5,6},{6,7},{7,0},{8,9},{9,10},{10,1... | collective-permute-start | bytes 786440 | tf_op jit(solution)/shard_map/ppermute | solution.py:26
  25.1 6.3 %collective-permute-start.3 = (f32[256,256]{1,0:T(8,128)S(1)}, f32[256,256]{1,0:T(8,128)S(1)}, u32[]{:S(2)}, u32[]{:S(2)}) collective-permute-start(f32[256,256]{1,0:T(8,128)S(1)} %get-tuple-element.59.f1), channel_id=1, source_target_pairs={{0,7},{1,0},{2,1},{3,2},{4,3},{5,4},{6,5},{7,6},{8,15},{9,8},{10,9... | collective-permute-start | bytes 786440 | tf_op jit(solution)/shard_map/ppermute | solution.py:26
  31.3 28.9 %copy-start.5 = (f32[256,256]{1,0:T(8,128)S(1)}, f32[256,256]{1,0:T(8,128)}, u32[]{:S(2)}) copy-start(f32[256,256]{1,0:T(8,128)} %coarse.3) | copy-start | bytes 786436
  32.9 1.9 %collective-permute-start.7 = (f32[128,384]{1,0:T(8,128)S(1)}, f32[128,384]{1,0:T(8,128)S(1)}, u32[]{:S(2)}, u32[]{:S(2)}) collective-permute-start(f32[128,384]{1,0:T(8,128)S(1)} %get-tuple-element.67), channel_id=1, source_target_pairs={{0,1},{1,0},{2,3},{3,2},{4,5},{5,4},{6,7},{7,6},{8,9},{9,8},{10,11... | collective-permute-start | bytes 589832 | tf_op jit(solution)/shard_map/ppermute | solution.py:38
  60.6 24.1 %collective-permute-start.9 = (f32[512,256]{1,0:T(8,128)S(1)}, f32[512,256]{1,0:T(8,128)S(1)}, u32[]{:S(2)}, u32[]{:S(2)}) collective-permute-start(f32[512,256]{1,0:T(8,128)S(1)} %get-tuple-element.73.f1), channel_id=1, source_target_pairs={{0,7},{1,0},{2,1},{3,2},{4,3},{5,4},{6,5},{7,6},{8,15},{9,8},{10,9... | collective-permute-start | bytes 1572872 | tf_op jit(solution)/shard_map/ppermute | solution.py:26
  63.8 21.0 %collective-permute-start.10 = (f32[512,256]{1,0:T(8,128)S(1)}, f32[512,256]{1,0:T(8,128)S(1)}, u32[]{:S(2)}, u32[]{:S(2)}) collective-permute-start(f32[512,256]{1,0:T(8,128)S(1)} %get-tuple-element.74.f0), channel_id=1, source_target_pairs={{0,1},{1,2},{2,3},{3,4},{4,5},{5,6},{6,7},{7,0},{8,9},{9,10},{10,1... | collective-permute-start | bytes 1572872 | tf_op jit(solution)/shard_map/ppermute | solution.py:26
  63.9 20.8 %collective-permute-start.11 = (f32[512,256]{1,0:T(8,128)S(1)}, f32[512,256]{1,0:T(8,128)S(1)}, u32[]{:S(2)}, u32[]{:S(2)}) collective-permute-start(f32[512,256]{1,0:T(8,128)S(1)} %get-tuple-element.75.f2), channel_id=1, source_target_pairs={{0,8},{8,0},{16,24},{24,16},{32,40},{40,32},{48,56},{56,48},{64,72... | collective-permute-start | bytes 1572872 | tf_op jit(solution)/shard_map/ppermute | solution.py:30
  63.9 20.8 %collective-permute-start.12 = (f32[512,256]{1,0:T(8,128)S(1)}, f32[512,256]{1,0:T(8,128)S(1)}, u32[]{:S(2)}, u32[]{:S(2)}) collective-permute-start(f32[512,256]{1,0:T(8,128)S(1)} %get-tuple-element.76.f3), channel_id=1, source_target_pairs={{0,248},{8,16},{16,8},{24,32},{32,24},{40,48},{48,40},{56,64},{64,... | collective-permute-start | bytes 1572872 | tf_op jit(solution)/shard_map/ppermute | solution.py:34
  83.3 1.5 %collective-permute-start.8 = (f32[128,384]{1,0:T(8,128)S(1)}, f32[128,384]{1,0:T(8,128)S(1)}, u32[]{:S(2)}, u32[]{:S(2)}) collective-permute-start(f32[128,384]{1,0:T(8,128)S(1)} %bitcast.35), channel_id=1, source_target_pairs={{0,1},{1,0},{2,3},{3,2},{4,5},{5,4},{6,7},{7,6},{8,9},{9,8},{10,11... | collective-permute-start | bytes 589832 | tf_op jit(solution)/shard_map/ppermute | solution.py:38
  86.7 7.6 %collective-permute-start.15 = (f32[256,256]{1,0:T(8,128)S(1)}, f32[256,256]{1,0:T(8,128)S(1)}, u32[]{:S(2)}, u32[]{:S(2)}) collective-permute-start(f32[256,256]{1,0:T(8,128)S(1)} %get-tuple-element.81.f2), channel_id=1, source_target_pairs={{0,8},{8,0},{16,24},{24,16},{32,40},{40,32},{48,56},{56,48},{64,72... | collective-permute-start | bytes 786440 | tf_op jit(solution)/shard_map/ppermute | solution.py:30
  86.8 11.1 %collective-permute-start.16 = (f32[256,256]{1,0:T(8,128)S(1)}, f32[256,256]{1,0:T(8,128)S(1)}, u32[]{:S(2)}, u32[]{:S(2)}) collective-permute-start(f32[256,256]{1,0:T(8,128)S(1)} %get-tuple-element.82.f3), channel_id=1, source_target_pairs={{0,248},{8,16},{16,8},{24,32},{32,24},{40,48},{48,40},{56,64},{64,... | collective-permute-start | bytes 786440 | tf_op jit(solution)/shard_map/ppermute | solution.py:34
  89.0 10.2 %collective-permute-start.14 = (f32[256,256]{1,0:T(8,128)S(1)}, f32[256,256]{1,0:T(8,128)S(1)}, u32[]{:S(2)}, u32[]{:S(2)}) collective-permute-start(f32[256,256]{1,0:T(8,128)S(1)} %get-tuple-element.79.f0), channel_id=1, source_target_pairs={{0,1},{1,2},{2,3},{3,4},{4,5},{5,6},{6,7},{7,0},{8,9},{9,10},{10,1... | collective-permute-start | bytes 786440 | tf_op jit(solution)/shard_map/ppermute | solution.py:26
  90.2 9.1 %collective-permute-start.13 = (f32[256,256]{1,0:T(8,128)S(1)}, f32[256,256]{1,0:T(8,128)S(1)}, u32[]{:S(2)}, u32[]{:S(2)}) collective-permute-start(f32[256,256]{1,0:T(8,128)S(1)} %get-tuple-element.80.f1), channel_id=1, source_target_pairs={{0,7},{1,0},{2,1},{3,2},{4,3},{5,4},{6,5},{7,6},{8,15},{9,8},{10,9... | collective-permute-start | bytes 786440 | tf_op jit(solution)/shard_map/ppermute | solution.py:26
  100.8 2.4 %collective-permute-start.17 = (f32[128,384]{1,0:T(8,128)S(1)}, f32[128,384]{1,0:T(8,128)S(1)}, u32[]{:S(2)}, u32[]{:S(2)}) collective-permute-start(f32[128,384]{1,0:T(8,128)S(1)} %get-tuple-element.92), channel_id=1, source_target_pairs={{0,1},{1,0},{2,3},{3,2},{4,5},{5,4},{6,7},{7,6},{8,9},{9,8},{10,11... | collective-permute-start | bytes 589832 | tf_op jit(solution)/shard_map/ppermute | solution.py:38
  113.4 14.3 %collective-permute-start.18 = (f32[256,256]{1,0:T(8,128)S(1)}, f32[256,256]{1,0:T(8,128)S(1)}, u32[]{:S(2)}, u32[]{:S(2)}) collective-permute-start(f32[256,256]{1,0:T(8,128)S(1)} %get-tuple-element.96), channel_id=1, source_target_pairs={{0,7},{1,0},{2,1},{3,2},{4,3},{5,4},{6,5},{7,6},{8,15},{9,8},{10,9... | collective-permute-start | bytes 786440 | tf_op jit(solution)/shard_map/ppermute | solution.py:26
  115.2 12.5 %collective-permute-start.19 = (f32[256,256]{1,0:T(8,128)S(1)}, f32[256,256]{1,0:T(8,128)S(1)}, u32[]{:S(2)}, u32[]{:S(2)}) collective-permute-start(f32[256,256]{1,0:T(8,128)S(1)} %get-tuple-element.97), channel_id=1, source_target_pairs={{0,248},{8,0},{16,8},{24,16},{32,24},{40,32},{48,40},{56,48},{64,5... | collective-permute-start | bytes 786440 | tf_op jit(solution)/shard_map/ppermute | solution.py:26
  137.6 4.2 %collective-permute-start.20 = (f32[128,384]{1,0:T(8,128)S(1)}, f32[128,384]{1,0:T(8,128)S(1)}, u32[]{:S(2)}, u32[]{:S(2)}) collective-permute-start(f32[128,384]{1,0:T(8,128)S(1)} %bitcast.33), channel_id=1, source_target_pairs={{0,1},{1,0},{2,3},{3,2},{4,5},{5,4},{6,7},{7,6},{8,9},{9,8},{10,11... | collective-permute-start | bytes 589832 | tf_op jit(solution)/shard_map/ppermute | solution.py:38

commit v5 on v4

--- a/solution.py
+++ b/solution.py
@@ -102,11 +102,24 @@
     return row * on.astype(F32)
 
 
-def faces_times(first, third, matrix, rows, i):
+def block_of(pair, rows, columns):
+    return pair[0][rows, columns], pair[1][rows, columns]
+
+
+def faces_times(first, third, matrix, row, i):
     at = slice(i * FACE, (i + 1) * FACE)
-    return product(first, parts(matrix[rows : rows + FACE, at])) + product(
-        third, parts(matrix[rows + 2 * FACE : rows + 3 * FACE, at])
-    )
+    return product(first, block_of(matrix, slice(row, row + FACE), at)) + product(
+        third, block_of(matrix, slice(row + 2 * FACE, row + 3 * FACE), at)
+    )
+
+
+def split_kernel(matrix, high, low):
+    for i in range(4):
+        keep(high, low, i, quarter(matrix, i))
+
+
+def fourth_kernel(joint_behind, lives_behind, high, low):
+    high[...], low[...] = parts(lives_behind[0:1, :] * joint_behind[...])
 
 
 def by_span(near_value, far_value):
@@ -118,26 +131,26 @@
     out[...] = jnp.broadcast_to(live_row(active, position()[0] < SPANS - 1), (8, FACE))
 
 
-def own_kernel(lives, deck, joint, matrix, part):
+def own_kernel(lives, deck, joint, high, low, part):
     first = parts((position()[1] < DECKS - 1).astype(F32) * deck[...])
     third = parts(lives[0:1, :] * joint[...])
     for i in range(4):
-        part[:, i * FACE : (i + 1) * FACE] = faces_times(first, third, matrix, 0, i)
-
-
-def behind_kernel(which, active, joint_behind, deck_behind, active_behind, part, matrix, *outs):
-    span, across = position()
+        part[:, i * FACE : (i + 1) * FACE] = faces_times(first, third, (high, low), 0, i)
+
+
+def behind_kernel(which, joint_high, joint_low, deck_behind, lives, lives_behind, part, high, low, *outs):
+    _, across = position()
     ones = jnp.ones((1, FACE), F32)
     lives = (
         ones * (across < DECKS - 1).astype(F32),
         ones * (across > 0).astype(F32),
-        live_row(active, span < SPANS - 1),
-        live_row(active_behind, span > 0),
+        lives[0:1, :],
+        lives_behind[0:1, :],
     )
     if len(outs) == 3:
         outs[2][...] = jnp.concatenate(lives + (jnp.zeros((4, FACE), F32),), axis=0)
-    second, fourth = parts(lives[1] * deck_behind[...]), parts(lives[3] * joint_behind[...])
-    values = [0.5 * (quarter(part, i) - faces_times(second, fourth, matrix, FACE, i)) for i in which]
+    second, fourth = parts(lives[1] * deck_behind[...]), (joint_high[...], joint_low[...])
+    values = [0.5 * (quarter(part, i) - faces_times(second, fourth, (high, low), FACE, i)) for i in which]
     if which[0] == 2:
         values = by_span(*values)
     outs[0][...], outs[1][...] = values
@@ -155,24 +168,24 @@
 def two_quarters(jumps, matrix, corners, at):
     pair = parts(jnp.concatenate(jumps, axis=1))
     rows = slice(at, at + 2 * FACE)
-    fields = [product(pair, parts(matrix[rows, i * FACE : (i + 1) * FACE])) for i in range(4)]
+    fields = [product(pair, block_of(matrix, rows, slice(i * FACE, (i + 1) * FACE))) for i in range(4)]
     return fields, product(pair, parts(corners[:, rows]), TRANS)
 
 
-def flex_span_kernel(masks, f2, f3, g2, g3, matrix, corners, part, corner_part, third, fourth):
+def flex_span_kernel(masks, f2, f3, g2, g3, high, low, corners, part, corner_part, third, fourth):
     third[...], fourth[...] = span_jumps(masks, (f2, f3), (g2, g3))
-    fields, corner = two_quarters([third[...], fourth[...]], matrix, corners, 2 * FACE)
+    fields, corner = two_quarters([third[...], fourth[...]], (high, low), corners, 2 * FACE)
     for i in range(4):
         part[:, i * FACE : (i + 1) * FACE] = fields[i]
     corner_part[...] = corner
 
 
-def flex_kernel(n_faces, masks, f0, f1, g0, g1, part, corner_part, third, fourth, matrix, corners, *refs):
+def flex_kernel(n_faces, masks, f0, f1, g0, g1, part, corner_part, third, fourth, high, low, corners, *refs):
     pairs, refs = refs[: 2 * n_faces], refs[2 * n_faces :]
     outs, (first, sent, held, table) = refs[:4], refs[4:]
     core = lax.axis_index("core")
     jumps = deck_jumps(masks, (f0, f1), (g0, g1))
-    fields, corner = two_quarters(jumps, matrix, corners, 0)
+    fields, corner = two_quarters(jumps, (high, low), corners, 0)
     first[...] = jumps[0]
     jumps = jumps + [third[...], fourth[...]]
     total = jnp.zeros((CASES, 1), F32)
@@ -243,7 +256,7 @@
 
 
 def precond_kernel(masks, mine, other, f0, f1, f2, f3, g0, g1, g2, g3,
-                   deck, joint, deck_behind, joint_behind, matrix,
+                   deck, joint, deck_behind, joint_behind, high, low,
                    v2, v3, u_high, u_low, image_deck, image_joint, res_deck, res_joint,
                    corner_deck, corner_joint, steps, whole):
     place_rows(mine, other, whole)
@@ -251,9 +264,9 @@
     step = whole[:, NC : NC + 1]
     steps[...] = whole[:, NC:]
     gaps = (deck, deck_behind, joint, joint_behind)
-    low = slice(CASES, 2 * CASES)
+    under = slice(CASES, 2 * CASES)
     images = deck_jumps(masks, (f0, f1), (g0, g1)) + span_jumps(masks, (f2, f3), (g2, g3))
-    corner = deck_jumps(masks, (f0, f1), (g0, g1), low) + span_jumps(masks, (f2, f3), (g2, g3), low)
+    corner = deck_jumps(masks, (f0, f1), (g0, g1), under) + span_jumps(masks, (f2, f3), (g2, g3), under)
     for i in range(4):
         image = images[i] + product(load, parts(corner[i]))
         gap = masks[i : i + 1, :] * gaps[i][...]
@@ -264,20 +277,23 @@
             corner_joint[...], image_joint[...], res_joint[...] = corner[i], image, res
         keep(u_high, u_low, i, res)
 
-    span_quarters(u_high, u_low, matrix, v2, v3)
-
-
-def two_of(first, u_high, u_low, matrix):
-    pair = u_high[...], u_low[...]
-    return [0.5 * product(pair, parts(quarter(matrix, first + i))) for i in range(2)]
-
-
-def span_quarters(u_high, u_low, matrix, v2, v3):
-    v2[...], v3[...] = by_span(*two_of(2, u_high, u_low, matrix))
-
-
-def deck_quarters(u_high, u_low, matrix, v0, v1):
-    v0[...], v1[...] = two_of(0, u_high, u_low, matrix)
+    span_quarters(u_high, u_low, high, low, v2, v3)
+
+
+def two_of(first, u_high, u_low, high, low):
+    pair, rows = (u_high[...], u_low[...]), slice(0, IFACE)
+    return [
+        0.5 * product(pair, block_of((high, low), rows, slice(i * FACE, (i + 1) * FACE)))
+        for i in (first, first + 1)
+    ]
+
+
+def span_quarters(u_high, u_low, high, low, v2, v3):
+    v2[...], v3[...] = by_span(*two_of(2, u_high, u_low, high, low))
+
+
+def deck_quarters(u_high, u_low, high, low, v0, v1):
+    v0[...], v1[...] = two_of(0, u_high, u_low, high, low)
 
 
 def final_kernel(masks, mine, other, steps, z_deck, z_joint, y_deck, y_joint,
@@ -349,45 +365,55 @@
     def flexed(n_faces, v, name, shapes, *pairs):
         got = exchange(v)
         part, corner, third, fourth = call(
-            flex_span_kernel, [wide, (CASES, NC), face, face], 7, name + "_span",
+            flex_span_kernel, [wide, (CASES, NC), face, face], 8, name + "_span",
             estimate=cost(CASES // 2), grant=10,
-        )(masks, *v[2:], *got[2:], flex, corners)
+        )(masks, *v[2:], *got[2:], *flex_pair, corners)
         *w, first, sent, held = call(
-            functools.partial(flex_kernel, n_faces), shapes + [face, half, half], 11 + 2 * n_faces,
+            functools.partial(flex_kernel, n_faces), shapes + [face, half, half], 12 + 2 * n_faces,
             name, scratch=(whole,), estimate=cost(CASES // 2), grant=10,
-        )(masks, *v[:2], *got[:2], part, corner, third, fourth, flex, corners, *pairs)
+        )(masks, *v[:2], *got[:2], part, corner, third, fourth, *flex_pair, corners, *pairs)
         return *w, first, third, sent, held
 
     joint_behind = cyclic(joint, SPAN, 1)
-    deck_behind = cyclic(deck, DECK, 1)
-    active_behind = cyclic(active, SPAN, 1)
+    (lives,) = call(lives_kernel, [(8, FACE)], 1, "lives", smem=(0,), estimate=cost(4 * CASES))(active)
+    deck_behind = cyclic(after(deck, lives), DECK, 1)
+    lives_behind = cyclic(lives, SPAN, 1)
     gaps = (deck, joint, deck_behind, joint_behind)
-    (lives,) = call(lives_kernel, [(8, FACE)], 1, "lives", smem=(0,), estimate=cost(4 * CASES))(active)
+    halves = [jax.ShapeDtypeStruct((IFACE, IFACE), BF16)] * 2
+    pre_pair, flex_pair = (
+        call(split_kernel, halves, 1, name, estimate=cost(CASES // 4), grant=4)(matrix)
+        for matrix, name in ((precond, "split_precond"), (flex, "split_flex"))
+    )
     (part,) = call(
-        own_kernel, [wide], 4, "own", estimate=cost(CASES // 2), grant=10
-    )(lives, deck, joint, precond)
-    behind = (active, joint_behind, deck_behind, active_behind, part, precond)
+        own_kernel, [wide], 5, "own", estimate=cost(CASES // 2), grant=10
+    )(lives, deck, joint, *pre_pair)
+    fourth = call(
+        fourth_kernel, [jax.ShapeDtypeStruct(face, BF16)] * 2, 2, "fourth", estimate=cost(CASES // 8)
+    )(joint_behind, lives_behind)
+    behind = (*fourth, deck_behind, lives, lives_behind, part, *pre_pair)
     v2, v3, masks = call(
-        functools.partial(behind_kernel, (2, 3)), pair + [(8, FACE)], 6, "behind_span",
-        smem=(0, 3), estimate=cost(CASES // 4), grant=10,
+        functools.partial(behind_kernel, (2, 3)), pair + [(8, FACE)], 8, "behind_span",
+        estimate=cost(CASES // 4), grant=10,
     )(*behind)
     v0, v1 = call(
-        functools.partial(behind_kernel, (0, 1)), pair, 6, "behind_deck",
-        smem=(0, 3), estimate=cost(CASES // 4), grant=10,
+        functools.partial(behind_kernel, (0, 1)), pair, 8, "behind_deck",
+        estimate=cost(CASES // 4), grant=10,
     )(*behind)
     *w, z_deck, z_joint, sent, held = flexed(1, (v0, v1, v2, v3), "flex_first", stacked, deck, joint)
     rows = scatter_rows(sent, held)
     loads, scalars = call(first_coarse_kernel, [copies, (PIECE, 128)], 2, "coarse_first")(
         along_z(rows), coarse_inverse
     )
-    got = exchange(after(w, loads))
+    *early, _ = after(w, rows)
+    got = exchange((*early, after(w[3], loads)))
+    loads = after(loads, got[:3])
     v2, v3, *u, image_deck, image_joint, res_deck, res_joint, corner_deck, corner_joint, steps = call(
-        precond_kernel, pair + narrow + [face] * 6 + [(CASES, 128)], 16, "precond_span",
+        precond_kernel, pair + narrow + [face] * 6 + [(CASES, 128)], 17, "precond_span",
         scratch=(whole,), estimate=cost(CASES // 2), grant=10,
-    )(masks, *gather_rows(loads), *w, *got, *gaps, precond)
+    )(masks, *gather_rows(loads), *w, *got, *gaps, *pre_pair)
     v0, v1 = call(
-        deck_quarters, pair, 3, "precond_deck", estimate=cost(CASES // 2), grant=10
-    )(*u, precond)
+        deck_quarters, pair, 4, "precond_deck", estimate=cost(CASES // 2), grant=10
+    )(*u, *pre_pair)
     *w, y_deck, y_joint, sent, held = flexed(
         2, (v0, v1, v2, v3), "flex_second", field, res_deck, res_joint, image_deck, image_joint
     )

time: 143 us -> 139 us (0.972)
  waiting for transfers between devices: 25.8 us -> 23 us
  starting transfers between devices: 26.3 us -> 24.1 us
    ppermute x3, starting transfers between devices: 5.39 us -> 2.96 us  [far(): lax.ppermute(block, SPAN, [(i, (i + (1 if i % 2 else -1)) % SPANS) for i...]
    ppermute x11, waiting for transfers between devices: 8.78 us -> 6.68 us  [cyclic(): return lax.ppermute(block, axes, [(i, (i + k) % n) for i in range(n)])]
    all_to_all x2, blocking collectives: 21.4 us -> 23 us  [scatter_rows(): return lax.all_to_all(block, ('y', 'x'), 0, 0)]
    all_to_all x2, blocking collectives: 24.9 us -> 23.3 us  [along_z(): return lax.all_to_all(copies, 'z', 0, 0)]
    pallas_call x7 -> x10, Pallas kernels: 8.82 us -> 8.96 us  [the longest x2 2.48 us: flexed(): call(flex_span_kernel, [wide, (CASES, NC), face, face], 8, name + '_span'...]
  transfers between devices with their start and end apart: 21 -> 21, of which waited for: 10 -> 11; matrix products, arithmetic and copies ran while one was open for 0% -> 0% of each run, Pallas kernels for 5% -> 6%
where the time goes in v5:
time: 139 us
  blocking collectives  74.7 us (54%)
  starting transfers between devices  24.1 us (17%)
  waiting for transfers between devices  23 us (17%)
  Pallas kernels  14.7 us (11%)
    all_to_all x2, blocking collectives, gather_rows(): mine = lax.all_to_all(copies, ('y', 'x'), 0, 0).reshape(HALF, WIDE)  28.3 us
    all_to_all x2, blocking collectives, along_z(): return lax.all_to_all(copies, 'z', 0, 0)  23.3 us
    all_to_all x2, blocking collectives, scatter_rows(): return lax.all_to_all(block, ('y', 'x'), 0, 0)  23 us
    ppermute x11, starting transfers between devices, cyclic(): return lax.ppermute(block, axes, [(i, (i + k) % n) for i in range(n)])  14.3 us
    ppermute x3, waiting for transfers between devices, far(): lax.ppermute(block, SPAN, [(i, (i + (1 if i % 2 else -1)) % SPANS) for i...  6.86 us
    ppermute x4, starting transfers between devices, swapped(): return lax.ppermute(block, 'core', [(0, 1), (1, 0)])  6.73 us
    ppermute x11, waiting for transfers between devices, cyclic(): return lax.ppermute(block, axes, [(i, (i + k) % n) for i in range(n)])  6.68 us
    ppermute x3, waiting for transfers between devices, near(): return lax.ppermute(block, SPAN, [(i, i ^ 1) for i in range(SPANS)])  5.16 us
  transfers between devices with their start and end apart: 21, of which 11 were waited for; matrix products, arithmetic and copies ran while one was open for 0% of the time, Pallas kernels for 6%

profile of v5, /device:TPU:1, one launch (start us, length us, event | category | flops | bytes accessed | tf_op | source)
XLA Modules:
  0.0 138.5 jit_solution(12889727939320908361)
XLA Ops:
  0.6 2.2 %collective-permute-start = (f32[256,256]{1,0:T(8,128)}, f32[256,256]{1,0:T(8,128)S(1)}, u32[]{:S(2)}, u32[]{:S(2)}) collective-permute-start(f32[256,256]{1,0:T(8,128)} %bitcast.18), channel_id=1, source_target_pairs={{0,8},{8,16},{16,24},{24,32},{32,40},{40,48},{48,56},{56,64},{64,7... | collective-permute-start | bytes 786440 | tf_op jit(solution)/shard_map/ppermute | solution.py:26
  4.4 2.1 %collective-permute-start.2 = (f32[256,256]{1,0:T(8,128)S(1)}, f32[256,256]{1,0:T(8,128)S(1)}, u32[]{:S(2)}, u32[]{:S(2)}) collective-permute-start(f32[256,256]{1,0:T(8,128)S(1)} %bitcast.22), channel_id=1, source_target_pairs={{0,1},{1,2},{2,3},{3,4},{4,5},{5,6},{6,7},{7,0},{8,9},{9,10},{10,1... | collective-permute-start | bytes 786440 | tf_op jit(solution)/shard_map/ppermute | solution.py:26
  6.5 1.3 collective-permute-start.1
  8.7 1.0 own.1.part
  9.7 6.2 %collective-permute-done.1.lives_behind = f32[8,256]{1,0:T(8,128)S(1)} collective-permute-done((f32[8,256]{1,0:T(8,128)S(1)}, f32[8,256]{1,0:T(8,128)S(1)}, u32[]{:S(2)}, u32[]{:S(2)}) %collective-permute-start.1) | collective-permute-done | bytes 8224 | tf_op jit(solution)/shard_map/ppermute | solution.py:26
  16.7 1.9 %collective-permute-start.6 = (f32[256,256]{1,0:T(8,128)S(1)}, f32[256,256]{1,0:T(8,128)S(1)}, u32[]{:S(2)}, u32[]{:S(2)}) collective-permute-start(f32[256,256]{1,0:T(8,128)S(1)} %get-tuple-element.74.f3), channel_id=1, source_target_pairs={{0,248},{8,16},{16,8},{24,32},{32,24},{40,48},{48,40},{56,64},{64,... | collective-permute-start | bytes 786440 | tf_op jit(solution)/shard_map/ppermute | solution.py:34
  19.3 3.1 %collective-permute-start.4 = (f32[256,256]{1,0:T(8,128)S(1)}, f32[256,256]{1,0:T(8,128)S(1)}, u32[]{:S(2)}, u32[]{:S(2)}) collective-permute-start(f32[256,256]{1,0:T(8,128)S(1)} %get-tuple-element.71.f0), channel_id=1, source_target_pairs={{0,1},{1,2},{2,3},{3,4},{4,5},{5,6},{6,7},{7,0},{8,9},{9,10},{10,1... | collective-permute-start | bytes 786440 | tf_op jit(solution)/shard_map/ppermute | solution.py:26
  23.3 3.4 %collective-permute-done.6.g3 = f32[256,256]{1,0:T(8,128)S(1)} collective-permute-done((f32[256,256]{1,0:T(8,128)S(1)}, f32[256,256]{1,0:T(8,128)S(1)}, u32[]{:S(2)}, u32[]{:S(2)}) %collective-permute-start.6) | collective-permute-done | bytes 262176 | tf_op jit(solution)/shard_map/ppermute | solution.py:34
  26.7 1.2 flex_first_span.1
  28.4 1.5 %flex_first.1 = (f32[512,256]{1,0:T(8,128)S(1)}, f32[512,256]{1,0:T(8,128)S(1)}, f32[512,256]{1,0:T(8,128)S(1)}, f32[512,256]{1,0:T(8,128)S(1)}, f32[256,256]{1,...) custom-call(f32[8,256]{1,0:T(8,128)S(1)} %get-tuple-element.70.masks, ...), custom_call_target="tpu_custom_call" | custom-call | flops 805306368 | bytes 8388608 | tf_op jit(solution)/shard_map/flex_first/pallas_call | solution.py:371
  29.9 1.8 %collective-permute-start.7 = (f32[128,384]{1,0:T(8,128)S(1)}, f32[128,384]{1,0:T(8,128)S(1)}, u32[]{:S(2)}, u32[]{:S(2)}) collective-permute-start(f32[128,384]{1,0:T(8,128)S(1)} %get-tuple-element.82), channel_id=1, source_target_pairs={{0,1},{1,0},{2,3},{3,2},{4,5},{5,4},{6,7},{7,6},{8,9},{9,8},{10,11... | collective-permute-start | bytes 589832 | tf_op jit(solution)/shard_map/ppermute | solution.py:38
  31.7 1.1 collective-permute-done.7.got
  32.8 11.1 %all_to_all.30.got = f32[16,8,384]{2,1,0:T(8,128)S(1)} all-to-all(f32[16,8,384]{2,1,0:T(8,128)S(1)} %add.2), channel_id=1, replica_groups=mesh['z'=8,'y'=4,'x'=4,'core'=2] {'y','x'}, dimensions={0} | all-to-all | bytes 393216 | tf_op jit(solution)/shard_map/all_to_all | solution.py:340
  43.9 1.8 %collective-permute-start.8 = (f32[512,256]{1,0:T(8,128)S(1)}, f32[512,256]{1,0:T(8,128)S(1)}, u32[]{:S(2)}, u32[]{:S(2)}) collective-permute-start(f32[512,256]{1,0:T(8,128)S(1)} %get-tuple-element.88.f1), channel_id=1, source_target_pairs={{0,7},{1,0},{2,1},{3,2},{4,3},{5,4},{6,5},{7,6},{8,15},{9,8},{10,9... | collective-permute-start | bytes 1572872 | tf_op jit(solution)/shard_map/ppermute | solution.py:26
  45.9 12.0 %all_to_all.31.got = f32[8,8,384]{2,1,0:T(8,128)S(1)} all-to-all(f32[8,8,384]{2,1,0:T(8,128)S(1)} %spread.2), channel_id=1, replica_groups=mesh['z'=8,'y'=4,'x'=4,'core'=2] {'z'}, dimensions={0} | all-to-all | bytes 196608 | tf_op jit(solution)/shard_map/all_to_all | solution.py:345
  59.1 18.5 %all_to_all.32 = f32[16,8,384]{2,1,0:T(8,128)S(1)} all-to-all(f32[16,8,384]{2,1,0:T(8,128)S(1)} %get-tuple-element.91), channel_id=1, replica_groups=mesh['z'=8,'y'=4,'x'=4,'core'=2] {'y','x'}, dimensions={0} | all-to-all | bytes 393216 | tf_op jit(solution)/shard_map/all_to_all | solution.py:349
  78.1 1.1 collective-permute-done.11.other
  79.2 1.8 %precond_span.1 = (f32[256,256]{1,0:T(8,128)S(1)}, f32[256,256]{1,0:T(8,128)S(1)}, bf16[256,1024]{1,0:T(8,128)(2,1)S(1)}, bf16[256,1024]{1,0:T(8,128)(2,1)S(1)},...) custom-call(f32[8,256]{1,0:T(8,128)S(1)} %get-tuple-element.70.masks, ...), custom_call_target="tpu_custom_call" | custom-call | flops 805306368 | bytes 8388608 | tf_op jit(solution)/shard_map/precond_span/pallas_call | solution.py:410
  82.6 1.2 collective-permute-start.14
  83.8 4.8 %collective-permute-done.15.g2 = f32[256,256]{1,0:T(8,128)S(1)} collective-permute-done((f32[256,256]{1,0:T(8,128)S(1)}, f32[256,256]{1,0:T(8,128)S(1)}, u32[]{:S(2)}, u32[]{:S(2)}) %collective-permute-start.15) | collective-permute-done | bytes 262176 | tf_op jit(solution)/shard_map/ppermute | solution.py:30
  88.6 3.4 %collective-permute-done.16.g3 = f32[256,256]{1,0:T(8,128)S(1)} collective-permute-done((f32[256,256]{1,0:T(8,128)S(1)}, f32[256,256]{1,0:T(8,128)S(1)}, u32[]{:S(2)}, u32[]{:S(2)}) %collective-permute-start.16) | collective-permute-done | bytes 262176 | tf_op jit(solution)/shard_map/ppermute | solution.py:34
  92.0 1.2 flex_second_span.1
  93.3 1.5 %flex_second.1 = (f32[256,256]{1,0:T(8,128)S(1)}, f32[256,256]{1,0:T(8,128)S(1)}, f32[256,256]{1,0:T(8,128)S(1)}, f32[256,256]{1,0:T(8,128)S(1)}, f32[256,256]{1...) custom-call(f32[8,256]{1,0:T(8,128)S(1)} %get-tuple-element.70.masks, ...), custom_call_target="tpu_custom_call" | custom-call | flops 805306368 | bytes 8388608 | tf_op jit(solution)/shard_map/flex_second/pallas_call | solution.py:371
  94.7 1.3 collective-permute-start.17
  96.0 1.1 collective-permute-done.17.got
  97.1 11.9 %all_to_all.33.got = f32[16,8,384]{2,1,0:T(8,128)S(1)} all-to-all(f32[16,8,384]{2,1,0:T(8,128)S(1)} %add.3), channel_id=1, replica_groups=mesh['z'=8,'y'=4,'x'=4,'core'=2] {'y','x'}, dimensions={0} | all-to-all | bytes 393216 | tf_op jit(solution)/shard_map/all_to_all | solution.py:340
  109.0 1.8 %collective-permute-start.18 = (f32[256,256]{1,0:T(8,128)S(1)}, f32[256,256]{1,0:T(8,128)S(1)}, u32[]{:S(2)}, u32[]{:S(2)}) collective-permute-start(f32[256,256]{1,0:T(8,128)S(1)} %get-tuple-element.112), channel_id=1, source_target_pairs={{0,7},{1,0},{2,1},{3,2},{4,3},{5,4},{6,5},{7,6},{8,15},{9,8},{10,9... | collective-permute-start | bytes 786440 | tf_op jit(solution)/shard_map/ppermute | solution.py:26
  111.4 11.3 %all_to_all.34.got = f32[8,8,384]{2,1,0:T(8,128)S(1)} all-to-all(f32[8,8,384]{2,1,0:T(8,128)S(1)} %spread.3), channel_id=1, replica_groups=mesh['z'=8,'y'=4,'x'=4,'core'=2] {'z'}, dimensions={0} | all-to-all | bytes 196608 | tf_op jit(solution)/shard_map/all_to_all | solution.py:345
  123.2 9.8 %all_to_all.35 = f32[16,8,384]{2,1,0:T(8,128)S(1)} all-to-all(f32[16,8,384]{2,1,0:T(8,128)S(1)} %coarse_second.1), channel_id=1, replica_groups=mesh['z'=8,'y'=4,'x'=4,'core'=2] {'y','x'}, dimensions={0} | all-to-all | bytes 393216 | tf_op jit(solution)/shard_map/all_to_all | solution.py:349
  133.0 3.1 %collective-permute-start.20 = (f32[128,384]{1,0:T(8,128)S(1)}, f32[128,384]{1,0:T(8,128)S(1)}, u32[]{:S(2)}, u32[]{:S(2)}) collective-permute-start(f32[128,384]{1,0:T(8,128)S(1)} %bitcast.26), channel_id=1, source_target_pairs={{0,1},{1,0},{2,3},{3,2},{4,5},{5,4},{6,7},{7,6},{8,9},{9,8},{10,11... | collective-permute-start | bytes 589832 | tf_op jit(solution)/shard_map/ppermute | solution.py:38
  136.1 1.1 collective-permute-done.20.other
  137.2 1.3 final.1
  (50 shorter events, 9.8 us)
Async XLA Ops:
  0.6 15.4 %collective-permute-start = (f32[256,256]{1,0:T(8,128)}, f32[256,256]{1,0:T(8,128)S(1)}, u32[]{:S(2)}, u32[]{:S(2)}) collective-permute-start(f32[256,256]{1,0:T(8,128)} %bitcast.18), channel_id=1, source_target_pairs={{0,8},{8,16},{16,24},{24,32},{32,40},{40,48},{48,56},{56,64},{64,7... | collective-permute-start | bytes 786440 | tf_op jit(solution)/shard_map/ppermute | solution.py:26
  2.8 0.7 copy-start.6
  3.5 0.9 copy-start.4
  3.5 4.3 %copy-start.1 = (f32[1,1,1024,1024]{3,2,1,0:T(8,128)S(1)}, f32[1,1,1024,1024]{3,2,1,0:T(8,128)}, u32[]{:S(2)}) copy-start(f32[1,1,1024,1024]{3,2,1,0:T(8,128)} %param.8) | copy-start | bytes 12582916
  4.4 11.6 %collective-permute-start.2 = (f32[256,256]{1,0:T(8,128)S(1)}, f32[256,256]{1,0:T(8,128)S(1)}, u32[]{:S(2)}, u32[]{:S(2)}) collective-permute-start(f32[256,256]{1,0:T(8,128)S(1)} %bitcast.22), channel_id=1, source_target_pairs={{0,1},{1,2},{2,3},{3,4},{4,5},{5,6},{6,7},{7,0},{8,9},{9,10},{10,1... | collective-permute-start | bytes 786440 | tf_op jit(solution)/shard_map/ppermute | solution.py:26
  6.5 9.5 %collective-permute-start.1 = (f32[8,256]{1,0:T(8,128)S(1)}, f32[8,256]{1,0:T(8,128)S(1)}, u32[]{:S(2)}, u32[]{:S(2)}) collective-permute-start(f32[8,256]{1,0:T(8,128)S(1)} %lives.1), channel_id=1, source_target_pairs={{0,8},{8,16},{16,24},{24,32},{32,40},{40,48},{48,56},{56,64},{64,7... | collective-permute-start | bytes 24584 | tf_op jit(solution)/shard_map/ppermute | solution.py:26
  7.8 1.0 copy-start.3
  16.6 6.7 %collective-permute-start.5 = (f32[256,256]{1,0:T(8,128)S(1)}, f32[256,256]{1,0:T(8,128)S(1)}, u32[]{:S(2)}, u32[]{:S(2)}) collective-permute-start(f32[256,256]{1,0:T(8,128)S(1)} %get-tuple-element.73.f2), channel_id=1, source_target_pairs={{0,8},{8,0},{16,24},{24,16},{32,40},{40,32},{48,56},{56,48},{64,72... | collective-permute-start | bytes 786440 | tf_op jit(solution)/shard_map/ppermute | solution.py:30
  16.7 5.7 %copy-start.2 = (f32[1,1,1024,1024]{3,2,1,0:T(8,128)S(1)}, f32[1,1,1024,1024]{3,2,1,0:T(8,128)}, u32[]{:S(2)}) copy-start(f32[1,1,1024,1024]{3,2,1,0:T(8,128)} %param.7) | copy-start | bytes 12582916
  16.7 10.0 %collective-permute-start.6 = (f32[256,256]{1,0:T(8,128)S(1)}, f32[256,256]{1,0:T(8,128)S(1)}, u32[]{:S(2)}, u32[]{:S(2)}) collective-permute-start(f32[256,256]{1,0:T(8,128)S(1)} %get-tuple-element.74.f3), channel_id=1, source_target_pairs={{0,248},{8,16},{16,8},{24,32},{32,24},{40,48},{48,40},{56,64},{64,... | collective-permute-start | bytes 786440 | tf_op jit(solution)/shard_map/ppermute | solution.py:34
  19.3 8.7 %collective-permute-start.4 = (f32[256,256]{1,0:T(8,128)S(1)}, f32[256,256]{1,0:T(8,128)S(1)}, u32[]{:S(2)}, u32[]{:S(2)}) collective-permute-start(f32[256,256]{1,0:T(8,128)S(1)} %get-tuple-element.71.f0), channel_id=1, source_target_pairs={{0,1},{1,2},{2,3},{3,4},{4,5},{5,6},{6,7},{7,0},{8,9},{9,10},{10,1... | collective-permute-start | bytes 786440 | tf_op jit(solution)/shard_map/ppermute | solution.py:26
  22.3 6.1 %collective-permute-start.3 = (f32[256,256]{1,0:T(8,128)S(1)}, f32[256,256]{1,0:T(8,128)S(1)}, u32[]{:S(2)}, u32[]{:S(2)}) collective-permute-start(f32[256,256]{1,0:T(8,128)S(1)} %get-tuple-element.72.f1), channel_id=1, source_target_pairs={{0,7},{1,0},{2,1},{3,2},{4,3},{5,4},{6,5},{7,6},{8,15},{9,8},{10,9... | collective-permute-start | bytes 786440 | tf_op jit(solution)/shard_map/ppermute | solution.py:26
  22.5 4.3 %copy-start = (f32[1,1,256,1024]{3,2,1,0:T(8,128)S(1)}, f32[1,1,256,1024]{3,2,1,0:T(8,128)}, u32[]{:S(2)}) copy-start(f32[1,1,256,1024]{3,2,1,0:T(8,128)} %param.9) | copy-start | bytes 3145732
  28.4 29.5 %copy-start.5 = (f32[256,256]{1,0:T(8,128)S(1)}, f32[256,256]{1,0:T(8,128)}, u32[]{:S(2)}) copy-start(f32[256,256]{1,0:T(8,128)} %coarse.3) | copy-start | bytes 786436
  29.9 2.9 %collective-permute-start.7 = (f32[128,384]{1,0:T(8,128)S(1)}, f32[128,384]{1,0:T(8,128)S(1)}, u32[]{:S(2)}, u32[]{:S(2)}) collective-permute-start(f32[128,384]{1,0:T(8,128)S(1)} %get-tuple-element.82), channel_id=1, source_target_pairs={{0,1},{1,0},{2,3},{3,2},{4,5},{5,4},{6,7},{7,6},{8,9},{9,8},{10,11... | collective-permute-start | bytes 589832 | tf_op jit(solution)/shard_map/ppermute | solution.py:38
  43.9 14.9 %collective-permute-start.8 = (f32[512,256]{1,0:T(8,128)S(1)}, f32[512,256]{1,0:T(8,128)S(1)}, u32[]{:S(2)}, u32[]{:S(2)}) collective-permute-start(f32[512,256]{1,0:T(8,128)S(1)} %get-tuple-element.88.f1), channel_id=1, source_target_pairs={{0,7},{1,0},{2,1},{3,2},{4,3},{5,4},{6,5},{7,6},{8,15},{9,8},{10,9... | collective-permute-start | bytes 1572872 | tf_op jit(solution)/shard_map/ppermute | solution.py:26
  45.7 13.1 %collective-permute-start.9 = (f32[512,256]{1,0:T(8,128)S(1)}, f32[512,256]{1,0:T(8,128)S(1)}, u32[]{:S(2)}, u32[]{:S(2)}) collective-permute-start(f32[512,256]{1,0:T(8,128)S(1)} %get-tuple-element.89.f0), channel_id=1, source_target_pairs={{0,1},{1,2},{2,3},{3,4},{4,5},{5,6},{6,7},{7,0},{8,9},{9,10},{10,1... | collective-permute-start | bytes 1572872 | tf_op jit(solution)/shard_map/ppermute | solution.py:26
  45.9 13.2 %collective-permute-start.10 = (f32[512,256]{1,0:T(8,128)S(1)}, f32[512,256]{1,0:T(8,128)S(1)}, u32[]{:S(2)}, u32[]{:S(2)}) collective-permute-start(f32[512,256]{1,0:T(8,128)S(1)} %get-tuple-element.90.f2), channel_id=1, source_target_pairs={{0,8},{8,0},{16,24},{24,16},{32,40},{40,32},{48,56},{56,48},{64,72... | collective-permute-start | bytes 1572872 | tf_op jit(solution)/shard_map/ppermute | solution.py:30
  58.3 19.8 %collective-permute-start.12 = (f32[512,256]{1,0:T(8,128)S(1)}, f32[512,256]{1,0:T(8,128)S(1)}, u32[]{:S(2)}, u32[]{:S(2)}) collective-permute-start(f32[512,256]{1,0:T(8,128)S(1)} %get-tuple-element.92.f3), channel_id=1, source_target_pairs={{0,248},{8,16},{16,8},{24,32},{32,24},{40,48},{48,40},{56,64},{64,... | collective-permute-start | bytes 1572872 | tf_op jit(solution)/shard_map/ppermute | solution.py:34
  77.6 1.6 %collective-permute-start.11 = (f32[128,384]{1,0:T(8,128)S(1)}, f32[128,384]{1,0:T(8,128)S(1)}, u32[]{:S(2)}, u32[]{:S(2)}) collective-permute-start(f32[128,384]{1,0:T(8,128)S(1)} %bitcast.28), channel_id=1, source_target_pairs={{0,1},{1,0},{2,3},{3,2},{4,5},{5,4},{6,7},{7,6},{8,9},{9,8},{10,11... | collective-permute-start | bytes 589832 | tf_op jit(solution)/shard_map/ppermute | solution.py:38
  81.0 7.6 %collective-permute-start.15 = (f32[256,256]{1,0:T(8,128)S(1)}, f32[256,256]{1,0:T(8,128)S(1)}, u32[]{:S(2)}, u32[]{:S(2)}) collective-permute-start(f32[256,256]{1,0:T(8,128)S(1)} %get-tuple-element.97.f2), channel_id=1, source_target_pairs={{0,8},{8,0},{16,24},{24,16},{32,40},{40,32},{48,56},{56,48},{64,72... | collective-permute-start | bytes 786440 | tf_op jit(solution)/shard_map/ppermute | solution.py:30
  81.1 10.9 %collective-permute-start.16 = (f32[256,256]{1,0:T(8,128)S(1)}, f32[256,256]{1,0:T(8,128)S(1)}, u32[]{:S(2)}, u32[]{:S(2)}) collective-permute-start(f32[256,256]{1,0:T(8,128)S(1)} %get-tuple-element.98.f3), channel_id=1, source_target_pairs={{0,248},{8,16},{16,8},{24,32},{32,24},{40,48},{48,40},{56,64},{64,... | collective-permute-start | bytes 786440 | tf_op jit(solution)/shard_map/ppermute | solution.py:34
  82.6 10.7 %collective-permute-start.14 = (f32[256,256]{1,0:T(8,128)S(1)}, f32[256,256]{1,0:T(8,128)S(1)}, u32[]{:S(2)}, u32[]{:S(2)}) collective-permute-start(f32[256,256]{1,0:T(8,128)S(1)} %get-tuple-element.95.f0), channel_id=1, source_target_pairs={{0,1},{1,2},{2,3},{3,4},{4,5},{5,6},{6,7},{7,0},{8,9},{9,10},{10,1... | collective-permute-start | bytes 786440 | tf_op jit(solution)/shard_map/ppermute | solution.py:26
  83.8 9.5 %collective-permute-start.13 = (f32[256,256]{1,0:T(8,128)S(1)}, f32[256,256]{1,0:T(8,128)S(1)}, u32[]{:S(2)}, u32[]{:S(2)}) collective-permute-start(f32[256,256]{1,0:T(8,128)S(1)} %get-tuple-element.96.f1), channel_id=1, source_target_pairs={{0,7},{1,0},{2,1},{3,2},{4,3},{5,4},{6,5},{7,6},{8,15},{9,8},{10,9... | collective-permute-start | bytes 786440 | tf_op jit(solution)/shard_map/ppermute | solution.py:26
  94.7 2.3 %collective-permute-start.17 = (f32[128,384]{1,0:T(8,128)S(1)}, f32[128,384]{1,0:T(8,128)S(1)}, u32[]{:S(2)}, u32[]{:S(2)}) collective-permute-start(f32[128,384]{1,0:T(8,128)S(1)} %get-tuple-element.108), channel_id=1, source_target_pairs={{0,1},{1,0},{2,3},{3,2},{4,5},{5,4},{6,7},{7,6},{8,9},{9,8},{10,11... | collective-permute-start | bytes 589832 | tf_op jit(solution)/shard_map/ppermute | solution.py:38
  109.0 14.2 %collective-permute-start.18 = (f32[256,256]{1,0:T(8,128)S(1)}, f32[256,256]{1,0:T(8,128)S(1)}, u32[]{:S(2)}, u32[]{:S(2)}) collective-permute-start(f32[256,256]{1,0:T(8,128)S(1)} %get-tuple-element.112), channel_id=1, source_target_pairs={{0,7},{1,0},{2,1},{3,2},{4,3},{5,4},{6,5},{7,6},{8,15},{9,8},{10,9... | collective-permute-start | bytes 786440 | tf_op jit(solution)/shard_map/ppermute | solution.py:26
  110.8 12.4 %collective-permute-start.19 = (f32[256,256]{1,0:T(8,128)S(1)}, f32[256,256]{1,0:T(8,128)S(1)}, u32[]{:S(2)}, u32[]{:S(2)}) collective-permute-start(f32[256,256]{1,0:T(8,128)S(1)} %get-tuple-element.113), channel_id=1, source_target_pairs={{0,248},{8,0},{16,8},{24,16},{32,24},{40,32},{48,40},{56,48},{64,5... | collective-permute-start | bytes 786440 | tf_op jit(solution)/shard_map/ppermute | solution.py:26
  133.0 4.2 %collective-permute-start.20 = (f32[128,384]{1,0:T(8,128)S(1)}, f32[128,384]{1,0:T(8,128)S(1)}, u32[]{:S(2)}, u32[]{:S(2)}) collective-permute-start(f32[128,384]{1,0:T(8,128)S(1)} %bitcast.26), channel_id=1, source_target_pairs={{0,1},{1,0},{2,3},{3,2},{4,5},{5,4},{6,7},{7,6},{8,9},{9,8},{10,11... | collective-permute-start | bytes 589832 | tf_op jit(solution)/shard_map/ppermute | solution.py:38

commit v6 on v5

--- a/solution.py
+++ b/solution.py
@@ -404,9 +404,8 @@
     loads, scalars = call(first_coarse_kernel, [copies, (PIECE, 128)], 2, "coarse_first")(
         along_z(rows), coarse_inverse
     )
-    *early, _ = after(w, rows)
-    got = exchange((*early, after(w[3], loads)))
-    loads = after(loads, got[:3])
+    got = exchange(after(w, rows))
+    loads = after(loads, got)
     v2, v3, *u, image_deck, image_joint, res_deck, res_joint, corner_deck, corner_joint, steps = call(
         precond_kernel, pair + narrow + [face] * 6 + [(CASES, 128)], 17, "precond_span",
         scratch=(whole,), estimate=cost(CASES // 2), grant=10,

time: 139 us -> 138 us (level)
  starting transfers between devices: 24.1 us -> 29.4 us
  blocking collectives: 74.7 us -> 69.8 us
    all_to_all x2, blocking collectives: 28.3 us -> 23.3 us  [gather_rows(): mine = lax.all_to_all(copies, ('y', 'x'), 0, 0).reshape(HALF, WIDE)]
    ppermute x3, starting transfers between devices: 2.96 us -> 5.82 us  [far(): lax.ppermute(block, SPAN, [(i, (i + (1 if i % 2 else -1)) % SPANS) for i...]
    all_to_all x2, blocking collectives: 23.3 us -> 25 us  [along_z(): return lax.all_to_all(copies, 'z', 0, 0)]
    ppermute x4, starting transfers between devices: 6.73 us -> 8.39 us  [swapped(): return lax.ppermute(block, 'core', [(0, 1), (1, 0)])]
    all_to_all x2, blocking collectives: 23 us -> 21.5 us  [scatter_rows(): return lax.all_to_all(block, ('y', 'x'), 0, 0)]
where the time goes in v6:
time: 138 us
  blocking collectives  69.8 us (51%)
  starting transfers between devices  29.4 us (21%)
  waiting for transfers between devices  22 us (16%)
  Pallas kernels  14.7 us (11%)
    all_to_all x2, blocking collectives, along_z(): return lax.all_to_all(copies, 'z', 0, 0)  25 us
    all_to_all x2, blocking collectives, gather_rows(): mine = lax.all_to_all(copies, ('y', 'x'), 0, 0).reshape(HALF, WIDE)  23.3 us
    all_to_all x2, blocking collectives, scatter_rows(): return lax.all_to_all(block, ('y', 'x'), 0, 0)  21.5 us
    ppermute x11, starting transfers between devices, cyclic(): return lax.ppermute(block, axes, [(i, (i + k) % n) for i in range(n)])  15 us
    ppermute x4, starting transfers between devices, swapped(): return lax.ppermute(block, 'core', [(0, 1), (1, 0)])  8.39 us
    ppermute x3, waiting for transfers between devices, far(): lax.ppermute(block, SPAN, [(i, (i + (1 if i % 2 else -1)) % SPANS) for i...  7.06 us
    ppermute x11, waiting for transfers between devices, cyclic(): return lax.ppermute(block, axes, [(i, (i + k) % n) for i in range(n)])  6.68 us
    ppermute x3, starting transfers between devices, far(): lax.ppermute(block, SPAN, [(i, (i + (1 if i % 2 else -1)) % SPANS) for i...  5.82 us
  transfers between devices with their start and end apart: 21, of which 11 were waited for; matrix products, arithmetic and copies ran while one was open for 0% of the time, Pallas kernels for 6%

profile of v6, /device:TPU:1, one launch (start us, length us, event | category | flops | bytes accessed | tf_op | source)
XLA Modules:
  0.0 137.9 jit_solution(484427425891199639)
XLA Ops:
  0.6 2.2 %collective-permute-start = (f32[256,256]{1,0:T(8,128)}, f32[256,256]{1,0:T(8,128)S(1)}, u32[]{:S(2)}, u32[]{:S(2)}) collective-permute-start(f32[256,256]{1,0:T(8,128)} %bitcast.18), channel_id=1, source_target_pairs={{0,8},{8,16},{16,24},{24,32},{32,40},{40,48},{48,56},{56,64},{64,7... | collective-permute-start | bytes 786440 | tf_op jit(solution)/shard_map/ppermute | solution.py:26
  4.4 2.1 %collective-permute-start.2 = (f32[256,256]{1,0:T(8,128)S(1)}, f32[256,256]{1,0:T(8,128)S(1)}, u32[]{:S(2)}, u32[]{:S(2)}) collective-permute-start(f32[256,256]{1,0:T(8,128)S(1)} %bitcast.22), channel_id=1, source_target_pairs={{0,1},{1,2},{2,3},{3,4},{4,5},{5,6},{6,7},{7,0},{8,9},{9,10},{10,1... | collective-permute-start | bytes 786440 | tf_op jit(solution)/shard_map/ppermute | solution.py:26
  6.5 1.3 collective-permute-start.1
  9.7 6.2 %collective-permute-done.1.lives_behind = f32[8,256]{1,0:T(8,128)S(1)} collective-permute-done((f32[8,256]{1,0:T(8,128)S(1)}, f32[8,256]{1,0:T(8,128)S(1)}, u32[]{:S(2)}, u32[]{:S(2)}) %collective-permute-start.1) | collective-permute-done | bytes 8224 | tf_op jit(solution)/shard_map/ppermute | solution.py:26
  16.7 1.9 %collective-permute-start.6 = (f32[256,256]{1,0:T(8,128)S(1)}, f32[256,256]{1,0:T(8,128)S(1)}, u32[]{:S(2)}, u32[]{:S(2)}) collective-permute-start(f32[256,256]{1,0:T(8,128)S(1)} %get-tuple-element.74.f3), channel_id=1, source_target_pairs={{0,248},{8,16},{16,8},{24,32},{32,24},{40,48},{48,40},{56,64},{64,... | collective-permute-start | bytes 786440 | tf_op jit(solution)/shard_map/ppermute | solution.py:34
  19.3 3.1 %collective-permute-start.4 = (f32[256,256]{1,0:T(8,128)S(1)}, f32[256,256]{1,0:T(8,128)S(1)}, u32[]{:S(2)}, u32[]{:S(2)}) collective-permute-start(f32[256,256]{1,0:T(8,128)S(1)} %get-tuple-element.71.f0), channel_id=1, source_target_pairs={{0,1},{1,2},{2,3},{3,4},{4,5},{5,6},{6,7},{7,0},{8,9},{9,10},{10,1... | collective-permute-start | bytes 786440 | tf_op jit(solution)/shard_map/ppermute | solution.py:26
  23.3 3.4 %collective-permute-done.6.g3 = f32[256,256]{1,0:T(8,128)S(1)} collective-permute-done((f32[256,256]{1,0:T(8,128)S(1)}, f32[256,256]{1,0:T(8,128)S(1)}, u32[]{:S(2)}, u32[]{:S(2)}) %collective-permute-start.6) | collective-permute-done | bytes 262176 | tf_op jit(solution)/shard_map/ppermute | solution.py:34
  26.7 1.2 flex_first_span.1
  28.4 1.5 %flex_first.1 = (f32[512,256]{1,0:T(8,128)S(1)}, f32[512,256]{1,0:T(8,128)S(1)}, f32[512,256]{1,0:T(8,128)S(1)}, f32[512,256]{1,0:T(8,128)S(1)}, f32[256,256]{1,...) custom-call(f32[8,256]{1,0:T(8,128)S(1)} %get-tuple-element.70.masks, ...), custom_call_target="tpu_custom_call" | custom-call | flops 805306368 | bytes 8388608 | tf_op jit(solution)/shard_map/flex_first/pallas_call | solution.py:371
  29.9 1.8 %collective-permute-start.7 = (f32[128,384]{1,0:T(8,128)S(1)}, f32[128,384]{1,0:T(8,128)S(1)}, u32[]{:S(2)}, u32[]{:S(2)}) collective-permute-start(f32[128,384]{1,0:T(8,128)S(1)} %get-tuple-element.82), channel_id=1, source_target_pairs={{0,1},{1,0},{2,3},{3,2},{4,5},{5,4},{6,7},{7,6},{8,9},{9,8},{10,11... | collective-permute-start | bytes 589832 | tf_op jit(solution)/shard_map/ppermute | solution.py:38
  31.7 1.1 collective-permute-done.7.got
  32.8 11.1 %all_to_all.30.got = f32[16,8,384]{2,1,0:T(8,128)S(1)} all-to-all(f32[16,8,384]{2,1,0:T(8,128)S(1)} %add.2), channel_id=1, replica_groups=mesh['z'=8,'y'=4,'x'=4,'core'=2] {'y','x'}, dimensions={0} | all-to-all | bytes 393216 | tf_op jit(solution)/shard_map/all_to_all | solution.py:340
  43.9 1.8 %collective-permute-start.8 = (f32[512,256]{1,0:T(8,128)S(1)}, f32[512,256]{1,0:T(8,128)S(1)}, u32[]{:S(2)}, u32[]{:S(2)}) collective-permute-start(f32[512,256]{1,0:T(8,128)S(1)} %get-tuple-element.88.f1), channel_id=1, source_target_pairs={{0,7},{1,0},{2,1},{3,2},{4,3},{5,4},{6,5},{7,6},{8,15},{9,8},{10,9... | collective-permute-start | bytes 1572872 | tf_op jit(solution)/shard_map/ppermute | solution.py:26
  45.9 2.2 %collective-permute-start.11 = (f32[512,256]{1,0:T(8,128)S(1)}, f32[512,256]{1,0:T(8,128)S(1)}, u32[]{:S(2)}, u32[]{:S(2)}) collective-permute-start(f32[512,256]{1,0:T(8,128)S(1)} %get-tuple-element.91.f3), channel_id=1, source_target_pairs={{0,248},{8,16},{16,8},{24,32},{32,24},{40,48},{48,40},{56,64},{64,... | collective-permute-start | bytes 1572872 | tf_op jit(solution)/shard_map/ppermute | solution.py:34
  48.2 13.0 %all_to_all.31.got = f32[8,8,384]{2,1,0:T(8,128)S(1)} all-to-all(f32[8,8,384]{2,1,0:T(8,128)S(1)} %spread.2), channel_id=1, replica_groups=mesh['z'=8,'y'=4,'x'=4,'core'=2] {'z'}, dimensions={0} | all-to-all | bytes 196608 | tf_op jit(solution)/shard_map/all_to_all | solution.py:345
  62.1 13.5 %all_to_all.32 = f32[16,8,384]{2,1,0:T(8,128)S(1)} all-to-all(f32[16,8,384]{2,1,0:T(8,128)S(1)} %get-tuple-element.92), channel_id=1, replica_groups=mesh['z'=8,'y'=4,'x'=4,'core'=2] {'y','x'}, dimensions={0} | all-to-all | bytes 393216 | tf_op jit(solution)/shard_map/all_to_all | solution.py:349
  75.6 1.9 %collective-permute-start.12 = (f32[128,384]{1,0:T(8,128)S(1)}, f32[128,384]{1,0:T(8,128)S(1)}, u32[]{:S(2)}, u32[]{:S(2)}) collective-permute-start(f32[128,384]{1,0:T(8,128)S(1)} %bitcast.28), channel_id=1, source_target_pairs={{0,1},{1,0},{2,3},{3,2},{4,5},{5,4},{6,7},{7,6},{8,9},{9,8},{10,11... | collective-permute-start | bytes 589832 | tf_op jit(solution)/shard_map/ppermute | solution.py:38
  77.5 1.1 collective-permute-done.12.other
  78.6 1.8 %precond_span.1 = (f32[256,256]{1,0:T(8,128)S(1)}, f32[256,256]{1,0:T(8,128)S(1)}, bf16[256,1024]{1,0:T(8,128)(2,1)S(1)}, bf16[256,1024]{1,0:T(8,128)(2,1)S(1)},...) custom-call(f32[8,256]{1,0:T(8,128)S(1)} %get-tuple-element.70.masks, ...), custom_call_target="tpu_custom_call" | custom-call | flops 805306368 | bytes 8388608 | tf_op jit(solution)/shard_map/precond_span/pallas_call | solution.py:409
  80.5 1.6 %collective-permute-start.16 = (f32[256,256]{1,0:T(8,128)S(1)}, f32[256,256]{1,0:T(8,128)S(1)}, u32[]{:S(2)}, u32[]{:S(2)}) collective-permute-start(f32[256,256]{1,0:T(8,128)S(1)} %get-tuple-element.98.f3), channel_id=1, source_target_pairs={{0,248},{8,16},{16,8},{24,32},{32,24},{40,48},{48,40},{56,64},{64,... | collective-permute-start | bytes 786440 | tf_op jit(solution)/shard_map/ppermute | solution.py:34
  84.1 3.8 %collective-permute-done.15.g2 = f32[256,256]{1,0:T(8,128)S(1)} collective-permute-done((f32[256,256]{1,0:T(8,128)S(1)}, f32[256,256]{1,0:T(8,128)S(1)}, u32[]{:S(2)}, u32[]{:S(2)}) %collective-permute-start.15) | collective-permute-done | bytes 262176 | tf_op jit(solution)/shard_map/ppermute | solution.py:30
  88.0 3.2 %collective-permute-done.16.g3 = f32[256,256]{1,0:T(8,128)S(1)} collective-permute-done((f32[256,256]{1,0:T(8,128)S(1)}, f32[256,256]{1,0:T(8,128)S(1)}, u32[]{:S(2)}, u32[]{:S(2)}) %collective-permute-start.16) | collective-permute-done | bytes 262176 | tf_op jit(solution)/shard_map/ppermute | solution.py:34
  91.2 1.2 flex_second_span.1
  92.5 1.5 %flex_second.1 = (f32[256,256]{1,0:T(8,128)S(1)}, f32[256,256]{1,0:T(8,128)S(1)}, f32[256,256]{1,0:T(8,128)S(1)}, f32[256,256]{1,0:T(8,128)S(1)}, f32[256,256]{1...) custom-call(f32[8,256]{1,0:T(8,128)S(1)} %get-tuple-element.70.masks, ...), custom_call_target="tpu_custom_call" | custom-call | flops 805306368 | bytes 8388608 | tf_op jit(solution)/shard_map/flex_second/pallas_call | solution.py:371
  93.9 1.5 %collective-permute-start.17 = (f32[128,384]{1,0:T(8,128)S(1)}, f32[128,384]{1,0:T(8,128)S(1)}, u32[]{:S(2)}, u32[]{:S(2)}) collective-permute-start(f32[128,384]{1,0:T(8,128)S(1)} %get-tuple-element.108), channel_id=1, source_target_pairs={{0,1},{1,0},{2,3},{3,2},{4,5},{5,4},{6,7},{7,6},{8,9},{9,8},{10,11... | collective-permute-start | bytes 589832 | tf_op jit(solution)/shard_map/ppermute | solution.py:38
  96.5 10.4 %all_to_all.33.got = f32[16,8,384]{2,1,0:T(8,128)S(1)} all-to-all(f32[16,8,384]{2,1,0:T(8,128)S(1)} %add.3), channel_id=1, replica_groups=mesh['z'=8,'y'=4,'x'=4,'core'=2] {'y','x'}, dimensions={0} | all-to-all | bytes 393216 | tf_op jit(solution)/shard_map/all_to_all | solution.py:340
  106.9 1.3 collective-permute-start.18
  108.2 2.0 %collective-permute-start.19 = (f32[256,256]{1,0:T(8,128)S(1)}, f32[256,256]{1,0:T(8,128)S(1)}, u32[]{:S(2)}, u32[]{:S(2)}) collective-permute-start(f32[256,256]{1,0:T(8,128)S(1)} %get-tuple-element.113), channel_id=1, source_target_pairs={{0,248},{8,0},{16,8},{24,16},{32,24},{40,32},{48,40},{56,48},{64,5... | collective-permute-start | bytes 786440 | tf_op jit(solution)/shard_map/ppermute | solution.py:26
  110.2 12.0 %all_to_all.34.got = f32[8,8,384]{2,1,0:T(8,128)S(1)} all-to-all(f32[8,8,384]{2,1,0:T(8,128)S(1)} %spread.3), channel_id=1, replica_groups=mesh['z'=8,'y'=4,'x'=4,'core'=2] {'z'}, dimensions={0} | all-to-all | bytes 196608 | tf_op jit(solution)/shard_map/all_to_all | solution.py:345
  122.6 9.8 %all_to_all.35 = f32[16,8,384]{2,1,0:T(8,128)S(1)} all-to-all(f32[16,8,384]{2,1,0:T(8,128)S(1)} %coarse_second.1), channel_id=1, replica_groups=mesh['z'=8,'y'=4,'x'=4,'core'=2] {'y','x'}, dimensions={0} | all-to-all | bytes 393216 | tf_op jit(solution)/shard_map/all_to_all | solution.py:349
  132.4 3.1 %collective-permute-start.20 = (f32[128,384]{1,0:T(8,128)S(1)}, f32[128,384]{1,0:T(8,128)S(1)}, u32[]{:S(2)}, u32[]{:S(2)}) collective-permute-start(f32[128,384]{1,0:T(8,128)S(1)} %bitcast.26), channel_id=1, source_target_pairs={{0,1},{1,0},{2,3},{3,2},{4,5},{5,4},{6,7},{7,6},{8,9},{9,8},{10,11... | collective-permute-start | bytes 589832 | tf_op jit(solution)/shard_map/ppermute | solution.py:38
  136.6 1.3 final.1
  (50 shorter events, 12.0 us)
Async XLA Ops:
  0.6 15.4 %collective-permute-start = (f32[256,256]{1,0:T(8,128)}, f32[256,256]{1,0:T(8,128)S(1)}, u32[]{:S(2)}, u32[]{:S(2)}) collective-permute-start(f32[256,256]{1,0:T(8,128)} %bitcast.18), channel_id=1, source_target_pairs={{0,8},{8,16},{16,24},{24,32},{32,40},{40,48},{48,56},{56,64},{64,7... | collective-permute-start | bytes 786440 | tf_op jit(solution)/shard_map/ppermute | solution.py:26
  2.8 0.7 copy-start.6
  3.5 0.9 copy-start.4
  3.5 4.3 %copy-start.1 = (f32[1,1,1024,1024]{3,2,1,0:T(8,128)S(1)}, f32[1,1,1024,1024]{3,2,1,0:T(8,128)}, u32[]{:S(2)}) copy-start(f32[1,1,1024,1024]{3,2,1,0:T(8,128)} %param.8) | copy-start | bytes 12582916
  4.4 11.6 %collective-permute-start.2 = (f32[256,256]{1,0:T(8,128)S(1)}, f32[256,256]{1,0:T(8,128)S(1)}, u32[]{:S(2)}, u32[]{:S(2)}) collective-permute-start(f32[256,256]{1,0:T(8,128)S(1)} %bitcast.22), channel_id=1, source_target_pairs={{0,1},{1,2},{2,3},{3,4},{4,5},{5,6},{6,7},{7,0},{8,9},{9,10},{10,1... | collective-permute-start | bytes 786440 | tf_op jit(solution)/shard_map/ppermute | solution.py:26
  6.5 9.5 %collective-permute-start.1 = (f32[8,256]{1,0:T(8,128)S(1)}, f32[8,256]{1,0:T(8,128)S(1)}, u32[]{:S(2)}, u32[]{:S(2)}) collective-permute-start(f32[8,256]{1,0:T(8,128)S(1)} %lives.1), channel_id=1, source_target_pairs={{0,8},{8,16},{16,24},{24,32},{32,40},{40,48},{48,56},{56,64},{64,7... | collective-permute-start | bytes 24584 | tf_op jit(solution)/shard_map/ppermute | solution.py:26
  7.8 1.0 copy-start.3
  16.6 6.7 %collective-permute-start.5 = (f32[256,256]{1,0:T(8,128)S(1)}, f32[256,256]{1,0:T(8,128)S(1)}, u32[]{:S(2)}, u32[]{:S(2)}) collective-permute-start(f32[256,256]{1,0:T(8,128)S(1)} %get-tuple-element.73.f2), channel_id=1, source_target_pairs={{0,8},{8,0},{16,24},{24,16},{32,40},{40,32},{48,56},{56,48},{64,72... | collective-permute-start | bytes 786440 | tf_op jit(solution)/shard_map/ppermute | solution.py:30
  16.7 5.7 %copy-start.2 = (f32[1,1,1024,1024]{3,2,1,0:T(8,128)S(1)}, f32[1,1,1024,1024]{3,2,1,0:T(8,128)}, u32[]{:S(2)}) copy-start(f32[1,1,1024,1024]{3,2,1,0:T(8,128)} %param.7) | copy-start | bytes 12582916
  16.7 10.0 %collective-permute-start.6 = (f32[256,256]{1,0:T(8,128)S(1)}, f32[256,256]{1,0:T(8,128)S(1)}, u32[]{:S(2)}, u32[]{:S(2)}) collective-permute-start(f32[256,256]{1,0:T(8,128)S(1)} %get-tuple-element.74.f3), channel_id=1, source_target_pairs={{0,248},{8,16},{16,8},{24,32},{32,24},{40,48},{48,40},{56,64},{64,... | collective-permute-start | bytes 786440 | tf_op jit(solution)/shard_map/ppermute | solution.py:34
  19.3 8.7 %collective-permute-start.4 = (f32[256,256]{1,0:T(8,128)S(1)}, f32[256,256]{1,0:T(8,128)S(1)}, u32[]{:S(2)}, u32[]{:S(2)}) collective-permute-start(f32[256,256]{1,0:T(8,128)S(1)} %get-tuple-element.71.f0), channel_id=1, source_target_pairs={{0,1},{1,2},{2,3},{3,4},{4,5},{5,6},{6,7},{7,0},{8,9},{9,10},{10,1... | collective-permute-start | bytes 786440 | tf_op jit(solution)/shard_map/ppermute | solution.py:26
  22.3 6.1 %collective-permute-start.3 = (f32[256,256]{1,0:T(8,128)S(1)}, f32[256,256]{1,0:T(8,128)S(1)}, u32[]{:S(2)}, u32[]{:S(2)}) collective-permute-start(f32[256,256]{1,0:T(8,128)S(1)} %get-tuple-element.72.f1), channel_id=1, source_target_pairs={{0,7},{1,0},{2,1},{3,2},{4,3},{5,4},{6,5},{7,6},{8,15},{9,8},{10,9... | collective-permute-start | bytes 786440 | tf_op jit(solution)/shard_map/ppermute | solution.py:26
  22.5 4.3 %copy-start = (f32[1,1,256,1024]{3,2,1,0:T(8,128)S(1)}, f32[1,1,256,1024]{3,2,1,0:T(8,128)}, u32[]{:S(2)}) copy-start(f32[1,1,256,1024]{3,2,1,0:T(8,128)} %param.9) | copy-start | bytes 3145732
  28.4 32.8 %copy-start.5 = (f32[256,256]{1,0:T(8,128)S(1)}, f32[256,256]{1,0:T(8,128)}, u32[]{:S(2)}) copy-start(f32[256,256]{1,0:T(8,128)} %coarse.3) | copy-start | bytes 786436
  29.9 2.9 %collective-permute-start.7 = (f32[128,384]{1,0:T(8,128)S(1)}, f32[128,384]{1,0:T(8,128)S(1)}, u32[]{:S(2)}, u32[]{:S(2)}) collective-permute-start(f32[128,384]{1,0:T(8,128)S(1)} %get-tuple-element.82), channel_id=1, source_target_pairs={{0,1},{1,0},{2,3},{3,2},{4,5},{5,4},{6,7},{7,6},{8,9},{9,8},{10,11... | collective-permute-start | bytes 589832 | tf_op jit(solution)/shard_map/ppermute | solution.py:38
  43.9 17.7 %collective-permute-start.8 = (f32[512,256]{1,0:T(8,128)S(1)}, f32[512,256]{1,0:T(8,128)S(1)}, u32[]{:S(2)}, u32[]{:S(2)}) collective-permute-start(f32[512,256]{1,0:T(8,128)S(1)} %get-tuple-element.88.f1), channel_id=1, source_target_pairs={{0,7},{1,0},{2,1},{3,2},{4,3},{5,4},{6,5},{7,6},{8,15},{9,8},{10,9... | collective-permute-start | bytes 1572872 | tf_op jit(solution)/shard_map/ppermute | solution.py:26
  45.7 15.9 %collective-permute-start.9 = (f32[512,256]{1,0:T(8,128)S(1)}, f32[512,256]{1,0:T(8,128)S(1)}, u32[]{:S(2)}, u32[]{:S(2)}) collective-permute-start(f32[512,256]{1,0:T(8,128)S(1)} %get-tuple-element.89.f0), channel_id=1, source_target_pairs={{0,1},{1,2},{2,3},{3,4},{4,5},{5,6},{6,7},{7,0},{8,9},{9,10},{10,1... | collective-permute-start | bytes 1572872 | tf_op jit(solution)/shard_map/ppermute | solution.py:26
  45.9 15.8 %collective-permute-start.10 = (f32[512,256]{1,0:T(8,128)S(1)}, f32[512,256]{1,0:T(8,128)S(1)}, u32[]{:S(2)}, u32[]{:S(2)}) collective-permute-start(f32[512,256]{1,0:T(8,128)S(1)} %get-tuple-element.90.f2), channel_id=1, source_target_pairs={{0,8},{8,0},{16,24},{24,16},{32,40},{40,32},{48,56},{56,48},{64,72... | collective-permute-start | bytes 1572872 | tf_op jit(solution)/shard_map/ppermute | solution.py:30
  45.9 16.2 %collective-permute-start.11 = (f32[512,256]{1,0:T(8,128)S(1)}, f32[512,256]{1,0:T(8,128)S(1)}, u32[]{:S(2)}, u32[]{:S(2)}) collective-permute-start(f32[512,256]{1,0:T(8,128)S(1)} %get-tuple-element.91.f3), channel_id=1, source_target_pairs={{0,248},{8,16},{16,8},{24,32},{32,24},{40,48},{48,40},{56,64},{64,... | collective-permute-start | bytes 1572872 | tf_op jit(solution)/shard_map/ppermute | solution.py:34
  75.6 3.0 %collective-permute-start.12 = (f32[128,384]{1,0:T(8,128)S(1)}, f32[128,384]{1,0:T(8,128)S(1)}, u32[]{:S(2)}, u32[]{:S(2)}) collective-permute-start(f32[128,384]{1,0:T(8,128)S(1)} %bitcast.28), channel_id=1, source_target_pairs={{0,1},{1,0},{2,3},{3,2},{4,5},{5,4},{6,7},{7,6},{8,9},{9,8},{10,11... | collective-permute-start | bytes 589832 | tf_op jit(solution)/shard_map/ppermute | solution.py:38
  80.4 7.6 %collective-permute-start.15 = (f32[256,256]{1,0:T(8,128)S(1)}, f32[256,256]{1,0:T(8,128)S(1)}, u32[]{:S(2)}, u32[]{:S(2)}) collective-permute-start(f32[256,256]{1,0:T(8,128)S(1)} %get-tuple-element.97.f2), channel_id=1, source_target_pairs={{0,8},{8,0},{16,24},{24,16},{32,40},{40,32},{48,56},{56,48},{64,72... | collective-permute-start | bytes 786440 | tf_op jit(solution)/shard_map/ppermute | solution.py:30
  80.5 10.7 %collective-permute-start.16 = (f32[256,256]{1,0:T(8,128)S(1)}, f32[256,256]{1,0:T(8,128)S(1)}, u32[]{:S(2)}, u32[]{:S(2)}) collective-permute-start(f32[256,256]{1,0:T(8,128)S(1)} %get-tuple-element.98.f3), channel_id=1, source_target_pairs={{0,248},{8,16},{16,8},{24,32},{32,24},{40,48},{48,40},{56,64},{64,... | collective-permute-start | bytes 786440 | tf_op jit(solution)/shard_map/ppermute | solution.py:34
  83.1 9.4 %collective-permute-start.14 = (f32[256,256]{1,0:T(8,128)S(1)}, f32[256,256]{1,0:T(8,128)S(1)}, u32[]{:S(2)}, u32[]{:S(2)}) collective-permute-start(f32[256,256]{1,0:T(8,128)S(1)} %get-tuple-element.95.f0), channel_id=1, source_target_pairs={{0,1},{1,2},{2,3},{3,4},{4,5},{5,6},{6,7},{7,0},{8,9},{9,10},{10,1... | collective-permute-start | bytes 786440 | tf_op jit(solution)/shard_map/ppermute | solution.py:26
  84.1 8.3 %collective-permute-start.13 = (f32[256,256]{1,0:T(8,128)S(1)}, f32[256,256]{1,0:T(8,128)S(1)}, u32[]{:S(2)}, u32[]{:S(2)}) collective-permute-start(f32[256,256]{1,0:T(8,128)S(1)} %get-tuple-element.96.f1), channel_id=1, source_target_pairs={{0,7},{1,0},{2,1},{3,2},{4,3},{5,4},{6,5},{7,6},{8,15},{9,8},{10,9... | collective-permute-start | bytes 786440 | tf_op jit(solution)/shard_map/ppermute | solution.py:26
  93.9 2.5 %collective-permute-start.17 = (f32[128,384]{1,0:T(8,128)S(1)}, f32[128,384]{1,0:T(8,128)S(1)}, u32[]{:S(2)}, u32[]{:S(2)}) collective-permute-start(f32[128,384]{1,0:T(8,128)S(1)} %get-tuple-element.108), channel_id=1, source_target_pairs={{0,1},{1,0},{2,3},{3,2},{4,5},{5,4},{6,7},{7,6},{8,9},{9,8},{10,11... | collective-permute-start | bytes 589832 | tf_op jit(solution)/shard_map/ppermute | solution.py:38
  106.9 15.7 %collective-permute-start.18 = (f32[256,256]{1,0:T(8,128)S(1)}, f32[256,256]{1,0:T(8,128)S(1)}, u32[]{:S(2)}, u32[]{:S(2)}) collective-permute-start(f32[256,256]{1,0:T(8,128)S(1)} %get-tuple-element.112), channel_id=1, source_target_pairs={{0,7},{1,0},{2,1},{3,2},{4,3},{5,4},{6,5},{7,6},{8,15},{9,8},{10,9... | collective-permute-start | bytes 786440 | tf_op jit(solution)/shard_map/ppermute | solution.py:26
  108.2 14.4 %collective-permute-start.19 = (f32[256,256]{1,0:T(8,128)S(1)}, f32[256,256]{1,0:T(8,128)S(1)}, u32[]{:S(2)}, u32[]{:S(2)}) collective-permute-start(f32[256,256]{1,0:T(8,128)S(1)} %get-tuple-element.113), channel_id=1, source_target_pairs={{0,248},{8,0},{16,8},{24,16},{32,24},{40,32},{48,40},{56,48},{64,5... | collective-permute-start | bytes 786440 | tf_op jit(solution)/shard_map/ppermute | solution.py:26
  132.4 4.2 %collective-permute-start.20 = (f32[128,384]{1,0:T(8,128)S(1)}, f32[128,384]{1,0:T(8,128)S(1)}, u32[]{:S(2)}, u32[]{:S(2)}) collective-permute-start(f32[128,384]{1,0:T(8,128)S(1)} %bitcast.26), channel_id=1, source_target_pairs={{0,1},{1,0},{2,3},{3,2},{4,5},{5,4},{6,7},{7,6},{8,9},{9,8},{10,11... | collective-permute-start | bytes 589832 | tf_op jit(solution)/shard_map/ppermute | solution.py:38

commit v7 on v6

--- a/solution.py
+++ b/solution.py
@@ -172,7 +172,7 @@
     return fields, product(pair, parts(corners[:, rows]), TRANS)
 
 
-def flex_span_kernel(masks, f2, f3, g2, g3, high, low, corners, part, corner_part, third, fourth):
+def flex_span_kernel(masks, f3, f2, g3, g2, high, low, corners, part, corner_part, third, fourth):
     third[...], fourth[...] = span_jumps(masks, (f2, f3), (g2, g3))
     fields, corner = two_quarters([third[...], fourth[...]], (high, low), corners, 2 * FACE)
     for i in range(4):
@@ -318,7 +318,8 @@
 def exchange(field):
     right, left, to_near, to_far = field
     right_got, left_got = cyclic(right, DECK, 1), cyclic(left, DECK, -1)
-    return left_got, right_got, near(to_near), far(to_far)
+    far_got = far(to_far)
+    return left_got, right_got, near(to_near), far_got
 
 
 def add_kernel(held, got, out):
@@ -367,7 +368,7 @@
         part, corner, third, fourth = call(
             flex_span_kernel, [wide, (CASES, NC), face, face], 8, name + "_span",
             estimate=cost(CASES // 2), grant=10,
-        )(masks, *v[2:], *got[2:], *flex_pair, corners)
+        )(masks, *v[:1:-1], *got[:1:-1], *flex_pair, corners)
         *w, first, sent, held = call(
             functools.partial(flex_kernel, n_faces), shapes + [face, half, half], 12 + 2 * n_faces,
             name, scratch=(whole,), estimate=cost(CASES // 2), grant=10,

time: 138 us -> 140 us (1.014)
  blocking collectives: 69.8 us -> 72.3 us
    ppermute x3, waiting for transfers between devices: 7.06 us -> 11.6 us  [far(): lax.ppermute(block, SPAN, [(i, (i + (1 if i % 2 else -1)) % SPANS) for i...]
    ppermute x3, waiting for transfers between devices: 3.92 us -> 0.01 us  [near(): return lax.ppermute(block, SPAN, [(i, i ^ 1) for i in range(SPANS)])]
    all_to_all x2, blocking collectives: 21.5 us -> 23.5 us  [scatter_rows(): return lax.all_to_all(block, ('y', 'x'), 0, 0)]
  transfers between devices with their start and end apart: 21 -> 21, of which waited for: 11 -> 7; matrix products, arithmetic and copies ran while one was open for 0% -> 0% of each run, Pallas kernels for 6% -> 6%
where the time goes in v7:
time: 140 us
  blocking collectives  72.3 us (52%)
  starting transfers between devices  28.5 us (20%)
  waiting for transfers between devices  22.1 us (16%)
  Pallas kernels  14.7 us (10%)
    all_to_all x2, blocking collectives, along_z(): return lax.all_to_all(copies, 'z', 0, 0)  26 us
    all_to_all x2, blocking collectives, scatter_rows(): return lax.all_to_all(block, ('y', 'x'), 0, 0)  23.5 us
    all_to_all x2, blocking collectives, gather_rows(): mine = lax.all_to_all(copies, ('y', 'x'), 0, 0).reshape(HALF, WIDE)  22.7 us
    ppermute x11, starting transfers between devices, cyclic(): return lax.ppermute(block, axes, [(i, (i + k) % n) for i in range(n)])  13.8 us
    ppermute x3, waiting for transfers between devices, far(): lax.ppermute(block, SPAN, [(i, (i + (1 if i % 2 else -1)) % SPANS) for i...  11.6 us
    ppermute x4, starting transfers between devices, swapped(): return lax.ppermute(block, 'core', [(0, 1), (1, 0)])  8.58 us
    ppermute x11, waiting for transfers between devices, cyclic(): return lax.ppermute(block, axes, [(i, (i + k) % n) for i in range(n)])  6.27 us
    ppermute x3, starting transfers between devices, far(): lax.ppermute(block, SPAN, [(i, (i + (1 if i % 2 else -1)) % SPANS) for i...  6.15 us
  transfers between devices with their start and end apart: 21, of which 7 were waited for; matrix products, arithmetic and copies ran while one was open for 0% of the time, Pallas kernels for 6%

profile of v7, /device:TPU:1, one launch (start us, length us, event | category | flops | bytes accessed | tf_op | source)
XLA Modules:
  0.0 139.7 jit_solution(13823907817306248800)
XLA Ops:
  0.6 2.2 %collective-permute-start = (f32[256,256]{1,0:T(8,128)}, f32[256,256]{1,0:T(8,128)S(1)}, u32[]{:S(2)}, u32[]{:S(2)}) collective-permute-start(f32[256,256]{1,0:T(8,128)} %bitcast.18), channel_id=1, source_target_pairs={{0,8},{8,16},{16,24},{24,32},{32,40},{40,48},{48,56},{56,64},{64,7... | collective-permute-start | bytes 786440 | tf_op jit(solution)/shard_map/ppermute | solution.py:26
  4.4 2.1 %collective-permute-start.2 = (f32[256,256]{1,0:T(8,128)S(1)}, f32[256,256]{1,0:T(8,128)S(1)}, u32[]{:S(2)}, u32[]{:S(2)}) collective-permute-start(f32[256,256]{1,0:T(8,128)S(1)} %bitcast.22), channel_id=1, source_target_pairs={{0,1},{1,2},{2,3},{3,4},{4,5},{5,6},{6,7},{7,0},{8,9},{9,10},{10,1... | collective-permute-start | bytes 786440 | tf_op jit(solution)/shard_map/ppermute | solution.py:26
  6.5 1.3 collective-permute-start.1
  9.7 6.2 %collective-permute-done.1.lives_behind = f32[8,256]{1,0:T(8,128)S(1)} collective-permute-done((f32[8,256]{1,0:T(8,128)S(1)}, f32[8,256]{1,0:T(8,128)S(1)}, u32[]{:S(2)}, u32[]{:S(2)}) %collective-permute-start.1) | collective-permute-done | bytes 8224 | tf_op jit(solution)/shard_map/ppermute | solution.py:26
  16.6 1.2 collective-permute-start.5
  18.4 2.9 %collective-permute-start.4 = (f32[256,256]{1,0:T(8,128)S(1)}, f32[256,256]{1,0:T(8,128)S(1)}, u32[]{:S(2)}, u32[]{:S(2)}) collective-permute-start(f32[256,256]{1,0:T(8,128)S(1)} %get-tuple-element.71.f0), channel_id=1, source_target_pairs={{0,1},{1,2},{2,3},{3,4},{4,5},{5,6},{6,7},{7,0},{8,9},{9,10},{10,1... | collective-permute-start | bytes 786440 | tf_op jit(solution)/shard_map/ppermute | solution.py:26
  22.2 4.5 %collective-permute-done.5.g3 = f32[256,256]{1,0:T(8,128)S(1)} collective-permute-done((f32[256,256]{1,0:T(8,128)S(1)}, f32[256,256]{1,0:T(8,128)S(1)}, u32[]{:S(2)}, u32[]{:S(2)}) %collective-permute-start.5) | collective-permute-done | bytes 262176 | tf_op jit(solution)/shard_map/ppermute | solution.py:34
  26.6 1.2 flex_first_span.1
  27.9 1.5 %flex_first.1 = (f32[512,256]{1,0:T(8,128)S(1)}, f32[512,256]{1,0:T(8,128)S(1)}, f32[512,256]{1,0:T(8,128)S(1)}, f32[512,256]{1,0:T(8,128)S(1)}, f32[256,256]{1,...) custom-call(f32[8,256]{1,0:T(8,128)S(1)} %get-tuple-element.70.masks, ...), custom_call_target="tpu_custom_call" | custom-call | flops 805306368 | bytes 8388608 | tf_op jit(solution)/shard_map/flex_first/pallas_call | solution.py:372
  29.4 2.2 %collective-permute-start.7 = (f32[128,384]{1,0:T(8,128)S(1)}, f32[128,384]{1,0:T(8,128)S(1)}, u32[]{:S(2)}, u32[]{:S(2)}) collective-permute-start(f32[128,384]{1,0:T(8,128)S(1)} %get-tuple-element.82), channel_id=1, source_target_pairs={{0,1},{1,0},{2,3},{3,2},{4,5},{5,4},{6,7},{7,6},{8,9},{9,8},{10,11... | collective-permute-start | bytes 589832 | tf_op jit(solution)/shard_map/ppermute | solution.py:38
  31.6 1.1 collective-permute-done.7.got
  32.7 11.1 %all_to_all.30.got = f32[16,8,384]{2,1,0:T(8,128)S(1)} all-to-all(f32[16,8,384]{2,1,0:T(8,128)S(1)} %add.2), channel_id=1, replica_groups=mesh['z'=8,'y'=4,'x'=4,'core'=2] {'y','x'}, dimensions={0} | all-to-all | bytes 393216 | tf_op jit(solution)/shard_map/all_to_all | solution.py:341
  43.8 1.8 %collective-permute-start.8 = (f32[512,256]{1,0:T(8,128)S(1)}, f32[512,256]{1,0:T(8,128)S(1)}, u32[]{:S(2)}, u32[]{:S(2)}) collective-permute-start(f32[512,256]{1,0:T(8,128)S(1)} %get-tuple-element.88.f1), channel_id=1, source_target_pairs={{0,7},{1,0},{2,1},{3,2},{4,3},{5,4},{6,5},{7,6},{8,15},{9,8},{10,9... | collective-permute-start | bytes 1572872 | tf_op jit(solution)/shard_map/ppermute | solution.py:26
  45.8 2.9 %collective-permute-start.11 = (f32[512,256]{1,0:T(8,128)S(1)}, f32[512,256]{1,0:T(8,128)S(1)}, u32[]{:S(2)}, u32[]{:S(2)}) collective-permute-start(f32[512,256]{1,0:T(8,128)S(1)} %get-tuple-element.91.f3), channel_id=1, source_target_pairs={{0,248},{8,16},{16,8},{24,32},{32,24},{40,48},{48,40},{56,64},{64,... | collective-permute-start | bytes 1572872 | tf_op jit(solution)/shard_map/ppermute | solution.py:34
  48.8 13.8 %all_to_all.31.got = f32[8,8,384]{2,1,0:T(8,128)S(1)} all-to-all(f32[8,8,384]{2,1,0:T(8,128)S(1)} %spread.2), channel_id=1, replica_groups=mesh['z'=8,'y'=4,'x'=4,'core'=2] {'z'}, dimensions={0} | all-to-all | bytes 196608 | tf_op jit(solution)/shard_map/all_to_all | solution.py:346
  63.0 13.0 %all_to_all.32 = f32[16,8,384]{2,1,0:T(8,128)S(1)} all-to-all(f32[16,8,384]{2,1,0:T(8,128)S(1)} %get-tuple-element.92), channel_id=1, replica_groups=mesh['z'=8,'y'=4,'x'=4,'core'=2] {'y','x'}, dimensions={0} | all-to-all | bytes 393216 | tf_op jit(solution)/shard_map/all_to_all | solution.py:350
  76.0 1.9 %collective-permute-start.12 = (f32[128,384]{1,0:T(8,128)S(1)}, f32[128,384]{1,0:T(8,128)S(1)}, u32[]{:S(2)}, u32[]{:S(2)}) collective-permute-start(f32[128,384]{1,0:T(8,128)S(1)} %bitcast.28), channel_id=1, source_target_pairs={{0,1},{1,0},{2,3},{3,2},{4,5},{5,4},{6,7},{7,6},{8,9},{9,8},{10,11... | collective-permute-start | bytes 589832 | tf_op jit(solution)/shard_map/ppermute | solution.py:38
  77.9 1.1 collective-permute-done.12.other
  79.0 1.8 %precond_span.1 = (f32[256,256]{1,0:T(8,128)S(1)}, f32[256,256]{1,0:T(8,128)S(1)}, bf16[256,1024]{1,0:T(8,128)(2,1)S(1)}, bf16[256,1024]{1,0:T(8,128)(2,1)S(1)},...) custom-call(f32[8,256]{1,0:T(8,128)S(1)} %get-tuple-element.70.masks, ...), custom_call_target="tpu_custom_call" | custom-call | flops 805306368 | bytes 8388608 | tf_op jit(solution)/shard_map/precond_span/pallas_call | solution.py:410
  80.8 2.0 %collective-permute-start.15 = (f32[256,256]{1,0:T(8,128)S(1)}, f32[256,256]{1,0:T(8,128)S(1)}, u32[]{:S(2)}, u32[]{:S(2)}) collective-permute-start(f32[256,256]{1,0:T(8,128)S(1)} %get-tuple-element.97.f3), channel_id=1, source_target_pairs={{0,248},{8,16},{16,8},{24,32},{32,24},{40,48},{48,40},{56,64},{64,... | collective-permute-start | bytes 786440 | tf_op jit(solution)/shard_map/ppermute | solution.py:34
  84.6 7.1 %collective-permute-done.15.g3 = f32[256,256]{1,0:T(8,128)S(1)} collective-permute-done((f32[256,256]{1,0:T(8,128)S(1)}, f32[256,256]{1,0:T(8,128)S(1)}, u32[]{:S(2)}, u32[]{:S(2)}) %collective-permute-start.15) | collective-permute-done | bytes 262176 | tf_op jit(solution)/shard_map/ppermute | solution.py:34
  91.7 1.2 flex_second_span.1
  93.0 1.5 %flex_second.1 = (f32[256,256]{1,0:T(8,128)S(1)}, f32[256,256]{1,0:T(8,128)S(1)}, f32[256,256]{1,0:T(8,128)S(1)}, f32[256,256]{1,0:T(8,128)S(1)}, f32[256,256]{1...) custom-call(f32[8,256]{1,0:T(8,128)S(1)} %get-tuple-element.70.masks, ...), custom_call_target="tpu_custom_call" | custom-call | flops 805306368 | bytes 8388608 | tf_op jit(solution)/shard_map/flex_second/pallas_call | solution.py:372
  94.4 1.3 collective-permute-start.17
  95.7 1.1 collective-permute-done.17.got
  96.8 12.4 %all_to_all.33.got = f32[16,8,384]{2,1,0:T(8,128)S(1)} all-to-all(f32[16,8,384]{2,1,0:T(8,128)S(1)} %add.3), channel_id=1, replica_groups=mesh['z'=8,'y'=4,'x'=4,'core'=2] {'y','x'}, dimensions={0} | all-to-all | bytes 393216 | tf_op jit(solution)/shard_map/all_to_all | solution.py:341
  109.2 1.3 collective-permute-start.18
  110.5 1.3 collective-permute-start.19
  111.8 12.2 %all_to_all.34.got = f32[8,8,384]{2,1,0:T(8,128)S(1)} all-to-all(f32[8,8,384]{2,1,0:T(8,128)S(1)} %spread.3), channel_id=1, replica_groups=mesh['z'=8,'y'=4,'x'=4,'core'=2] {'z'}, dimensions={0} | all-to-all | bytes 196608 | tf_op jit(solution)/shard_map/all_to_all | solution.py:346
  124.4 9.8 %all_to_all.35 = f32[16,8,384]{2,1,0:T(8,128)S(1)} all-to-all(f32[16,8,384]{2,1,0:T(8,128)S(1)} %coarse_second.1), channel_id=1, replica_groups=mesh['z'=8,'y'=4,'x'=4,'core'=2] {'y','x'}, dimensions={0} | all-to-all | bytes 393216 | tf_op jit(solution)/shard_map/all_to_all | solution.py:350
  134.2 3.1 %collective-permute-start.20 = (f32[128,384]{1,0:T(8,128)S(1)}, f32[128,384]{1,0:T(8,128)S(1)}, u32[]{:S(2)}, u32[]{:S(2)}) collective-permute-start(f32[128,384]{1,0:T(8,128)S(1)} %bitcast.26), channel_id=1, source_target_pairs={{0,1},{1,0},{2,3},{3,2},{4,5},{5,4},{6,7},{7,6},{8,9},{9,8},{10,11... | collective-permute-start | bytes 589832 | tf_op jit(solution)/shard_map/ppermute | solution.py:38
  138.4 1.3 final.1
  (50 shorter events, 9.5 us)
Async XLA Ops:
  0.6 15.4 %collective-permute-start = (f32[256,256]{1,0:T(8,128)}, f32[256,256]{1,0:T(8,128)S(1)}, u32[]{:S(2)}, u32[]{:S(2)}) collective-permute-start(f32[256,256]{1,0:T(8,128)} %bitcast.18), channel_id=1, source_target_pairs={{0,8},{8,16},{16,24},{24,32},{32,40},{40,48},{48,56},{56,64},{64,7... | collective-permute-start | bytes 786440 | tf_op jit(solution)/shard_map/ppermute | solution.py:26
  2.8 0.7 copy-start.6
  3.5 0.9 copy-start.4
  3.5 4.3 %copy-start.1 = (f32[1,1,1024,1024]{3,2,1,0:T(8,128)S(1)}, f32[1,1,1024,1024]{3,2,1,0:T(8,128)}, u32[]{:S(2)}) copy-start(f32[1,1,1024,1024]{3,2,1,0:T(8,128)} %param.8) | copy-start | bytes 12582916
  4.4 11.6 %collective-permute-start.2 = (f32[256,256]{1,0:T(8,128)S(1)}, f32[256,256]{1,0:T(8,128)S(1)}, u32[]{:S(2)}, u32[]{:S(2)}) collective-permute-start(f32[256,256]{1,0:T(8,128)S(1)} %bitcast.22), channel_id=1, source_target_pairs={{0,1},{1,2},{2,3},{3,4},{4,5},{5,6},{6,7},{7,0},{8,9},{9,10},{10,1... | collective-permute-start | bytes 786440 | tf_op jit(solution)/shard_map/ppermute | solution.py:26
  6.5 9.5 %collective-permute-start.1 = (f32[8,256]{1,0:T(8,128)S(1)}, f32[8,256]{1,0:T(8,128)S(1)}, u32[]{:S(2)}, u32[]{:S(2)}) collective-permute-start(f32[8,256]{1,0:T(8,128)S(1)} %lives.1), channel_id=1, source_target_pairs={{0,8},{8,16},{16,24},{24,32},{32,40},{40,48},{48,56},{56,64},{64,7... | collective-permute-start | bytes 24584 | tf_op jit(solution)/shard_map/ppermute | solution.py:26
  7.8 1.0 copy-start.3
  16.6 10.0 %collective-permute-start.5 = (f32[256,256]{1,0:T(8,128)S(1)}, f32[256,256]{1,0:T(8,128)S(1)}, u32[]{:S(2)}, u32[]{:S(2)}) collective-permute-start(f32[256,256]{1,0:T(8,128)S(1)} %get-tuple-element.73.f3), channel_id=1, source_target_pairs={{0,248},{8,16},{16,8},{24,32},{32,24},{40,48},{48,40},{56,64},{64,... | collective-permute-start | bytes 786440 | tf_op jit(solution)/shard_map/ppermute | solution.py:34
  17.9 3.5 %copy-start.2 = (f32[1,1,1024,1024]{3,2,1,0:T(8,128)S(1)}, f32[1,1,1024,1024]{3,2,1,0:T(8,128)}, u32[]{:S(2)}) copy-start(f32[1,1,1024,1024]{3,2,1,0:T(8,128)} %param.7) | copy-start | bytes 12582916
  17.9 8.8 %collective-permute-start.6 = (f32[256,256]{1,0:T(8,128)S(1)}, f32[256,256]{1,0:T(8,128)S(1)}, u32[]{:S(2)}, u32[]{:S(2)}) collective-permute-start(f32[256,256]{1,0:T(8,128)S(1)} %get-tuple-element.74.f2), channel_id=1, source_target_pairs={{0,8},{8,0},{16,24},{24,16},{32,40},{40,32},{48,56},{56,48},{64,72... | collective-permute-start | bytes 786440 | tf_op jit(solution)/shard_map/ppermute | solution.py:30
  18.4 9.4 %collective-permute-start.4 = (f32[256,256]{1,0:T(8,128)S(1)}, f32[256,256]{1,0:T(8,128)S(1)}, u32[]{:S(2)}, u32[]{:S(2)}) collective-permute-start(f32[256,256]{1,0:T(8,128)S(1)} %get-tuple-element.71.f0), channel_id=1, source_target_pairs={{0,1},{1,2},{2,3},{3,4},{4,5},{5,6},{6,7},{7,0},{8,9},{9,10},{10,1... | collective-permute-start | bytes 786440 | tf_op jit(solution)/shard_map/ppermute | solution.py:26
  21.4 6.5 %collective-permute-start.3 = (f32[256,256]{1,0:T(8,128)S(1)}, f32[256,256]{1,0:T(8,128)S(1)}, u32[]{:S(2)}, u32[]{:S(2)}) collective-permute-start(f32[256,256]{1,0:T(8,128)S(1)} %get-tuple-element.72.f1), channel_id=1, source_target_pairs={{0,7},{1,0},{2,1},{3,2},{4,3},{5,4},{6,5},{7,6},{8,15},{9,8},{10,9... | collective-permute-start | bytes 786440 | tf_op jit(solution)/shard_map/ppermute | solution.py:26
  21.4 5.2 %copy-start = (f32[1,1,256,1024]{3,2,1,0:T(8,128)S(1)}, f32[1,1,256,1024]{3,2,1,0:T(8,128)}, u32[]{:S(2)}) copy-start(f32[1,1,256,1024]{3,2,1,0:T(8,128)} %param.9) | copy-start | bytes 3145732
  27.9 34.7 %copy-start.5 = (f32[256,256]{1,0:T(8,128)S(1)}, f32[256,256]{1,0:T(8,128)}, u32[]{:S(2)}) copy-start(f32[256,256]{1,0:T(8,128)} %coarse.3) | copy-start | bytes 786436
  29.4 3.3 %collective-permute-start.7 = (f32[128,384]{1,0:T(8,128)S(1)}, f32[128,384]{1,0:T(8,128)S(1)}, u32[]{:S(2)}, u32[]{:S(2)}) collective-permute-start(f32[128,384]{1,0:T(8,128)S(1)} %get-tuple-element.82), channel_id=1, source_target_pairs={{0,1},{1,0},{2,3},{3,2},{4,5},{5,4},{6,7},{7,6},{8,9},{9,8},{10,11... | collective-permute-start | bytes 589832 | tf_op jit(solution)/shard_map/ppermute | solution.py:38
  43.8 19.2 %collective-permute-start.8 = (f32[512,256]{1,0:T(8,128)S(1)}, f32[512,256]{1,0:T(8,128)S(1)}, u32[]{:S(2)}, u32[]{:S(2)}) collective-permute-start(f32[512,256]{1,0:T(8,128)S(1)} %get-tuple-element.88.f1), channel_id=1, source_target_pairs={{0,7},{1,0},{2,1},{3,2},{4,3},{5,4},{6,5},{7,6},{8,15},{9,8},{10,9... | collective-permute-start | bytes 1572872 | tf_op jit(solution)/shard_map/ppermute | solution.py:26
  45.6 17.4 %collective-permute-start.9 = (f32[512,256]{1,0:T(8,128)S(1)}, f32[512,256]{1,0:T(8,128)S(1)}, u32[]{:S(2)}, u32[]{:S(2)}) collective-permute-start(f32[512,256]{1,0:T(8,128)S(1)} %get-tuple-element.89.f0), channel_id=1, source_target_pairs={{0,1},{1,2},{2,3},{3,4},{4,5},{5,6},{6,7},{7,0},{8,9},{9,10},{10,1... | collective-permute-start | bytes 1572872 | tf_op jit(solution)/shard_map/ppermute | solution.py:26
  45.8 17.2 %collective-permute-start.10 = (f32[512,256]{1,0:T(8,128)S(1)}, f32[512,256]{1,0:T(8,128)S(1)}, u32[]{:S(2)}, u32[]{:S(2)}) collective-permute-start(f32[512,256]{1,0:T(8,128)S(1)} %get-tuple-element.90.f2), channel_id=1, source_target_pairs={{0,8},{8,0},{16,24},{24,16},{32,40},{40,32},{48,56},{56,48},{64,72... | collective-permute-start | bytes 1572872 | tf_op jit(solution)/shard_map/ppermute | solution.py:30
  45.8 17.2 %collective-permute-start.11 = (f32[512,256]{1,0:T(8,128)S(1)}, f32[512,256]{1,0:T(8,128)S(1)}, u32[]{:S(2)}, u32[]{:S(2)}) collective-permute-start(f32[512,256]{1,0:T(8,128)S(1)} %get-tuple-element.91.f3), channel_id=1, source_target_pairs={{0,248},{8,16},{16,8},{24,32},{32,24},{40,48},{48,40},{56,64},{64,... | collective-permute-start | bytes 1572872 | tf_op jit(solution)/shard_map/ppermute | solution.py:34
  76.0 3.0 %collective-permute-start.12 = (f32[128,384]{1,0:T(8,128)S(1)}, f32[128,384]{1,0:T(8,128)S(1)}, u32[]{:S(2)}, u32[]{:S(2)}) collective-permute-start(f32[128,384]{1,0:T(8,128)S(1)} %bitcast.28), channel_id=1, source_target_pairs={{0,1},{1,0},{2,3},{3,2},{4,5},{5,4},{6,7},{7,6},{8,9},{9,8},{10,11... | collective-permute-start | bytes 589832 | tf_op jit(solution)/shard_map/ppermute | solution.py:38
  80.8 10.9 %collective-permute-start.15 = (f32[256,256]{1,0:T(8,128)S(1)}, f32[256,256]{1,0:T(8,128)S(1)}, u32[]{:S(2)}, u32[]{:S(2)}) collective-permute-start(f32[256,256]{1,0:T(8,128)S(1)} %get-tuple-element.97.f3), channel_id=1, source_target_pairs={{0,248},{8,16},{16,8},{24,32},{32,24},{40,48},{48,40},{56,64},{64,... | collective-permute-start | bytes 786440 | tf_op jit(solution)/shard_map/ppermute | solution.py:34
  82.8 8.9 %collective-permute-start.16 = (f32[256,256]{1,0:T(8,128)S(1)}, f32[256,256]{1,0:T(8,128)S(1)}, u32[]{:S(2)}, u32[]{:S(2)}) collective-permute-start(f32[256,256]{1,0:T(8,128)S(1)} %get-tuple-element.98.f2), channel_id=1, source_target_pairs={{0,8},{8,0},{16,24},{24,16},{32,40},{40,32},{48,56},{56,48},{64,72... | collective-permute-start | bytes 786440 | tf_op jit(solution)/shard_map/ppermute | solution.py:30
  83.8 9.2 %collective-permute-start.14 = (f32[256,256]{1,0:T(8,128)S(1)}, f32[256,256]{1,0:T(8,128)S(1)}, u32[]{:S(2)}, u32[]{:S(2)}) collective-permute-start(f32[256,256]{1,0:T(8,128)S(1)} %get-tuple-element.95.f0), channel_id=1, source_target_pairs={{0,1},{1,2},{2,3},{3,4},{4,5},{5,6},{6,7},{7,0},{8,9},{9,10},{10,1... | collective-permute-start | bytes 786440 | tf_op jit(solution)/shard_map/ppermute | solution.py:26
  84.6 8.4 %collective-permute-start.13 = (f32[256,256]{1,0:T(8,128)S(1)}, f32[256,256]{1,0:T(8,128)S(1)}, u32[]{:S(2)}, u32[]{:S(2)}) collective-permute-start(f32[256,256]{1,0:T(8,128)S(1)} %get-tuple-element.96.f1), channel_id=1, source_target_pairs={{0,7},{1,0},{2,1},{3,2},{4,3},{5,4},{6,5},{7,6},{8,15},{9,8},{10,9... | collective-permute-start | bytes 786440 | tf_op jit(solution)/shard_map/ppermute | solution.py:26
  94.4 2.3 %collective-permute-start.17 = (f32[128,384]{1,0:T(8,128)S(1)}, f32[128,384]{1,0:T(8,128)S(1)}, u32[]{:S(2)}, u32[]{:S(2)}) collective-permute-start(f32[128,384]{1,0:T(8,128)S(1)} %get-tuple-element.108), channel_id=1, source_target_pairs={{0,1},{1,0},{2,3},{3,2},{4,5},{5,4},{6,7},{7,6},{8,9},{9,8},{10,11... | collective-permute-start | bytes 589832 | tf_op jit(solution)/shard_map/ppermute | solution.py:38
  109.2 15.2 %collective-permute-start.18 = (f32[256,256]{1,0:T(8,128)S(1)}, f32[256,256]{1,0:T(8,128)S(1)}, u32[]{:S(2)}, u32[]{:S(2)}) collective-permute-start(f32[256,256]{1,0:T(8,128)S(1)} %get-tuple-element.112), channel_id=1, source_target_pairs={{0,7},{1,0},{2,1},{3,2},{4,3},{5,4},{6,5},{7,6},{8,15},{9,8},{10,9... | collective-permute-start | bytes 786440 | tf_op jit(solution)/shard_map/ppermute | solution.py:26
  110.5 13.9 %collective-permute-start.19 = (f32[256,256]{1,0:T(8,128)S(1)}, f32[256,256]{1,0:T(8,128)S(1)}, u32[]{:S(2)}, u32[]{:S(2)}) collective-permute-start(f32[256,256]{1,0:T(8,128)S(1)} %get-tuple-element.113), channel_id=1, source_target_pairs={{0,248},{8,0},{16,8},{24,16},{32,24},{40,32},{48,40},{56,48},{64,5... | collective-permute-start | bytes 786440 | tf_op jit(solution)/shard_map/ppermute | solution.py:26
  134.2 4.2 %collective-permute-start.20 = (f32[128,384]{1,0:T(8,128)S(1)}, f32[128,384]{1,0:T(8,128)S(1)}, u32[]{:S(2)}, u32[]{:S(2)}) collective-permute-start(f32[128,384]{1,0:T(8,128)S(1)} %bitcast.26), channel_id=1, source_target_pairs={{0,1},{1,0},{2,3},{3,2},{4,5},{5,4},{6,7},{7,6},{8,9},{9,8},{10,11... | collective-permute-start | bytes 589832 | tf_op jit(solution)/shard_map/ppermute | solution.py:38
